TPU v7x, 256 devices: a whole 4x4x8 slice. The times are simulated.
256 devices in a mesh: space: 256 (over z, y, x, core).
Axes of the slice: x: 4, y: 4, z: 8, core: 2. Of those that a mesh axis runs over, the one named last changes fastest.
Arguments:
- positions: float32 [3, 32768], P(None, 'space'), may hold values from 0 to 2560, as said below
- species: int32 [32768], P('space'), may hold values from 0 to 5
- neighbours: int32 [24, 32768], P(None, 'space'), may hold values from 0 to 255, as said below
- counts: int32 [32768], P('space'), may hold values from 1 to 24, as said below
- ghost_index: int32 [2, 16384], P(None, 'space'), may hold values from 0 to 127, as said below
- embed: float32 [6, 64], replicated, may hold values from -6 to 6
- radial_in: float32 [2, 8, 64], replicated, may hold values from -2 to 2
- radial_mid: float32 [2, 64, 64], replicated, may hold values from -0.75 to 0.75
- radial_out: float32 [2, 64, 128], replicated, may hold values from -0.75 to 0.75
- mix_one: float32 [3, 64, 64], replicated, may hold values from -0.75 to 0.75
- vec_mix: float32 [64, 64], replicated, may hold values from -0.75 to 0.75
- mix_two: float32 [2, 64, 64], replicated, may hold values from -0.75 to 0.75
- readout: float32 [2, 64], replicated, may hold values from -0.75 to 0.75
Outputs:
- atom_energy: float32 [32768], P('space')
- forces: float32 [3, 32768], P(None, 'space')
Inputs may be any that keep to these rules, and one draw needn't show every extreme that they name: `neighbours`: entries index the owning domain's table: local atoms first, then the 64 lower ghosts in the order of ghost_index row 0, then the 64 upper ghosts in the order of row 1; never the atom itself. `counts`: slots at or beyond an atom's count are padding; the first atom of every domain uses all 24 slots. `ghost_index`: row 0 of domain d holds each local index of 64 or more of domain d-1 once, row 1 each local index under 64 of domain d+1 once, in orders drawn from the seed. `positions`: the first coordinate of an atom of domain d lies in [10 d, 10 d + 10], the second in [0, 32], the third in [0, 4]; a domain holds 0.1 atoms per cubic angstrom.
All inputs are finite; a program needn't handle non-finite values.
Results may differ from a plain program's by a relative error of at most 0.0003.
Values sent between devices are 32-bit elements; how exact they have to be, the bound alone decides.
No kernel may reach another device: no remote copies, remote signals or barrier semaphores. Data moves between devices by JAX's collectives and lax.ppermute only.
A program may use at most 64 MiB of HBM per device.

v0:
```python
import jax
import jax.numpy as jnp
from jax import lax
from jax.sharding import PartitionSpec as P

RADIUS = 5.0
SOFTEN = 0.25


def shifted(block, axis, distance):
    devices = range(lax.axis_size(axis))
    route = [(i - distance, i) for i in devices if i - distance in devices]
    return lax.ppermute(block, axis, route)


def silu(v):
    return v * jax.nn.sigmoid(v)


def hdot(a, b):
    return jnp.dot(a, b, precision=lax.Precision.HIGHEST, preferred_element_type=jnp.float32)


def lookup(table, selector):
    return hdot(table, selector)


def edge_terms(pos_table, selector, counts, slots, nbasis):
    atoms = counts.shape[0]
    pos_own = pos_table[:, :atoms]
    far = lookup(pos_table, selector).reshape(3, slots, atoms)
    vector = far - pos_own[:, None, :]
    dist = jnp.sqrt(jnp.sum(vector * vector, axis=0) + SOFTEN)
    unit = vector / dist[None]
    ratio = jnp.minimum(dist / RADIUS, 1.0)
    envelope = 1.0 - 21.0 * ratio**5 + 35.0 * ratio**6 - 15.0 * ratio**7
    valid = (lax.broadcasted_iota(jnp.int32, (slots, atoms), 0) < counts[None, :]).astype(
        jnp.float32
    )
    order = (lax.broadcasted_iota(jnp.int32, (nbasis, 1, 1), 0) + 1).astype(jnp.float32)
    basis = (
        jnp.sin(order * (jnp.pi / RADIUS) * dist[None]) * (RADIUS / dist * envelope * valid)[None]
    )
    return (unit, basis.reshape(nbasis, slots * atoms))


def radial(basis, layer, radial_in, radial_mid, radial_out):
    hidden = silu(hdot(radial_in[layer].T, basis))
    hidden = silu(hdot(radial_mid[layer].T, hidden))
    return hdot(radial_out[layer].T, hidden)


def layer_one(
    pos_table,
    h0_table,
    selector,
    counts,
    slots,
    radial_in,
    radial_mid,
    radial_out,
    mix_one,
    vec_mix,
):
    atoms = counts.shape[0]
    width = h0_table.shape[0]
    unit, basis = edge_terms(pos_table, selector, counts, slots, radial_in.shape[1])
    weights = radial(basis, 0, radial_in, radial_mid, radial_out)
    w_a = weights[:width].reshape(width, slots, atoms)
    w_b = weights[width:].reshape(width, slots, atoms)
    h_far = lookup(h0_table, selector).reshape(width, slots, atoms)
    scale = 1.0 / jnp.sqrt(jnp.float32(slots))
    scalar_msg = jnp.sum(w_a * h_far, axis=1) * scale
    carried = w_b * h_far
    vector_msg = jnp.sum(carried[None] * unit[:, None], axis=2) * scale
    square = jnp.sum(vector_msg * vector_msg, axis=0)
    h0_own = h0_table[:, :atoms]
    s_one = silu(
        hdot(mix_one[0].T, scalar_msg) + hdot(mix_one[1].T, h0_own) + hdot(mix_one[2].T, square)
    )
    v_one = jnp.einsum("cd,xca->xda", vec_mix, vector_msg, precision=lax.Precision.HIGHEST)
    return jnp.concatenate([s_one[None], v_one], axis=0)


def layer_two(
    pos_table,
    feat_table,
    selector,
    counts,
    slots,
    radial_in,
    radial_mid,
    radial_out,
    mix_two,
    readout,
):
    atoms = counts.shape[0]
    width = feat_table.shape[1]
    columns = feat_table.shape[2]
    unit, basis = edge_terms(pos_table, selector, counts, slots, radial_in.shape[1])
    weights = radial(basis, 1, radial_in, radial_mid, radial_out)
    w_a = weights[:width].reshape(width, slots, atoms)
    w_b = weights[width:].reshape(width, slots, atoms)
    far = lookup(feat_table.reshape(4 * width, columns), selector).reshape(4, width, slots, atoms)
    along = jnp.sum(far[1:] * unit[:, None], axis=0)
    scale = 1.0 / jnp.sqrt(jnp.float32(slots))
    message = jnp.sum(w_a * far[0] + w_b * along, axis=1) * scale
    s_own = feat_table[0, :, :atoms]
    s_two = silu(hdot(mix_two[0].T, message) + hdot(mix_two[1].T, s_own))
    return hdot(readout[0][None], s_own)[0] + hdot(readout[1][None], s_two)[0]


def inputs_block(block, by):
    return shifted(block, "space", by)


def features_block(block, by):
    return shifted(block, "space", by)


def feature_grads_block(block, by):
    return shifted(block, "space", by)


def position_grads_block(block, by):
    return shifted(block, "space", by)


def body(
    positions,
    species,
    neighbours,
    counts,
    ghost_index,
    embed,
    radial_in,
    radial_mid,
    radial_out,
    mix_one,
    vec_mix,
    mix_two,
    readout,
):
    atoms = positions.shape[1]
    slots = neighbours.shape[0]
    onehot = (
        species[None, :] == lax.broadcasted_iota(jnp.int32, (embed.shape[0], atoms), 0)
    ).astype(jnp.float32)
    h0_own = hdot(embed.T, onehot)
    stacked = jnp.concatenate([positions, h0_own], axis=0)
    remap = jnp.concatenate(
        [
            lax.broadcasted_iota(jnp.int32, (atoms,), 0),
            atoms + ghost_index[0],
            2 * atoms + ghost_index[1],
        ]
    )
    table_rows = jnp.take(remap, neighbours)

    def spread(block, mover):
        return jnp.concatenate([block, mover(block, 1), mover(block, -1)], axis=-1)

    def collect(grads, mover):
        own = grads[..., :atoms]
        own = own + mover(grads[..., atoms : 2 * atoms], -1)
        return own + mover(grads[..., 2 * atoms :], 1)

    move_inputs, move_features = (inputs_block, features_block)
    move_feature_grads, move_position_grads = (feature_grads_block, position_grads_block)
    table_in = spread(stacked, move_inputs)
    pos_table = table_in[:3]
    h0_table = table_in[3:]
    columns = pos_table.shape[1]
    selector = (
        table_rows.reshape(1, -1) == lax.broadcasted_iota(jnp.int32, (columns, 1), 0)
    ).astype(jnp.float32)

    def first(pt):
        return layer_one(
            pt,
            h0_table,
            selector,
            counts,
            slots,
            radial_in,
            radial_mid,
            radial_out,
            mix_one,
            vec_mix,
        )

    def second(pt, ft):
        return layer_two(
            pt, ft, selector, counts, slots, radial_in, radial_mid, radial_out, mix_two, readout
        )

    feats, pull_one = jax.vjp(first, pos_table)
    feat_table = spread(feats, move_features)
    atom_energy, pull_two = jax.vjp(second, pos_table, feat_table)
    grad_pos_two, grad_feat_table = pull_two(jnp.ones_like(atom_energy))
    grad_feats = collect(grad_feat_table, move_feature_grads)
    grad_pos_one = pull_one(grad_feats)[0]
    grad_positions = collect(grad_pos_one + grad_pos_two, move_position_grads)
    return (atom_energy, -grad_positions)


def solution(mesh):
    placed = (
        P(None, "space"),
        P("space"),
        P(None, "space"),
        P("space"),
        P(None, "space"),
        P(),
        P(),
        P(),
        P(),
        P(),
        P(),
        P(),
        P(),
    )
    return jax.shard_map(
        body, mesh=mesh, in_specs=placed, out_specs=(P("space"), P(None, "space")), check_vma=False
    )
```

profile of v0, /device:TPU:128, one launch (start us, length us, event | category | flops | bytes accessed | tf_op | source)
XLA Modules:
  0.0 124.2 jit_solution(7252087809836720529)
XLA Ops:
  2.3 6.1 %collective-permute-start.1 = (f32[67,128]{1,0:T(8,128)S(1)}, f32[67,128]{1,0:T(8,128)S(1)}, u32[]{:S(2)}, u32[]{:S(2)}) collective-permute-start(f32[67,128]{1,0:T(8,128)S(1)} %pad_maximum_fusion.8), channel_id=1, source_target_pairs={{1,0},{2,1},{3,2},{4,3},{5,4},{6,5},{7,6},{8,7},{9,8},{10,9},{11,1... | collective-permute-start | bytes 102920 | tf_op jit(solution)/shard_map/ppermute | solution.py:13
  8.4 1.9 %collective-permute-start = (f32[67,128]{1,0:T(8,128)S(1)}, f32[67,128]{1,0:T(8,128)S(1)}, u32[]{:S(2)}, u32[]{:S(2)}) collective-permute-start(f32[67,128]{1,0:T(8,128)S(1)} %pad_maximum_fusion.8), channel_id=1, source_target_pairs={{0,1},{1,2},{2,3},{3,4},{4,5},{5,6},{6,7},{7,8},{8,9},{9,10},{10,1... | collective-permute-start | bytes 102920 | tf_op jit(solution)/shard_map/ppermute | solution.py:13
  11.7 1.3 %slice_bitcast_fusion.7 = (f32[64]{0:T(128)}, f32[64]{0:T(128)}) fusion(f32[2,64]{1,0:T(2,128)} %param.25), kind=kLoop, calls=%fused_computation.307 | loop fusion | bytes 1024 | tf_op jit(solution)/shard_map/reshape.1
  13.9 19.5 %gather_fusion = s32[3072]{0:T(1024)S(1)} fusion(s32[256]{0:T(256)S(1)} %pad_add_fusion.1, s32[3072]{0:T(1024)S(1)} %bitcast_clamp_fusion), kind=kCustom, calls=%fused_computation | custom fusion | bytes 36864 | tf_op jit(solution)/shard_map/jit(_take)/gather | solution.py:158
  33.5 2.2 %multiply_reduce_fusion.4 = (f32[3072]{0:T(1024)S(1)}, f32[3,3072]{1,0:T(4,128)}, f32[3,3072]{1,0:T(4,128)S(1)}) fusion(f32[1,3,24,128]{3,2,1,0:T(8,128)S(1)} %broadcast_bitcast_fusion, s32[3072]{0:T(1024)S(1)} %fusion.170, f32[67,128]{1,0:T(8,128)S(1)} %collective-permute-done.1, f32[67,128]{1,0:T(8,128)S(1)} %collective-permute-done, ...), kind=kOutput, calls=%fused_computation.163 | convolution fusion | flops 43675008 | bytes 238080 | tf_op jit(solution)/shard_map/jvp()/dot_general | solution.py:21
  40.0 1.6 %convolution_bitcast_fusion.1 = f32[128,3072]{1,0:T(8,128)S(1)} fusion(f32[64,3072]{1,0:T(8,128)S(1)} %convolution_bitcast_fusion.9, f32[2,64,128]{2,1,0:T(8,128)S(1)} %copy-done.13), kind=kOutput, calls=%fused_computation.10 | convolution fusion | flops 302776320 | bytes 2392064 | tf_op jit(solution)/shard_map/jvp()/dot_general | solution.py:21
  41.5 1.8 %fusion.4 = f32[64,3072]{1,0:T(8,128)S(1)} fusion(s32[3072]{0:T(1024)S(1)} %fusion.170, f32[67,128]{1,0:T(8,128)S(1)} %collective-permute-done.1, f32[67,128]{1,0:T(8,128)S(1)} %collective-permute-done, f32[64,128]{1,0:T(8,128)S(1)} %bitcast.302, f32[3,128]{1,0:T(4,128)S(1)} %copy-done.17), kind=kOutput, calls=%fused_computation.6 | convolution fusion | flops 907223040 | bytes 901632 | tf_op jit(solution)/shard_map/jvp()/dot_general | solution.py:21
  46.2 9.1 %collective-permute-start.3 = (f32[4,64,128]{2,1,0:T(8,128)S(1)}, f32[4,64,128]{2,1,0:T(8,128)S(1)}, u32[]{:S(2)}, u32[]{:S(2)}) collective-permute-start(f32[4,64,128]{2,1,0:T(8,128)S(1)} %pad_maximum_fusion.1), channel_id=1, source_target_pairs={{1,0},{2,1},{3,2},{4,3},{5,4},{6,5},{7,6},{8,7},{9,8},{10,9},{11,1... | collective-permute-start | bytes 393224 | tf_op jit(solution)/shard_map/ppermute | solution.py:13
  55.3 2.1 %collective-permute-start.2 = (f32[4,64,128]{2,1,0:T(8,128)S(1)}, f32[4,64,128]{2,1,0:T(8,128)S(1)}, u32[]{:S(2)}, u32[]{:S(2)}) collective-permute-start(f32[4,64,128]{2,1,0:T(8,128)S(1)} %pad_maximum_fusion.1), channel_id=1, source_target_pairs={{0,1},{1,2},{2,3},{3,4},{4,5},{5,6},{6,7},{7,8},{8,9},{9,10},{10,1... | collective-permute-start | bytes 393224 | tf_op jit(solution)/shard_map/ppermute | solution.py:13
  58.5 1.6 %convolution_bitcast_fusion = f32[128,3072]{1,0:T(8,128)S(1)} fusion(f32[64,3072]{1,0:T(8,128)S(1)} %convolution_bitcast_fusion.8, f32[2,64,128]{2,1,0:T(8,128)S(1)} %copy-done.13), kind=kOutput, calls=%fused_computation.9 | convolution fusion | flops 302776320 | bytes 2392064 | tf_op jit(solution)/shard_map/jvp()/dot_general | solution.py:21
  60.8 6.3 %collective-permute-done.2 = f32[4,64,128]{2,1,0:T(8,128)S(1)} collective-permute-done((f32[4,64,128]{2,1,0:T(8,128)S(1)}, f32[4,64,128]{2,1,0:T(8,128)S(1)}, u32[]{:S(2)}, u32[]{:S(2)}) %collective-permute-start.2) | collective-permute-done | bytes 131104 | tf_op jit(solution)/shard_map/ppermute | solution.py:13
  67.1 2.8 %fusion.3 = f32[256,3072]{1,0:T(8,128)S(1)} fusion(f32[256,384]{1,0:T(8,128)S(1)} %bitcast.293, s32[3072]{0:T(1024)S(1)} %fusion.170), kind=kOutput, calls=%fused_computation.5 | convolution fusion | flops 3625058304 | bytes 3551232 | tf_op jit(solution)/shard_map/jvp()/dot_general | solution.py:21
  74.0 1.9 %pad_add_fusion = f32[4,64,24,128]{3,2,1,0:T(8,128)} fusion(f32[3,64,24,128]{3,2,1,0:T(8,128)S(1)} %get-tuple-element.23, f32[1,64,24,128]{3,2,1,0:T(8,128)S(1)} %bitcast_multiply_fusion.6), kind=kLoop, calls=%fused_computation.21 | loop fusion | flops 786432 | bytes 6291456 | tf_op jit(solution)/shard_map/transpose(jvp())/add_any | solution.py:105
  75.9 4.5 %dot_general.142 = f32[4,64,3072]{2,1,0:T(8,128)} reshape(f32[4,64,24,128]{3,2,1,0:T(8,128)} %pad_add_fusion) | data formatting | bytes 6291456 | tf_op jit(solution)/shard_map/transpose(jvp())/dot_general | solution.py:21
  80.4 5.1 %fusion.22 = f32[4,64,384]{2,1,0:T(8,128)S(1)} fusion(f32[4,64,3072]{2,1,0:T(8,128)} %dot_general.142, s32[3072]{0:T(1024)S(1)} %fusion.170, f32[1,64,128]{2,1,0:T(8,128)} %fusion.31), kind=kOutput, calls=%fused_computation.42 | convolution fusion | flops 3625156608 | bytes 3584000 | tf_op jit(solution)/shard_map/transpose(jvp())/dot_general | solution.py:21
  85.5 2.8 %collective-permute-start.4 = (f32[4,64,128]{2,1,0:T(8,128)S(1)}, f32[4,64,128]{2,1,0:T(8,128)S(1)}, u32[]{:S(2)}, u32[]{:S(2)}) collective-permute-start(f32[4,64,128]{2,1,0:T(8,128)S(1)} %get-tuple-element.27), channel_id=1, source_target_pairs={{1,0},{2,1},{3,2},{4,3},{5,4},{6,5},{7,6},{8,7},{9,8},{10,9},{11,1... | collective-permute-start | bytes 393224 | tf_op jit(solution)/shard_map/ppermute | solution.py:13
  88.3 2.1 %collective-permute-start.5 = (f32[4,64,128]{2,1,0:T(8,128)S(1)}, f32[4,64,128]{2,1,0:T(8,128)S(1)}, u32[]{:S(2)}, u32[]{:S(2)}) collective-permute-start(f32[4,64,128]{2,1,0:T(8,128)S(1)} %get-tuple-element.28), channel_id=1, source_target_pairs={{0,1},{1,2},{2,3},{3,4},{4,5},{5,6},{6,7},{7,8},{8,9},{9,10},{10,1... | collective-permute-start | bytes 393224 | tf_op jit(solution)/shard_map/ppermute | solution.py:13
  92.4 1.2 convolution_bitcast_fusion.6
  93.6 6.5 %collective-permute-done.5 = f32[4,64,128]{2,1,0:T(8,128)S(1)} collective-permute-done((f32[4,64,128]{2,1,0:T(8,128)S(1)}, f32[4,64,128]{2,1,0:T(8,128)S(1)}, u32[]{:S(2)}, u32[]{:S(2)}) %collective-permute-start.5) | collective-permute-done | bytes 131104 | tf_op jit(solution)/shard_map/ppermute | solution.py:13
  106.3 2.2 %fusion.36 = f32[3,384]{1,0:T(4,128)S(1)} fusion(s32[3072]{0:T(1024)S(1)} %fusion.170, f32[1,3,24,128]{3,2,1,0:T(8,128)S(1)} %bitcast.297, f32[3,3072]{1,0:T(4,128)S(1)} %copy-done.16, f32[3072]{0:T(1024)S(1)} %get-tuple-element.30, f32[3072]{0:T(1024)S(1)} %get-tuple-element.36, f32[3,128]{1,0:T(4,128)S(1)} %neg.92), kind=kOutput, calls=%fused_computation.68 | convolution fusion | flops 43684992 | bytes 116736 | tf_op jit(solution)/shard_map/transpose(jvp())/dot_general | solution.py:21
  108.5 2.1 %fusion.35 = f32[3,384]{1,0:T(4,128)S(1)} fusion(f32[3,384]{1,0:T(4,128)S(1)} %fusion.36, s32[3072]{0:T(1024)S(1)} %fusion.170, f32[1,3,24,128]{3,2,1,0:T(8,128)S(1)} %bitcast.295, f32[3,3072]{1,0:T(4,128)S(1)} %copy-done.16, f32[3072]{0:T(1024)S(1)} %get-tuple-element.29, f32[3072]{0:T(1024)S(1)} %get-tuple-element.36, f32[3,128]{1,0:T(4,128)S(1)} %neg.85), kind=kOutput, calls=%fused_computation.67 | convolution fusion | flops 43686144 | bytes 121344 | tf_op jit(solution)/shard_map/transpose(jvp())/dot_general | solution.py:21
  110.6 2.6 %collective-permute-start.6 = (f32[3,128]{1,0:T(4,128)S(1)}, f32[3,128]{1,0:T(4,128)S(1)}, u32[]{:S(2)}, u32[]{:S(2)}) collective-permute-start(f32[3,128]{1,0:T(4,128)S(1)} %get-tuple-element.37), channel_id=1, source_target_pairs={{1,0},{2,1},{3,2},{4,3},{5,4},{6,5},{7,6},{8,7},{9,8},{10,9},{11,1... | collective-permute-start | bytes 4616 | tf_op jit(solution)/shard_map/ppermute | solution.py:13
  113.2 1.9 %collective-permute-start.7 = (f32[3,128]{1,0:T(4,128)S(1)}, f32[3,128]{1,0:T(4,128)S(1)}, u32[]{:S(2)}, u32[]{:S(2)}) collective-permute-start(f32[3,128]{1,0:T(4,128)S(1)} %get-tuple-element.38), channel_id=1, source_target_pairs={{0,1},{1,2},{2,3},{3,4},{4,5},{5,6},{6,7},{7,8},{8,9},{9,10},{10,1... | collective-permute-start | bytes 4616 | tf_op jit(solution)/shard_map/ppermute | solution.py:13
  115.9 7.7 %collective-permute-done.7 = f32[3,128]{1,0:T(4,128)S(1)} collective-permute-done((f32[3,128]{1,0:T(4,128)S(1)}, f32[3,128]{1,0:T(4,128)S(1)}, u32[]{:S(2)}, u32[]{:S(2)}) %collective-permute-start.7) | collective-permute-done | bytes 1568 | tf_op jit(solution)/shard_map/ppermute | solution.py:13
  (145 shorter events, 25.7 us)
Async XLA Ops:
  0.6 44.3 %copy-start = (f32[64,64]{1,0:T(8,128)S(1)}, f32[64,64]{1,0:T(8,128)}, u32[]{:S(2)}) copy-start(f32[64,64]{1,0:T(8,128)} %param.23) | copy-start | bytes 49156
  2.3 31.2 %collective-permute-start.1 = (f32[67,128]{1,0:T(8,128)S(1)}, f32[67,128]{1,0:T(8,128)S(1)}, u32[]{:S(2)}, u32[]{:S(2)}) collective-permute-start(f32[67,128]{1,0:T(8,128)S(1)} %pad_maximum_fusion.8), channel_id=1, source_target_pairs={{1,0},{2,1},{3,2},{4,3},{5,4},{6,5},{7,6},{8,7},{9,8},{10,9},{11,1... | collective-permute-start | bytes 102920 | tf_op jit(solution)/shard_map/ppermute | solution.py:13
  8.4 25.1 %collective-permute-start = (f32[67,128]{1,0:T(8,128)S(1)}, f32[67,128]{1,0:T(8,128)S(1)}, u32[]{:S(2)}, u32[]{:S(2)}) collective-permute-start(f32[67,128]{1,0:T(8,128)S(1)} %pad_maximum_fusion.8), channel_id=1, source_target_pairs={{0,1},{1,2},{2,3},{3,4},{4,5},{5,6},{6,7},{7,8},{8,9},{9,10},{10,1... | collective-permute-start | bytes 102920 | tf_op jit(solution)/shard_map/ppermute | solution.py:13
  13.9 19.6 %copy-start.15 = (s32[24,128]{1,0:T(8,128)S(1)}, s32[24,128]{1,0:T(8,128)}, u32[]{:S(2)}) copy-start(s32[24,128]{1,0:T(8,128)} %param.15) | copy-start | bytes 36868
  13.9 19.6 %copy-start.17 = (f32[3,128]{1,0:T(4,128)S(1)}, f32[3,128]{1,0:T(4,128)}, u32[]{:S(2)}) copy-start(f32[3,128]{1,0:T(4,128)} %param.13) | copy-start | bytes 4612
  13.9 21.8 %copy-start.20 = (s32[128]{0:T(128)S(1)}, s32[128]{0:T(128)}, u32[]{:S(2)}) copy-start(s32[128]{0:T(128)} %param.16) | copy-start | bytes 1540
  13.9 21.8 %copy-start.19 = (f32[2,8,64]{2,1,0:T(8,128)S(1)}, f32[2,8,64]{2,1,0:T(8,128)}, u32[]{:S(2)}) copy-start(f32[2,8,64]{2,1,0:T(8,128)} %param.19) | copy-start | bytes 12292
  33.5 6.5 %copy-start.21 = (f32[8]{0:T(128)}, f32[8]{0:T(128)S(1)}, u32[]{:S(2)}) copy-start(f32[8]{0:T(128)S(1)} %convert_multiply_fusion) | copy-start | bytes 100
  36.9 20.6 %copy-start.7 = (f32[64,3072]{1,0:T(8,128)}, f32[64,3072]{1,0:T(8,128)S(1)}, u32[]{:S(2)}) copy-start(f32[64,3072]{1,0:T(8,128)S(1)} %convolution_bitcast_fusion.4) | copy-start | bytes 2359300
  44.4 14.1 %copy-start.1 = (f32[8,8,24,128]{3,2,1,0:T(8,128)}, f32[8,8,24,128]{3,2,1,0:T(8,128)S(1)}, u32[]{:S(2)}) copy-start(f32[8,8,24,128]{3,2,1,0:T(8,128)S(1)} %copy.21) | copy-start | bytes 2359300
  46.2 14.5 %collective-permute-start.3 = (f32[4,64,128]{2,1,0:T(8,128)S(1)}, f32[4,64,128]{2,1,0:T(8,128)S(1)}, u32[]{:S(2)}, u32[]{:S(2)}) collective-permute-start(f32[4,64,128]{2,1,0:T(8,128)S(1)} %pad_maximum_fusion.1), channel_id=1, source_target_pairs={{1,0},{2,1},{3,2},{4,3},{5,4},{6,5},{7,6},{8,7},{9,8},{10,9},{11,1... | collective-permute-start | bytes 393224 | tf_op jit(solution)/shard_map/ppermute | solution.py:13
  55.3 11.7 %collective-permute-start.2 = (f32[4,64,128]{2,1,0:T(8,128)S(1)}, f32[4,64,128]{2,1,0:T(8,128)S(1)}, u32[]{:S(2)}, u32[]{:S(2)}) collective-permute-start(f32[4,64,128]{2,1,0:T(8,128)S(1)} %pad_maximum_fusion.1), channel_id=1, source_target_pairs={{0,1},{1,2},{2,3},{3,4},{4,5},{5,6},{6,7},{7,8},{8,9},{9,10},{10,1... | collective-permute-start | bytes 393224 | tf_op jit(solution)/shard_map/ppermute | solution.py:13
  58.5 8.6 %copy-start.33 = (f32[64,3072]{1,0:T(8,128)}, f32[64,3072]{1,0:T(8,128)S(1)}, u32[]{:S(2)}) copy-start(f32[64,3072]{1,0:T(8,128)S(1)} %convolution_bitcast_fusion.8) | copy-start | bytes 2359300
  80.4 10.2 %copy-start.4 = (f32[64,24,128]{2,1,0:T(8,128)S(1)}, f32[64,24,128]{2,1,0:T(8,128)}, u32[]{:S(2)}) copy-start(f32[64,24,128]{2,1,0:T(8,128)} %copy-done.3) | copy-start | bytes 2359300
  85.5 8.0 %collective-permute-start.4 = (f32[4,64,128]{2,1,0:T(8,128)S(1)}, f32[4,64,128]{2,1,0:T(8,128)S(1)}, u32[]{:S(2)}, u32[]{:S(2)}) collective-permute-start(f32[4,64,128]{2,1,0:T(8,128)S(1)} %get-tuple-element.27), channel_id=1, source_target_pairs={{1,0},{2,1},{3,2},{4,3},{5,4},{6,5},{7,6},{8,7},{9,8},{10,9},{11,1... | collective-permute-start | bytes 393224 | tf_op jit(solution)/shard_map/ppermute | solution.py:13
  88.3 11.7 %collective-permute-start.5 = (f32[4,64,128]{2,1,0:T(8,128)S(1)}, f32[4,64,128]{2,1,0:T(8,128)S(1)}, u32[]{:S(2)}, u32[]{:S(2)}) collective-permute-start(f32[4,64,128]{2,1,0:T(8,128)S(1)} %get-tuple-element.28), channel_id=1, source_target_pairs={{0,1},{1,2},{2,3},{3,4},{4,5},{5,6},{6,7},{7,8},{8,9},{9,10},{10,1... | collective-permute-start | bytes 393224 | tf_op jit(solution)/shard_map/ppermute | solution.py:13
  92.4 7.7 %copy-start.12 = (f32[3,64,64]{2,1,0:T(8,128)S(1)}, f32[3,64,64]{2,1,0:T(8,128)}, u32[]{:S(2)}) copy-start(f32[3,64,64]{2,1,0:T(8,128)} %param.22) | copy-start | bytes 147460
  92.4 8.3 %copy-start.2 = (f32[8,8,24,128]{3,2,1,0:T(8,128)S(1)}, f32[8,8,24,128]{3,2,1,0:T(8,128)}, u32[]{:S(2)}) copy-start(f32[8,8,24,128]{3,2,1,0:T(8,128)} %copy-done.1) | copy-start | bytes 2359300
  93.6 7.6 %copy-start.6 = (f32[64,3072]{1,0:T(8,128)S(1)}, f32[64,3072]{1,0:T(8,128)}, u32[]{:S(2)}) copy-start(f32[64,3072]{1,0:T(8,128)} %copy-done.5) | copy-start | bytes 2359300
  106.0 9.2 %copy-start.24 = (f32[2,64]{1,0:T(2,128)S(1)}, f32[2,64]{1,0:T(2,128)}, u32[]{:S(2)}) copy-start(f32[2,64]{1,0:T(2,128)} %param.25) | copy-start | bytes 1540
  106.0 9.2 %copy-start.30 = (f32[64,128]{1,0:T(8,128)S(1)}, f32[64,128]{1,0:T(8,128)}, u32[]{:S(2)}) copy-start(f32[64,128]{1,0:T(8,128)} %copy-done.29) | copy-start | bytes 98308
  106.0 9.2 %copy-start.35 = (f32[128]{0:T(128)S(1)}, f32[128]{0:T(128)}, u32[]{:S(2)}) copy-start(f32[128]{0:T(128)} %convolution_bitcast_fusion.15) | copy-start | bytes 1540
  110.6 5.3 %collective-permute-start.6 = (f32[3,128]{1,0:T(4,128)S(1)}, f32[3,128]{1,0:T(4,128)S(1)}, u32[]{:S(2)}, u32[]{:S(2)}) collective-permute-start(f32[3,128]{1,0:T(4,128)S(1)} %get-tuple-element.37), channel_id=1, source_target_pairs={{1,0},{2,1},{3,2},{4,3},{5,4},{6,5},{7,6},{8,7},{9,8},{10,9},{11,1... | collective-permute-start | bytes 4616 | tf_op jit(solution)/shard_map/ppermute | solution.py:13
  113.2 10.3 %collective-permute-start.7 = (f32[3,128]{1,0:T(4,128)S(1)}, f32[3,128]{1,0:T(4,128)S(1)}, u32[]{:S(2)}, u32[]{:S(2)}) collective-permute-start(f32[3,128]{1,0:T(4,128)S(1)} %get-tuple-element.38), channel_id=1, source_target_pairs={{0,1},{1,2},{2,3},{3,4},{4,5},{5,6},{6,7},{7,8},{8,9},{9,10},{10,1... | collective-permute-start | bytes 4616 | tf_op jit(solution)/shard_map/ppermute | solution.py:13
  (20 other events, 34.4 us)
where the time goes:
time: 125 us; the launch traced here: 124 us
  matrix products  35.2 us (28%)
  local copies, waits for them, and re-layouts  30.3 us (24%)
  starting transfers between devices  28.7 us (23%)
  waiting for transfers between devices  20.5 us (16%)
  other arithmetic  7.87 us (6%)
  between operations  1.62 us (1%)
    dot_general x30, matrix products, hdot(): jnp.dot(a, b, precision=lax.Precision.HIGHEST, preferred_element_type=jnp...  34.7 us
    ppermute x8, starting transfers between devices, shifted(): return lax.ppermute(block, axis, route)  28.7 us
    ppermute x8, waiting for transfers between devices, shifted(): return lax.ppermute(block, axis, route)  20.5 us
    gather x1, local copies, waits for them, and re-layouts, body(): table_rows = jnp.take(remap, neighbours)  19.5 us
    unnamed x80, local copies, waits for them, and re-layouts  4.8 us
    dot_general x1, local copies, waits for them, and re-layouts, hdot(): jnp.dot(a, b, precision=lax.Precision.HIGHEST, preferred_element_type=jnp...  4.51 us
  transfers between devices with their start and end apart: 8, of which 3 were waited for; matrix products, arithmetic and copies ran while one was open for 24% of the time, Pallas kernels for 0%

commit v1 on v0

v1 whole, which is shorter than its diff:
```python
import functools

import jax
import jax.numpy as jnp
from jax import lax
from jax.experimental import pallas as pl
from jax.experimental.pallas import tpu as pltpu
from jax.sharding import PartitionSpec as P

RADIUS = 5.0
SOFTEN = 0.25
F32 = jnp.float32
BF16 = jnp.bfloat16
HALF = 64
CHUNK = 4
MIB = 1024 * 1024


def hdot(a, b, dims=(((1,), (0,)), ((), ()))):
    return lax.dot_general(
        a, b, dims, precision=lax.Precision.HIGHEST, preferred_element_type=F32
    )


def hdot_t(a, b):
    return hdot(a, b, (((0,), (0,)), ((), ())))


def bdot(a, b):
    return jnp.dot(a, b, preferred_element_type=F32)


def bdot_nt(a, b):
    return lax.dot_general(a, b, (((1,), (1,)), ((), ())), preferred_element_type=F32)


def high(x):
    return x.astype(BF16).astype(F32)


def split_rows(x):
    hi = x.astype(BF16)
    lo = (x - hi.astype(F32)).astype(BF16)
    return hi, lo


def stack3(x):
    hi, lo = split_rows(x)
    return jnp.concatenate([hi, lo, hi], axis=0)


def sigmoid(v):
    return 0.5 + 0.5 * jnp.tanh(0.5 * v)


def roll64(x):
    return pltpu.roll(x, HALF, 1)


def lane_low(rows):
    return lax.broadcasted_iota(jnp.int32, (rows, 128), 1) < HALF


def parity_odd(rows):
    odd = lax.rem(lax.axis_index("space"), 2)
    return jnp.full((rows, 128), odd, jnp.int32) > 0


def prep_kernel(nb_ref, gi_ref, rin_ref, rmid_ref, rout_ref, sel_ref, win_ref, wmid_ref, wout_ref):
    atoms = nb_ref.shape[1]
    slots = nb_ref.shape[0]
    rows = lax.broadcasted_iota(jnp.int32, (atoms, atoms), 0)
    perm = (rows == jnp.broadcast_to(gi_ref[...], (atoms, atoms))).astype(F32).astype(BF16)
    for k in range(slots):
        nb = jnp.broadcast_to(nb_ref[k : k + 1, :], (atoms, atoms))
        lanes = pl.ds(k * atoms, atoms)
        sel_ref[0:atoms, lanes] = (rows == nb).astype(F32).astype(BF16)
        ghost = (rows + atoms == nb).astype(F32).astype(BF16)
        sel_ref[atoms : 2 * atoms, lanes] = bdot(perm, ghost).astype(BF16)
    for layer in range(2):
        w = rin_ref[layer]
        h = high(w)
        lo = w - h
        win_ref[layer] = jnp.concatenate([h, h, lo, lo], axis=0).T.astype(BF16)
        w = rmid_ref[layer]
        h = high(w)
        wmid_ref[layer] = jnp.concatenate([h, h, w - h], axis=0).T.astype(BF16)
        w = rout_ref[layer]
        h = high(w)
        wout_ref[layer] = jnp.concatenate([h, h, w - h], axis=0).T.astype(BF16)


def basis_rows(b):
    h = high(b)
    lo = b - h
    return jnp.concatenate([h, lo, h, lo], axis=0).astype(BF16)


def radial(win, wmid, wout, b):
    v1 = bdot(win, basis_rows(b))
    z1 = v1 * sigmoid(v1)
    v2 = bdot(wmid, stack3(z1))
    z2 = v2 * sigmoid(v2)
    return bdot(wout, stack3(z2))


def silu_pair(v, t):
    s = sigmoid(v)
    z = v * s
    return z, (s + z * (1.0 - s)) * t


def radial_pair(win, wmid, wout, b, db):
    z1, t1 = silu_pair(bdot(win, basis_rows(b)), bdot(win, basis_rows(db)))
    z2, t2 = silu_pair(bdot(wmid, stack3(z1)), bdot(wmid, stack3(t1)))
    return bdot(wout, stack3(z2)), bdot(wout, stack3(t2))


def tile8(x, times):
    return jnp.concatenate([x] * times, axis=0)


def geometry(far, own, valid):
    vec = [f - o for f, o in zip(far, own)]
    r2 = vec[0] * vec[0] + vec[1] * vec[1] + vec[2] * vec[2] + SOFTEN
    inv = lax.rsqrt(r2)
    inv = inv * (1.5 - 0.5 * r2 * inv * inv)
    rho = r2 * inv
    unit = [v * inv for v in vec]
    x = jnp.minimum(rho * (1.0 / RADIUS), 1.0)
    y = 1.0 - x
    x2 = x * x
    env = y * y * y * (1.0 + x * (3.0 + x * (6.0 + x * (10.0 + x * 15.0))))
    denv = (-105.0 / RADIUS) * x2 * x2 * y * y
    f = RADIUS * inv * env * valid
    df = RADIUS * inv * (denv - env * inv) * valid
    n = (lax.broadcasted_iota(jnp.int32, rho.shape, 0) + 1).astype(F32)
    turns = n * x
    whole = jnp.floor(turns + 0.5)
    frac = (turns - whole) * jnp.pi
    parity = whole - 2.0 * jnp.floor(0.5 * whole)
    sign = 1.0 - 2.0 * parity
    q = frac * frac
    sin = frac * (
        1.0
        + q * (-1 / 6 + q * (1 / 120 + q * (-1 / 5040 + q * (1 / 362880 + q * (-1 / 39916800)))))
    )
    cos = 1.0 + q * (
        -1 / 2
        + q * (1 / 24 + q * (-1 / 720 + q * (1 / 40320 + q * (-1 / 3628800 + q * (1 / 479001600)))))
    )
    sin = sin * sign
    cos = cos * sign
    return unit, inv, sin * f, sin * df + (n * (jnp.pi / RADIUS)) * cos * f


def layer_one_kernel(
    own_ref,
    near_ref,
    far_ref,
    sel_ref,
    counts_ref,
    embed_ref,
    win_ref,
    wmid_ref,
    wout_ref,
    mix_ref,
    vec_ref,
    feats_ref,
    near_out,
    far_out,
    geom_ref,
    pre_ref,
    b_ref,
    hfar_ref,
    tab_ref,
):
    atoms = own_ref.shape[1]
    slots = counts_ref.shape[0] and sel_ref.shape[1] // atoms
    width = embed_ref.shape[1]
    species = embed_ref.shape[0]
    odd4 = parity_odd(4)
    low4 = lane_low(4)
    own = own_ref[...]
    from_far = jnp.logical_xor(odd4, jnp.logical_not(low4))
    ghost = jnp.where(from_far, far_ref[...], near_ref[...])
    table = jnp.concatenate([own, ghost], axis=1)
    for c in range(3):
        p = jnp.broadcast_to(table[c : c + 1], (8, 2 * atoms))
        h = p.astype(BF16)
        rest = p - h.astype(F32)
        m = rest.astype(BF16)
        lo = (rest - m.astype(F32)).astype(BF16)
        part = jnp.concatenate([h.astype(F32), m.astype(F32), lo.astype(F32)], axis=0)
        tab_ref[c * 24 : c * 24 + 24, :] = part
    kind = jnp.broadcast_to(table[3:4], (species, 2 * atoms))
    onehot = (
        kind == (lax.broadcasted_iota(jnp.int32, (species, 2 * atoms), 0) + 1).astype(F32)
    ).astype(F32)
    h0 = hdot_t(embed_ref[...], onehot)
    h0_hi = high(h0)
    tab_ref[72 : 72 + width, :] = h0_hi
    tab_ref[72 + width : 72 + 2 * width, :] = h0 - h0_hi
    tab = tab_ref[...].astype(BF16)
    h0_own = h0[:, :atoms]

    step = CHUNK * atoms
    own_rep = [
        jnp.concatenate([jnp.broadcast_to(own[c : c + 1], (8, atoms))] * CHUNK, axis=1)
        for c in range(3)
    ]
    counts = jnp.broadcast_to(counts_ref[...], (8, atoms))
    a_sum = jnp.zeros((width, atoms), F32)
    b_sum = [jnp.zeros((width, atoms), F32) for _ in range(3)]
    for j in range(slots // CHUNK):
        lanes = pl.ds(j * step, step)
        g = bdot(tab, sel_ref[:, lanes])
        far = [g[24 * c : 24 * c + 8] + g[24 * c + 8 : 24 * c + 16] + g[24 * c + 16 : 24 * c + 24] for c in range(3)]
        h_far = g[72 : 72 + width] + g[72 + width : 72 + 2 * width]
        hfar_ref[:, lanes] = h_far
        valid = jnp.concatenate(
            [(counts > (j * CHUNK + k)).astype(F32) for k in range(CHUNK)], axis=1
        )
        unit, inv, b, db = geometry(far, own_rep, valid)
        for c in range(3):
            geom_ref[c, :, lanes] = unit[c]
        geom_ref[3, :, lanes] = inv
        geom_ref[4, :, lanes] = b
        geom_ref[5, :, lanes] = db
        w = radial(win_ref[0], wmid_ref[0], wout_ref[0], b)
        wa = w[:width] * h_far
        wb = w[width:] * h_far
        for k in range(CHUNK):
            s = slice(k * atoms, (k + 1) * atoms)
            a_sum = a_sum + wa[:, s]
            for c in range(3):
                b_sum[c] = b_sum[c] + wb[:, s] * tile8(unit[c][:, s], width // 8)
    scale = 1.0 / jnp.sqrt(F32(slots))
    a_sum = a_sum * scale
    b_all = jnp.concatenate([x * scale for x in b_sum], axis=1)
    sq = b_all * b_all
    q = sq[:, :atoms] + sq[:, atoms : 2 * atoms] + sq[:, 2 * atoms :]
    pre = hdot_t(mix_ref[0], a_sum) + hdot_t(mix_ref[1], h0_own) + hdot_t(mix_ref[2], q)
    pre_ref[...] = pre
    b_ref[...] = b_all
    s1 = pre * sigmoid(pre)
    v1 = hdot_t(vec_ref[...], b_all)
    lo_part = jnp.concatenate([s1, v1[:, :atoms]], axis=0)
    hi_part = jnp.concatenate([v1[:, atoms : 2 * atoms], v1[:, 2 * atoms :]], axis=0)
    feats_ref[0 : 2 * width] = lo_part
    feats_ref[2 * width :] = hi_part
    pack_halves(lo_part, hi_part, near_out, far_out)


def pack_halves(lo_part, hi_part, near_out, far_out):
    rows = lo_part.shape[0]
    low = lane_low(rows)
    odd = parity_odd(rows)
    lo_roll = roll64(lo_part)
    hi_roll = roll64(hi_part)
    low_lanes = jnp.where(low, lo_part, hi_roll)
    high_lanes = jnp.where(low, lo_roll, hi_part)
    near_out[...] = jnp.where(odd, low_lanes, high_lanes)
    far_out[...] = jnp.where(odd, high_lanes, low_lanes)


def radial_two_kernel(geom_ref, win_ref, wmid_ref, wout_ref, w_ref, dw_ref):
    n = geom_ref.shape[2]
    step = CHUNK * 128
    for j in range(n // step):
        lanes = pl.ds(j * step, step)
        w, dw = radial_pair(
            win_ref[1], wmid_ref[1], wout_ref[1], geom_ref[4, :, lanes], geom_ref[5, :, lanes]
        )
        w_ref[:, lanes] = w
        dw_ref[:, lanes] = dw


def edge_gradient(unit, inv, drho, du):
    dot = unit[0] * du[0] + unit[1] * du[1] + unit[2] * du[2]
    radial_part = drho - dot * inv
    return [unit[c] * radial_part + du[c] * inv for c in range(3)]


def sum_rows(x):
    return jnp.sum(x, axis=0, keepdims=True)


def position_rows(grads):
    g = jnp.concatenate([jnp.broadcast_to(x, (8, x.shape[1])) for x in grads], axis=0)
    x = jnp.concatenate([g[0:1], g[8:9], g[16:17], jnp.zeros((5, g.shape[1]), F32)], axis=0)
    h = high(x)
    return jnp.concatenate([h, x - h], axis=0).astype(BF16)


def layer_two_kernel(
    feats_ref,
    near_ref,
    far_ref,
    sel_ref,
    geom_ref,
    w_ref,
    dw_ref,
    mix_ref,
    read_ref,
    energy_ref,
    gown_ref,
    near_out,
    far_out,
    gpos_ref,
    far_scr,
    along_scr,
):
    atoms = feats_ref.shape[1]
    width = mix_ref.shape[1]
    slots = sel_ref.shape[1] // atoms
    rows = 2 * width
    low = lane_low(rows)
    odd = parity_odd(rows)
    near = near_ref[...]
    far = far_ref[...]
    upper = jnp.where(odd, far, near)
    lower = jnp.where(odd, near, far)
    g_lo = jnp.where(low, upper, roll64(lower))
    g_hi = jnp.where(low, roll64(upper), lower)
    feats = feats_ref[...]
    table = jnp.concatenate([feats, jnp.concatenate([g_lo, g_hi], axis=0)], axis=1)
    t_hi, t_lo = split_rows(table)
    tab = jnp.concatenate([t_hi, t_lo], axis=0)
    step = CHUNK * atoms
    m = jnp.zeros((width, atoms), F32)
    for j in range(slots // CHUNK):
        lanes = pl.ds(j * step, step)
        g = bdot(tab, sel_ref[:, lanes])
        f = g[: 4 * width] + g[4 * width :]
        far_scr[:, lanes] = f
        along = f[width : 2 * width] * tile8(geom_ref[0, :, lanes], width // 8)
        along = along + f[2 * width : 3 * width] * tile8(geom_ref[1, :, lanes], width // 8)
        along = along + f[3 * width :] * tile8(geom_ref[2, :, lanes], width // 8)
        along_scr[:, lanes] = along
        msg = w_ref[0:width, lanes] * f[:width] + w_ref[width : 2 * width, lanes] * along
        for k in range(CHUNK):
            m = m + msg[:, k * atoms : (k + 1) * atoms]
    scale = 1.0 / jnp.sqrt(F32(slots))
    s1 = feats[:width]
    pre = hdot_t(mix_ref[0], m * scale) + hdot_t(mix_ref[1], s1)
    sg = sigmoid(pre)
    s2 = pre * sg
    energy_ref[...] = hdot(read_ref[0:1], s1) + hdot(read_ref[1:2], s2)
    read = read_ref[...].T
    r_one = jnp.broadcast_to(read[:, 0:1], (width, atoms))
    r_two = jnp.broadcast_to(read[:, 1:2], (width, atoms))
    gpre = r_two * (sg + s2 * (1.0 - sg))
    gm = hdot(mix_ref[0], gpre) * scale
    gs_own = r_one + hdot(mix_ref[1], gpre)
    gm_rep = jnp.concatenate([gm] * CHUNK, axis=1)
    acc = jnp.zeros((8 * width + 16, 2 * atoms), F32)
    own_pos = [jnp.zeros((1, atoms), F32) for _ in range(3)]
    for j in range(slots // CHUNK):
        lanes = pl.ds(j * step, step)
        unit = [geom_ref[c, :, lanes] for c in range(3)]
        ga = w_ref[0:width, lanes] * gm_rep
        gb = w_ref[width : 2 * width, lanes] * gm_rep
        gv = [gb * tile8(unit[c], width // 8) for c in range(3)]
        drho = gm_rep * (
            dw_ref[0:width, lanes] * far_scr[0:width, lanes]
            + dw_ref[width : 2 * width, lanes] * along_scr[:, lanes]
        )
        du = [sum_rows(gb * far_scr[(c + 1) * width : (c + 2) * width, lanes]) for c in range(3)]
        gp = edge_gradient(
            [u[0:1] for u in unit], geom_ref[3, 0:1, lanes], sum_rows(drho), du
        )
        for k in range(CHUNK):
            for c in range(3):
                own_pos[c] = own_pos[c] + gp[c][:, k * atoms : (k + 1) * atoms]
        grads = jnp.concatenate([ga] + gv, axis=0)
        hi, lo = split_rows(grads)
        acc = acc + bdot_nt(
            jnp.concatenate([hi, lo, position_rows(gp)], axis=0), sel_ref[:, lanes]
        )
    grads = acc[: 4 * width] + acc[4 * width : 8 * width]
    own = grads[:, :atoms]
    gown_ref[0:width] = own[0:width] + gs_own
    gown_ref[width:] = own[width:]
    ghost = grads[:, atoms:]
    pack_halves_by_lane(ghost[: 2 * width], ghost[2 * width :], near_out, far_out)
    pos = acc[8 * width : 8 * width + 8] + acc[8 * width + 8 :]
    centre = jnp.concatenate(own_pos + [jnp.zeros((5, atoms), F32)], axis=0)
    gpos_ref[:, :atoms] = pos[:, :atoms] - centre
    gpos_ref[:, atoms:] = pos[:, atoms:]


def pack_halves_by_lane(lo_part, hi_part, near_out, far_out):
    rows = lo_part.shape[0]
    low = lane_low(rows)
    odd = parity_odd(rows)
    to_upper = jnp.where(low, lo_part, roll64(hi_part))
    to_lower = jnp.where(low, roll64(lo_part), hi_part)
    near_out[...] = jnp.where(odd, to_lower, to_upper)
    far_out[...] = jnp.where(odd, to_upper, to_lower)


def tangent_one_kernel(geom_ref, hfar_ref, win_ref, wmid_ref, wout_ref, out_ref):
    n = geom_ref.shape[2]
    width = hfar_ref.shape[0]
    step = CHUNK * 128
    for j in range(n // step):
        lanes = pl.ds(j * step, step)
        w, dw = radial_pair(
            win_ref[0], wmid_ref[0], wout_ref[0], geom_ref[4, :, lanes], geom_ref[5, :, lanes]
        )
        h = hfar_ref[:, lanes]
        out_ref[0:width, lanes] = dw[:width] * h
        out_ref[width : 2 * width, lanes] = dw[width:] * h
        out_ref[2 * width :, lanes] = w[width:] * h


def back_one_kernel(
    gown_ref,
    near_ref,
    far_ref,
    sel_ref,
    geom_ref,
    edge_ref,
    pre_ref,
    b_ref,
    mix_ref,
    vec_ref,
    gpos_in,
    gpos_ref,
):
    atoms = gown_ref.shape[1]
    width = mix_ref.shape[1]
    slots = sel_ref.shape[1] // atoms
    rows = 2 * width
    low = lane_low(rows)
    odd = parity_odd(rows)
    near = near_ref[...]
    far = far_ref[...]
    upper = jnp.where(odd, far, near)
    lower = jnp.where(odd, near, far)
    g_lo = gown_ref[0:rows] + jnp.where(low, lower, roll64(upper))
    g_hi = gown_ref[rows:] + jnp.where(low, roll64(lower), upper)
    scale = 1.0 / jnp.sqrt(F32(slots))
    pre = pre_ref[...]
    sg = sigmoid(pre)
    gpre = g_lo[:width] * (sg + pre * sg * (1.0 - sg))
    ga = hdot(mix_ref[0], gpre) * scale
    gq = hdot(mix_ref[2], gpre)
    gv = jnp.concatenate([g_lo[width:], g_hi[:width], g_hi[width:]], axis=1)
    gb_all = hdot(vec_ref[...], gv) + 2.0 * b_ref[...] * jnp.concatenate([gq] * 3, axis=1)
    gb = [gb_all[:, c * atoms : (c + 1) * atoms] * scale for c in range(3)]
    ga_rep = jnp.concatenate([ga] * CHUNK, axis=1)
    gb_rep = [jnp.concatenate([g] * CHUNK, axis=1) for g in gb]
    step = CHUNK * atoms
    acc = jnp.zeros((16, 2 * atoms), F32)
    own_pos = [jnp.zeros((1, atoms), F32) for _ in range(3)]
    for j in range(slots // CHUNK):
        lanes = pl.ds(j * step, step)
        unit = [geom_ref[c, :, lanes] for c in range(3)]
        gbu = gb_rep[0] * tile8(unit[0], width // 8)
        gbu = gbu + gb_rep[1] * tile8(unit[1], width // 8)
        gbu = gbu + gb_rep[2] * tile8(unit[2], width // 8)
        drho = edge_ref[0:width, lanes] * ga_rep + edge_ref[width : 2 * width, lanes] * gbu
        carried = edge_ref[2 * width :, lanes]
        du = [sum_rows(carried * gb_rep[c]) for c in range(3)]
        gp = edge_gradient(
            [u[0:1] for u in unit], geom_ref[3, 0:1, lanes], sum_rows(drho), du
        )
        for k in range(CHUNK):
            for c in range(3):
                own_pos[c] = own_pos[c] + gp[c][:, k * atoms : (k + 1) * atoms]
        acc = acc + bdot_nt(position_rows(gp), sel_ref[:, lanes])
    pos = acc[0:8] + acc[8:16] + gpos_in[...]
    centre = jnp.concatenate(own_pos + [jnp.zeros((5, atoms), F32)], axis=0)
    gpos_ref[:, :atoms] = pos[:, :atoms] - centre
    gpos_ref[:, atoms:] = pos[:, atoms:]


def call(kernel, out_shapes, args, scratch=(), flops=0, transcendentals=0):
    moved = sum(x.size * x.dtype.itemsize for x in list(args) + list(out_shapes))
    return pl.pallas_call(
        kernel,
        out_shape=out_shapes,
        in_specs=[pl.BlockSpec(memory_space=pltpu.VMEM)] * len(args),
        out_specs=[pl.BlockSpec(memory_space=pltpu.VMEM)] * len(out_shapes),
        scratch_shapes=list(scratch),
        cost_estimate=pl.CostEstimate(
            flops=flops, bytes_accessed=moved, transcendentals=transcendentals
        ),
        compiler_params=pltpu.CompilerParams(vmem_limit_bytes=48 * MIB),
    )(*args)


def shape(dims, dtype=F32):
    return jax.ShapeDtypeStruct(dims, dtype)


def body(
    positions,
    species,
    neighbours,
    counts,
    ghost_index,
    embed,
    radial_in,
    radial_mid,
    radial_out,
    mix_one,
    vec_mix,
    mix_two,
    readout,
):
    atoms = positions.shape[1]
    slots = neighbours.shape[0]
    edges = slots * atoms
    nbasis, hidden = radial_in.shape[1:]
    width = embed.shape[1]
    devices = lax.axis_size("space")
    near_route = [(i, i ^ 1) for i in range(devices)]
    far_route = [(i, ((i + 1) ^ 1) - 1) for i in range(1, devices - 1)]

    def swap_near(x):
        return lax.ppermute(x, "space", near_route)

    def swap_far(x):
        return lax.ppermute(x, "space", far_route)

    own = jnp.concatenate([positions, (species + 1).astype(F32)[None]], axis=0)
    near = swap_near(own)
    far = swap_far(own)
    sel, win, wmid, wout = call(
        prep_kernel,
        [
            shape((2 * atoms, edges), BF16),
            shape((2, hidden, 4 * nbasis), BF16),
            shape((2, hidden, 3 * hidden), BF16),
            shape((2, 2 * width, 3 * hidden), BF16),
        ],
        [neighbours, ghost_index.reshape(1, atoms), radial_in, radial_mid, radial_out],
        flops=10**8,
    )
    feats, near_f, far_f, geom, pre, b_all, h_far = call(
        layer_one_kernel,
        [
            shape((4 * width, atoms)),
            shape((2 * width, atoms)),
            shape((2 * width, atoms)),
            shape((6, 8, edges)),
            shape((width, atoms)),
            shape((width, 3 * atoms)),
            shape((width, edges)),
        ],
        [own, near, far, sel, counts[None], embed, win, wmid, wout, mix_one, vec_mix],
        scratch=[pltpu.VMEM((72 + 2 * width, 2 * atoms), F32)],
        flops=10**9,
    )
    near_f = swap_near(near_f)
    far_f = swap_far(far_f)
    w, dw = call(
        radial_two_kernel,
        [shape((2 * width, edges)), shape((2 * width, edges))],
        [geom, win, wmid, wout],
        flops=2 * 10**9,
    )
    energy, g_own, near_g, far_g, gpos = call(
        layer_two_kernel,
        [
            shape((1, atoms)),
            shape((4 * width, atoms)),
            shape((2 * width, atoms)),
            shape((2 * width, atoms)),
            shape((8, 2 * atoms)),
        ],
        [feats, near_f, far_f, sel, geom, w, dw, mix_two, readout],
        scratch=[pltpu.VMEM((4 * width, edges), F32), pltpu.VMEM((width, edges), F32)],
        flops=10**9,
    )
    near_g = swap_near(near_g)
    far_g = swap_far(far_g)
    (edge,) = call(
        tangent_one_kernel,
        [shape((3 * width, edges))],
        [geom, h_far, win, wmid, wout],
        flops=2 * 10**9,
    )
    (gpos,) = call(
        back_one_kernel,
        [shape((8, 2 * atoms))],
        [g_own, near_g, far_g, sel, geom, edge, pre, b_all, mix_one, vec_mix, gpos],
        flops=10**9,
    )
    ghost = gpos[:3, atoms:]
    near_p = swap_near(ghost)
    far_p = swap_far(ghost)
    odd = lax.rem(lax.axis_index("space"), 2) == 1
    low = lax.broadcasted_iota(jnp.int32, (3, atoms), 1) < HALF
    come = jnp.where(low == odd, near_p, far_p)
    return (energy[0], -(gpos[:3, :atoms] + come))


def solution(mesh):
    placed = (
        P(None, "space"),
        P("space"),
        P(None, "space"),
        P("space"),
        P(None, "space"),
        P(),
        P(),
        P(),
        P(),
        P(),
        P(),
        P(),
        P(),
    )
    return jax.shard_map(
        body, mesh=mesh, in_specs=placed, out_specs=(P("space"), P(None, "space")), check_vma=False
    )
```

time: 125 us -> 58.9 us (0.47)
  the two profiles are of different devices: /device:TPU:128 before, /device:TPU:127 now
where the time goes in v1:
time: 58.9 us; the launch traced here: 58.1 us
  starting transfers between devices  20.5 us (35%)
  Pallas kernels  15.4 us (26%)
  waiting for transfers between devices  12.7 us (22%)
  local copies, waits for them, and re-layouts  6.86 us (12%)
  other arithmetic  1.94 us (3%)
  between operations  0.79 us (1%)
    ppermute x4, starting transfers between devices, swap_far(): return lax.ppermute(x, 'space', far_route)  19.6 us
    pallas_call x6, Pallas kernels, call(): pl.pallas_call(kernel, out_shape=out_shapes, in_specs=[pl.BlockSpec(memor...  15.4 us
    ppermute x4, waiting for transfers between devices, swap_far(): return lax.ppermute(x, 'space', far_route)  12.6 us
    unnamed x24, local copies, waits for them, and re-layouts  6.1 us
  transfers between devices with their start and end apart: 8, of which 4 were waited for; matrix products, arithmetic and copies ran while one was open for 1% of the time, Pallas kernels for 11%

profile of v1, /device:TPU:127, one launch (start us, length us, event | category | flops | bytes accessed | tf_op | source)
XLA Modules:
  0.0 58.1 jit_solution(8834840298557291128)
XLA Ops:
  0.6 0.7 %convert_bitcast_fusion = f32[1,128]{1,0:T(1,128)S(1)} fusion(s32[128]{0:T(128)} %param.14), kind=kLoop, calls=%fused_computation.4 | loop fusion | flops 256 | bytes 1024 | tf_op jit(solution)/shard_map/broadcast_in_dim | solution.py:529
  1.3 0.7 %pad_maximum_fusion.own_ref = f32[4,128]{1,0:T(4,128)S(1)} fusion(f32[1,128]{1,0:T(1,128)S(1)} %convert_bitcast_fusion, f32[3,128]{1,0:T(4,128)} %param.13), kind=kLoop, calls=%fused_computation.2 | loop fusion | flops 512 | bytes 4096 | tf_op jit(solution)/shard_map/concatenate | solution.py:529
  2.0 0.7 %collective-permute-start = (f32[4,128]{1,0:T(4,128)S(1)}, f32[4,128]{1,0:T(4,128)S(1)}, u32[]{:S(2)}, u32[]{:S(2)}) collective-permute-start(f32[4,128]{1,0:T(4,128)S(1)} %pad_maximum_fusion.own_ref), channel_id=1, source_target_pairs={{0,1},{1,0},{2,3},{3,2},{4,5},{5,4},{6,7},{7,6},{8,9},{9,8},{10,11... | collective-permute-start | bytes 6152 | tf_op jit(solution)/shard_map/ppermute | solution.py:524
  2.7 4.2 %collective-permute-start.1 = (f32[4,128]{1,0:T(4,128)S(1)}, f32[4,128]{1,0:T(4,128)S(1)}, u32[]{:S(2)}, u32[]{:S(2)}) collective-permute-start(f32[4,128]{1,0:T(4,128)S(1)} %pad_maximum_fusion.own_ref), channel_id=1, source_target_pairs={{1,2},{2,1},{3,4},{4,3},{5,6},{6,5},{7,8},{8,7},{9,10},{10,9},{11,... | collective-permute-start | bytes 6152 | tf_op jit(solution)/shard_map/ppermute | solution.py:527
  6.9 0.8 %reshape.7.gi_ref = s32[1,128]{1,0:T(1,128)S(1)} reshape(s32[2,64]{1,0:T(2,128)} %param.17) | data formatting | bytes 1024 | tf_op jit(solution)/shard_map/reshape | solution.py:540
  7.6 0.8 %copy-done.6 = f32[2,64,64]{2,1,0:T(8,128)S(1)} copy-done((f32[2,64,64]{2,1,0:T(8,128)S(1)}, f32[2,64,64]{2,1,0:T(8,128)}, u32[]{:S(2)}) %copy-start.6) | copy-done | bytes 32792
  8.5 0.8 %copy-done.7 = f32[2,64,128]{2,1,0:T(8,128)S(1)} copy-done((f32[2,64,128]{2,1,0:T(8,128)S(1)}, f32[2,64,128]{2,1,0:T(8,128)}, u32[]{:S(2)}) %copy-start.7) | copy-done | bytes 65560
  9.3 0.7 %copy-done.8 = s32[24,128]{1,0:T(8,128)S(1)} copy-done((s32[24,128]{1,0:T(8,128)S(1)}, s32[24,128]{1,0:T(8,128)}, u32[]{:S(2)}) %copy-start.8) | copy-done | bytes 12312
  10.0 0.7 %copy-done.9 = f32[2,8,64]{2,1,0:T(8,128)S(1)} copy-done((f32[2,8,64]{2,1,0:T(8,128)S(1)}, f32[2,8,64]{2,1,0:T(8,128)}, u32[]{:S(2)}) %copy-start.9) | copy-done | bytes 4120
  11.3 1.7 %collective-permute-done.1.far_ref = f32[4,128]{1,0:T(4,128)S(1)} collective-permute-done((f32[4,128]{1,0:T(4,128)S(1)}, f32[4,128]{1,0:T(4,128)S(1)}, u32[]{:S(2)}, u32[]{:S(2)}) %collective-permute-start.1) | collective-permute-done | bytes 2080 | tf_op jit(solution)/shard_map/ppermute | solution.py:527
  13.0 0.9 %copy-done = f32[3,64,64]{2,1,0:T(8,128)S(1)} copy-done((f32[3,64,64]{2,1,0:T(8,128)S(1)}, f32[3,64,64]{2,1,0:T(8,128)}, u32[]{:S(2)}) %copy-start) | copy-done | bytes 49176
  13.9 0.8 %copy-done.3 = f32[64,64]{1,0:T(8,128)S(1)} copy-done((f32[64,64]{1,0:T(8,128)S(1)}, f32[64,64]{1,0:T(8,128)}, u32[]{:S(2)}) %copy-start.3) | copy-done | bytes 16408
  14.6 0.7 %copy-done.10 = f32[6,64]{1,0:T(8,128)S(1)} copy-done((f32[6,64]{1,0:T(8,128)S(1)}, f32[6,64]{1,0:T(8,128)}, u32[]{:S(2)}) %copy-start.10) | copy-done | bytes 1560
  16.0 4.1 %shard_map.141 = (f32[256,128]{1,0:T(8,128)S(1)}, f32[128,128]{1,0:T(8,128)S(1)}, f32[128,128]{1,0:T(8,128)S(1)}, f32[6,8,3072]{2,1,0:T(8,128)S(1)}, f32[64,128]...) custom-call(f32[4,128]{1,0:T(4,128)S(1)} %pad_maximum_fusion.own_ref, ...), custom_call_target="tpu_custom_call" | custom-call | flops 1000000000 | bytes 3571712 | tf_op jit(solution)/shard_map/pallas_call | solution.py:482
  20.1 5.1 %collective-permute-start.3 = (f32[128,128]{1,0:T(8,128)S(1)}, f32[128,128]{1,0:T(8,128)S(1)}, u32[]{:S(2)}, u32[]{:S(2)}) collective-permute-start(f32[128,128]{1,0:T(8,128)S(1)} %get-tuple-element.26), channel_id=1, source_target_pairs={{1,2},{2,1},{3,4},{4,3},{5,6},{6,5},{7,8},{8,7},{9,10},{10,9},{11,... | collective-permute-start | bytes 196616 | tf_op jit(solution)/shard_map/ppermute | solution.py:527
  25.3 2.9 %shard_map.142 = (f32[128,3072]{1,0:T(8,128)S(1)}, f32[128,3072]{1,0:T(8,128)S(1)}) custom-call(f32[6,8,3072]{2,1,0:T(8,128)S(1)} %get-tuple-element.27.geom_ref, bf16[2,64,32]{2,1,0:T(8,128)(2,1)S(1)} %get-tuple-element.21.win_ref, bf16[2,64,192]{2,1,0:T(8,128)(2,1)S(1)} %get-tuple-element.22.wmid_ref, bf16[2,128,192]{2,1,0:T(8,128)(2,1)S(1)} %get-tuple-element.23.wout_ref), custom_call_target="tpu_custom_call" | custom-call | flops 2000000000 | bytes 3891200 | tf_op jit(solution)/shard_map/pallas_call | solution.py:482
  28.2 3.0 %collective-permute-done.3.far_ref = f32[128,128]{1,0:T(8,128)S(1)} collective-permute-done((f32[128,128]{1,0:T(8,128)S(1)}, f32[128,128]{1,0:T(8,128)S(1)}, u32[]{:S(2)}, u32[]{:S(2)}) %collective-permute-start.3) | collective-permute-done | bytes 65568 | tf_op jit(solution)/shard_map/ppermute | solution.py:527
  31.2 3.6 %shard_map.143 = (f32[1,128]{1,0:T(1,128)}, f32[256,128]{1,0:T(8,128)S(1)}, f32[128,128]{1,0:T(8,128)S(1)}, f32[128,128]{1,0:T(8,128)S(1)}, f32[8,256]{1,0:T(8,128)S(1)}) custom-call(f32[256,128]{1,0:T(8,128)S(1)} %get-tuple-element.24.feats_ref, f32[128,128]{1,0:T(8,128)S(1)} %collective-permute-done.2.near_ref, ...), custom_call_target="tpu_custom_call" | custom-call | flops 1000000000 | bytes 5874688 | tf_op jit(solution)/shard_map/pallas_call | solution.py:482
  34.7 5.3 %collective-permute-start.5 = (f32[128,128]{1,0:T(8,128)S(1)}, f32[128,128]{1,0:T(8,128)S(1)}, u32[]{:S(2)}, u32[]{:S(2)}) collective-permute-start(f32[128,128]{1,0:T(8,128)S(1)} %get-tuple-element.33), channel_id=1, source_target_pairs={{1,2},{2,1},{3,4},{4,3},{5,6},{6,5},{7,8},{8,7},{9,10},{10,9},{11,... | collective-permute-start | bytes 196616 | tf_op jit(solution)/shard_map/ppermute | solution.py:527
  40.0 2.9 %shard_map.144.edge_ref = f32[192,3072]{1,0:T(8,128)S(1)} custom-call(f32[6,8,3072]{2,1,0:T(8,128)S(1)} %get-tuple-element.27.geom_ref, f32[64,3072]{1,0:T(8,128)S(1)} %get-tuple-element.34.hfar_ref, bf16[2,64,32]{2,1,0:T(8,128)(2,1)S(1)} %get-tuple-element.21.win_ref, bf16[2,64,192]{2,1,0:T(8,128)(2,1)S(1)} %get-tuple-element.22.wmid_ref, ...), custom_call_target="tpu_custom_call" | custom-call | flops 2000000000 | bytes 3891200 | tf_op jit(solution)/shard_map/pallas_call | solution.py:482
  43.0 2.8 %collective-permute-done.5.far_ref = f32[128,128]{1,0:T(8,128)S(1)} collective-permute-done((f32[128,128]{1,0:T(8,128)S(1)}, f32[128,128]{1,0:T(8,128)S(1)}, u32[]{:S(2)}, u32[]{:S(2)}) %collective-permute-start.5) | collective-permute-done | bytes 65568 | tf_op jit(solution)/shard_map/ppermute | solution.py:527
  45.7 1.4 %shard_map.145 = f32[8,256]{1,0:T(8,128)S(1)} custom-call(f32[256,128]{1,0:T(8,128)S(1)} %get-tuple-element.31.gown_ref, f32[128,128]{1,0:T(8,128)S(1)} %collective-permute-done.4.near_ref, f32[128,128]{1,0:T(8,128)S(1)} %collective-permute-done.5.far_ref, bf16[256,3072]{1,0:T(8,128)(2,1)S(1)} %get-tuple-element.20.sel_ref, ...), custom_call_target="tpu_custom_call" | custom-call | flops 1000000000 | bytes 4997120 | tf_op jit(solution)/shard_map/pallas_call | solution.py:482
  47.2 5.1 %collective-permute-start.7 = (f32[3,128]{1,0:T(4,128)S(1)}, f32[3,128]{1,0:T(4,128)S(1)}, u32[]{:S(2)}, u32[]{:S(2)}) collective-permute-start(f32[3,128]{1,0:T(4,128)S(1)} %slice.9), channel_id=1, source_target_pairs={{1,2},{2,1},{3,4},{4,3},{5,6},{6,5},{7,8},{8,7},{9,10},{10,9},{11,... | collective-permute-start | bytes 4616 | tf_op jit(solution)/shard_map/ppermute | solution.py:527
  52.3 5.2 %collective-permute-done.7 = f32[3,128]{1,0:T(4,128)S(1)} collective-permute-done((f32[3,128]{1,0:T(4,128)S(1)}, f32[3,128]{1,0:T(4,128)S(1)}, u32[]{:S(2)}, u32[]{:S(2)}) %collective-permute-start.7) | collective-permute-done | bytes 1568 | tf_op jit(solution)/shard_map/ppermute | solution.py:527
  (28 shorter events, 2.0 us)
Async XLA Ops:
  2.0 9.3 %collective-permute-start = (f32[4,128]{1,0:T(4,128)S(1)}, f32[4,128]{1,0:T(4,128)S(1)}, u32[]{:S(2)}, u32[]{:S(2)}) collective-permute-start(f32[4,128]{1,0:T(4,128)S(1)} %pad_maximum_fusion.own_ref), channel_id=1, source_target_pairs={{0,1},{1,0},{2,3},{3,2},{4,5},{5,4},{6,7},{7,6},{8,9},{9,8},{10,11... | collective-permute-start | bytes 6152 | tf_op jit(solution)/shard_map/ppermute | solution.py:524
  2.7 10.3 %collective-permute-start.1 = (f32[4,128]{1,0:T(4,128)S(1)}, f32[4,128]{1,0:T(4,128)S(1)}, u32[]{:S(2)}, u32[]{:S(2)}) collective-permute-start(f32[4,128]{1,0:T(4,128)S(1)} %pad_maximum_fusion.own_ref), channel_id=1, source_target_pairs={{1,2},{2,1},{3,4},{4,3},{5,6},{6,5},{7,8},{8,7},{9,10},{10,9},{11,... | collective-permute-start | bytes 6152 | tf_op jit(solution)/shard_map/ppermute | solution.py:527
  7.6 0.8 %copy-start.6 = (f32[2,64,64]{2,1,0:T(8,128)S(1)}, f32[2,64,64]{2,1,0:T(8,128)}, u32[]{:S(2)}) copy-start(f32[2,64,64]{2,1,0:T(8,128)} %rmid_ref.1) | copy-start | bytes 98308
  8.5 0.8 %copy-start.7 = (f32[2,64,128]{2,1,0:T(8,128)S(1)}, f32[2,64,128]{2,1,0:T(8,128)}, u32[]{:S(2)}) copy-start(f32[2,64,128]{2,1,0:T(8,128)} %rout_ref.1) | copy-start | bytes 196612
  9.3 0.7 %copy-start.8 = (s32[24,128]{1,0:T(8,128)S(1)}, s32[24,128]{1,0:T(8,128)}, u32[]{:S(2)}) copy-start(s32[24,128]{1,0:T(8,128)} %nb_ref.1) | copy-start | bytes 36868
  10.0 0.7 %copy-start.9 = (f32[2,8,64]{2,1,0:T(8,128)S(1)}, f32[2,8,64]{2,1,0:T(8,128)}, u32[]{:S(2)}) copy-start(f32[2,8,64]{2,1,0:T(8,128)} %rin_ref.1) | copy-start | bytes 12292
  13.0 0.9 %copy-start = (f32[3,64,64]{2,1,0:T(8,128)S(1)}, f32[3,64,64]{2,1,0:T(8,128)}, u32[]{:S(2)}) copy-start(f32[3,64,64]{2,1,0:T(8,128)} %mix_ref.5) | copy-start | bytes 147460
  13.9 0.8 %copy-start.3 = (f32[64,64]{1,0:T(8,128)S(1)}, f32[64,64]{1,0:T(8,128)}, u32[]{:S(2)}) copy-start(f32[64,64]{1,0:T(8,128)} %vec_ref.3) | copy-start | bytes 49156
  14.6 0.7 %copy-start.10 = (f32[6,64]{1,0:T(8,128)S(1)}, f32[6,64]{1,0:T(8,128)}, u32[]{:S(2)}) copy-start(f32[6,64]{1,0:T(8,128)} %embed_ref.1) | copy-start | bytes 4612
  15.3 0.7 %copy-start.11 = (s32[128]{0:T(128)S(1)}, s32[128]{0:T(128)}, u32[]{:S(2)}) copy-start(s32[128]{0:T(128)} %param.16) | copy-start | bytes 1540
  20.0 8.1 %collective-permute-start.2 = (f32[128,128]{1,0:T(8,128)S(1)}, f32[128,128]{1,0:T(8,128)S(1)}, u32[]{:S(2)}, u32[]{:S(2)}) collective-permute-start(f32[128,128]{1,0:T(8,128)S(1)} %get-tuple-element.25), channel_id=1, source_target_pairs={{0,1},{1,0},{2,3},{3,2},{4,5},{5,4},{6,7},{7,6},{8,9},{9,8},{10,11... | collective-permute-start | bytes 196616 | tf_op jit(solution)/shard_map/ppermute | solution.py:524
  20.1 11.0 %collective-permute-start.3 = (f32[128,128]{1,0:T(8,128)S(1)}, f32[128,128]{1,0:T(8,128)S(1)}, u32[]{:S(2)}, u32[]{:S(2)}) collective-permute-start(f32[128,128]{1,0:T(8,128)S(1)} %get-tuple-element.26), channel_id=1, source_target_pairs={{1,2},{2,1},{3,4},{4,3},{5,6},{6,5},{7,8},{8,7},{9,10},{10,9},{11,... | collective-permute-start | bytes 196616 | tf_op jit(solution)/shard_map/ppermute | solution.py:527
  25.2 5.9 %copy-start.2 = (f32[2,64,64]{2,1,0:T(8,128)S(1)}, f32[2,64,64]{2,1,0:T(8,128)}, u32[]{:S(2)}) copy-start(f32[2,64,64]{2,1,0:T(8,128)} %mix_ref.4) | copy-start | bytes 98308
  25.2 5.9 %copy-start.5 = (f32[2,64]{1,0:T(2,128)S(1)}, f32[2,64]{1,0:T(2,128)}, u32[]{:S(2)}) copy-start(f32[2,64]{1,0:T(2,128)} %read_ref.1) | copy-start | bytes 1540
  34.7 8.2 %collective-permute-start.4 = (f32[128,128]{1,0:T(8,128)S(1)}, f32[128,128]{1,0:T(8,128)S(1)}, u32[]{:S(2)}, u32[]{:S(2)}) collective-permute-start(f32[128,128]{1,0:T(8,128)S(1)} %get-tuple-element.32), channel_id=1, source_target_pairs={{0,1},{1,0},{2,3},{3,2},{4,5},{5,4},{6,7},{7,6},{8,9},{9,8},{10,11... | collective-permute-start | bytes 196616 | tf_op jit(solution)/shard_map/ppermute | solution.py:524
  34.7 11.0 %collective-permute-start.5 = (f32[128,128]{1,0:T(8,128)S(1)}, f32[128,128]{1,0:T(8,128)S(1)}, u32[]{:S(2)}, u32[]{:S(2)}) collective-permute-start(f32[128,128]{1,0:T(8,128)S(1)} %get-tuple-element.33), channel_id=1, source_target_pairs={{1,2},{2,1},{3,4},{4,3},{5,6},{6,5},{7,8},{8,7},{9,10},{10,9},{11,... | collective-permute-start | bytes 196616 | tf_op jit(solution)/shard_map/ppermute | solution.py:527
  40.0 5.7 %copy-start.1 = (f32[3,64,64]{2,1,0:T(8,128)S(1)}, f32[3,64,64]{2,1,0:T(8,128)}, u32[]{:S(2)}) copy-start(f32[3,64,64]{2,1,0:T(8,128)} %mix_ref.5) | copy-start | bytes 147460
  40.0 5.7 %copy-start.4 = (f32[64,64]{1,0:T(8,128)S(1)}, f32[64,64]{1,0:T(8,128)}, u32[]{:S(2)}) copy-start(f32[64,64]{1,0:T(8,128)} %vec_ref.3) | copy-start | bytes 49156
  47.1 5.2 %collective-permute-start.6 = (f32[3,128]{1,0:T(4,128)S(1)}, f32[3,128]{1,0:T(4,128)S(1)}, u32[]{:S(2)}, u32[]{:S(2)}) collective-permute-start(f32[3,128]{1,0:T(4,128)S(1)} %slice.9), channel_id=1, source_target_pairs={{0,1},{1,0},{2,3},{3,2},{4,5},{5,4},{6,7},{7,6},{8,9},{9,8},{10,11... | collective-permute-start | bytes 4616 | tf_op jit(solution)/shard_map/ppermute | solution.py:524
  47.2 10.3 %collective-permute-start.7 = (f32[3,128]{1,0:T(4,128)S(1)}, f32[3,128]{1,0:T(4,128)S(1)}, u32[]{:S(2)}, u32[]{:S(2)}) collective-permute-start(f32[3,128]{1,0:T(4,128)S(1)} %slice.9), channel_id=1, source_target_pairs={{1,2},{2,1},{3,4},{4,3},{5,6},{6,5},{7,8},{8,7},{9,10},{10,9},{11,... | collective-permute-start | bytes 4616 | tf_op jit(solution)/shard_map/ppermute | solution.py:527

commit v2 on v1

--- a/solution.py
+++ b/solution.py
@@ -66,11 +66,79 @@
     return jnp.full((rows, 128), odd, jnp.int32) > 0
 
 
-def prep_kernel(nb_ref, gi_ref, rin_ref, rmid_ref, rout_ref, sel_ref, win_ref, wmid_ref, wout_ref):
+def pack_kernel(pos_hbm, kind_hbm, own_ref, pos_ref, kind_ref, sems):
+    copies = [
+        pltpu.make_async_copy(pos_hbm, pos_ref, sems.at[0]),
+        pltpu.make_async_copy(kind_hbm, kind_ref, sems.at[1]),
+    ]
+    for c in copies:
+        c.start()
+    for c in copies:
+        c.wait()
+    own_ref[0:3, :] = pos_ref[...]
+    own_ref[3:4, :] = (kind_ref[...] + 1).astype(F32)
+
+
+def prep_kernel(
+    nb_hbm,
+    gi_hbm,
+    rin_hbm,
+    rmid_hbm,
+    rout_hbm,
+    counts_hbm,
+    embed_hbm,
+    mix_one_hbm,
+    vec_hbm,
+    mix_two_hbm,
+    read_hbm,
+    sel_ref,
+    win_ref,
+    wmid_ref,
+    wout_ref,
+    counts_ref,
+    embed_ref,
+    mix_one_ref,
+    vec_ref,
+    mix_two_ref,
+    read_ref,
+    nb_ref,
+    gi_ref,
+    rin_ref,
+    rmid_ref,
+    rout_ref,
+    sems,
+):
+    moves = [
+        (nb_hbm, nb_ref),
+        (gi_hbm, gi_ref),
+        (rin_hbm, rin_ref),
+        (rmid_hbm, rmid_ref),
+        (rout_hbm, rout_ref),
+        (counts_hbm, counts_ref),
+        (embed_hbm, embed_ref),
+        (mix_one_hbm, mix_one_ref),
+        (vec_hbm, vec_ref),
+        (mix_two_hbm, mix_two_ref),
+        (read_hbm, read_ref),
+    ]
+    copies = [
+        pltpu.make_async_copy(src, dst, sems.at[i]) for i, (src, dst) in enumerate(moves)
+    ]
+    for c in copies:
+        c.start()
+    for c in copies:
+        c.wait()
     atoms = nb_ref.shape[1]
     slots = nb_ref.shape[0]
     rows = lax.broadcasted_iota(jnp.int32, (atoms, atoms), 0)
-    perm = (rows == jnp.broadcast_to(gi_ref[...], (atoms, atoms))).astype(F32).astype(BF16)
+    half_rows = lax.broadcasted_iota(jnp.int32, (atoms, HALF), 0)
+    perm = jnp.concatenate(
+        [
+            (half_rows == jnp.broadcast_to(gi_ref[i : i + 1, :], (atoms, HALF))).astype(F32)
+            for i in range(2)
+        ],
+        axis=1,
+    ).astype(BF16)
     for k in range(slots):
         nb = jnp.broadcast_to(nb_ref[k : k + 1, :], (atoms, atoms))
         lanes = pl.ds(k * atoms, atoms)
@@ -427,7 +495,8 @@
     mix_ref,
     vec_ref,
     gpos_in,
-    gpos_ref,
+    gown_out,
+    ghost_out,
 ):
     atoms = gown_ref.shape[1]
     width = mix_ref.shape[1]
@@ -473,16 +542,18 @@
         acc = acc + bdot_nt(position_rows(gp), sel_ref[:, lanes])
     pos = acc[0:8] + acc[8:16] + gpos_in[...]
     centre = jnp.concatenate(own_pos + [jnp.zeros((5, atoms), F32)], axis=0)
-    gpos_ref[:, :atoms] = pos[:, :atoms] - centre
-    gpos_ref[:, atoms:] = pos[:, atoms:]
-
-
-def call(kernel, out_shapes, args, scratch=(), flops=0, transcendentals=0):
+    gown_out[...] = pos[:, :atoms] - centre
+    ghost_out[...] = pos[:, atoms:]
+
+
+def call(kernel, out_shapes, args, scratch=(), flops=0, transcendentals=0, space=pltpu.VMEM):
+    if space is pltpu.HBM:
+        args = [pltpu.with_memory_space_constraint(x, pltpu.HBM) for x in args]
     moved = sum(x.size * x.dtype.itemsize for x in list(args) + list(out_shapes))
     return pl.pallas_call(
         kernel,
         out_shape=out_shapes,
-        in_specs=[pl.BlockSpec(memory_space=pltpu.VMEM)] * len(args),
+        in_specs=[pl.BlockSpec(memory_space=space)] * len(args),
         out_specs=[pl.BlockSpec(memory_space=pltpu.VMEM)] * len(out_shapes),
         scratch_shapes=list(scratch),
         cost_estimate=pl.CostEstimate(
@@ -526,19 +597,36 @@
     def swap_far(x):
         return lax.ppermute(x, "space", far_route)
 
-    own = jnp.concatenate([positions, (species + 1).astype(F32)[None]], axis=0)
+    own = call(
+        pack_kernel,
+        [shape((4, atoms))],
+        [positions, species[None]],
+        scratch=[
+            pltpu.VMEM((3, atoms), F32),
+            pltpu.VMEM((1, atoms), jnp.int32),
+            pltpu.SemaphoreType.DMA((2,)),
+        ],
+        space=pltpu.HBM,
+    )[0]
     near = swap_near(own)
     far = swap_far(own)
-    sel, win, wmid, wout = call(
+    weights = [radial_in, radial_mid, radial_out]
+    passed = [counts[None], embed, mix_one, vec_mix, mix_two, readout]
+    moved = [neighbours, ghost_index] + weights + passed
+    sel, win, wmid, wout, counts, embed, mix_one, vec_mix, mix_two, readout = call(
         prep_kernel,
         [
             shape((2 * atoms, edges), BF16),
             shape((2, hidden, 4 * nbasis), BF16),
             shape((2, hidden, 3 * hidden), BF16),
             shape((2, 2 * width, 3 * hidden), BF16),
-        ],
-        [neighbours, ghost_index.reshape(1, atoms), radial_in, radial_mid, radial_out],
+        ]
+        + [shape(x.shape, x.dtype) for x in passed],
+        moved,
+        scratch=[pltpu.VMEM(x.shape, x.dtype) for x in [neighbours, ghost_index] + weights]
+        + [pltpu.SemaphoreType.DMA((len(moved),))],
         flops=10**8,
+        space=pltpu.HBM,
     )
     feats, near_f, far_f, geom, pre, b_all, h_far = call(
         layer_one_kernel,
@@ -551,7 +639,7 @@
             shape((width, 3 * atoms)),
             shape((width, edges)),
         ],
-        [own, near, far, sel, counts[None], embed, win, wmid, wout, mix_one, vec_mix],
+        [own, near, far, sel, counts, embed, win, wmid, wout, mix_one, vec_mix],
         scratch=[pltpu.VMEM((72 + 2 * width, 2 * atoms), F32)],
         flops=10**9,
     )
@@ -584,19 +672,18 @@
         [geom, h_far, win, wmid, wout],
         flops=2 * 10**9,
     )
-    (gpos,) = call(
+    g_centre, ghost = call(
         back_one_kernel,
-        [shape((8, 2 * atoms))],
+        [shape((8, atoms)), shape((8, atoms))],
         [g_own, near_g, far_g, sel, geom, edge, pre, b_all, mix_one, vec_mix, gpos],
         flops=10**9,
     )
-    ghost = gpos[:3, atoms:]
     near_p = swap_near(ghost)
     far_p = swap_far(ghost)
     odd = lax.rem(lax.axis_index("space"), 2) == 1
     low = lax.broadcasted_iota(jnp.int32, (3, atoms), 1) < HALF
-    come = jnp.where(low == odd, near_p, far_p)
-    return (energy[0], -(gpos[:3, :atoms] + come))
+    come = jnp.where(low == odd, near_p[:3], far_p[:3])
+    return (energy[0], -(g_centre[:3] + come))
 
 
 def solution(mesh):

time: 58.9 us -> 54.8 us (0.930)
  local copies, waits for them, and re-layouts: 6.86 us -> 0 us
  waiting for transfers between devices: 12.7 us -> 17.8 us
  starting transfers between devices: 20.5 us -> 18.1 us
  Pallas kernels: 15.4 us -> 17.3 us
  other arithmetic: 1.94 us -> 0.59 us
    unnamed x24 -> x0, local copies, waits for them, and re-layouts: 6.1 us -> none
    ppermute x4, waiting for transfers between devices: 12.6 us -> 17.8 us  [swap_far(): return lax.ppermute(x, 'space', far_route)]
    ppermute x4, starting transfers between devices: 19.6 us -> 17.1 us  [swap_far(): return lax.ppermute(x, 'space', far_route)]
    pallas_call x6 -> x7, Pallas kernels: 15.4 us -> 17.3 us  [call(): pl.pallas_call(kernel, out_shape=out_shapes, in_specs=[pl.BlockSpec(memor...]
    reshape x1 -> x0, local copies, waits for them, and re-layouts: 0.76 us -> none  [body(): ghost_index.reshape(1, atoms)]
    concatenate x1 -> x0, other arithmetic: 0.69 us -> none  [body(): own = jnp.concatenate([positions, (species + 1).astype(F32)[None]], axis=0)]
    broadcast_in_dim x1 -> x0, other arithmetic: 0.66 us -> none  [body(): own = jnp.concatenate([positions, (species + 1).astype(F32)[None]], axis=0)]
  transfers between devices with their start and end apart: 8 -> 8, of which waited for: 4 -> 4; matrix products, arithmetic and copies ran while one was open for 1% -> 0% of each run, Pallas kernels for 11% -> 14%
where the time goes in v2:
time: 54.8 us; the launch traced here: 54.5 us
  starting transfers between devices  18.1 us (33%)
  waiting for transfers between devices  17.8 us (32%)
  Pallas kernels  17.3 us (32%)
  between operations  0.75 us (1%)
  other arithmetic  0.59 us (1%)
    ppermute x4, waiting for transfers between devices, swap_far(): return lax.ppermute(x, 'space', far_route)  17.8 us
    pallas_call x7, Pallas kernels, call(): pl.pallas_call(kernel, out_shape=out_shapes, in_specs=[pl.BlockSpec(memor...  17.3 us
    ppermute x4, starting transfers between devices, swap_far(): return lax.ppermute(x, 'space', far_route)  17.1 us
  transfers between devices with their start and end apart: 8, of which 4 were waited for; matrix products, arithmetic and copies ran while one was open for 0% of the time, Pallas kernels for 14%

profile of v2, /device:TPU:127, one launch (start us, length us, event | category | flops | bytes accessed | tf_op | source)
XLA Modules:
  0.0 54.5 jit_solution(90058554882129736)
XLA Ops:
  0.6 0.7 %shard_map.140.own_ref = f32[4,128]{1,0:T(4,128)S(1)} custom-call(f32[3,128]{1,0:T(4,128)} %pos_hbm.1, s32[1,128]{1,0:T(1,128)} %bitcast.3), custom_call_target="tpu_custom_call" | custom-call | bytes 4096 | tf_op jit(solution)/shard_map/pallas_call | solution.py:553
  1.3 0.8 %collective-permute-start = (f32[4,128]{1,0:T(4,128)S(1)}, f32[4,128]{1,0:T(4,128)S(1)}, u32[]{:S(2)}, u32[]{:S(2)}) collective-permute-start(f32[4,128]{1,0:T(4,128)S(1)} %shard_map.140.own_ref), channel_id=1, source_target_pairs={{0,1},{1,0},{2,3},{3,2},{4,5},{5,4},{6,7},{7,6},{8,9},{9,8},{10,11... | collective-permute-start | bytes 6152 | tf_op jit(solution)/shard_map/ppermute | solution.py:595
  2.1 4.2 %collective-permute-start.1 = (f32[4,128]{1,0:T(4,128)S(1)}, f32[4,128]{1,0:T(4,128)S(1)}, u32[]{:S(2)}, u32[]{:S(2)}) collective-permute-start(f32[4,128]{1,0:T(4,128)S(1)} %shard_map.140.own_ref), channel_id=1, source_target_pairs={{1,2},{2,1},{3,4},{4,3},{5,6},{6,5},{7,8},{8,7},{9,10},{10,9},{11,... | collective-permute-start | bytes 6152 | tf_op jit(solution)/shard_map/ppermute | solution.py:598
  6.3 1.7 %shard_map.141 = (bf16[256,3072]{1,0:T(8,128)(2,1)S(1)}, bf16[2,64,32]{2,1,0:T(8,128)(2,1)S(1)}, bf16[2,64,192]{2,1,0:T(8,128)(2,1)S(1)}, bf16[2,128,192]{2,1,0:...) custom-call(s32[24,128]{1,0:T(8,128)} %nb_hbm.1, ...), custom_call_target="tpu_custom_call" | custom-call | flops 100000000 | bytes 2045440 | tf_op jit(solution)/shard_map/pallas_call | solution.py:553
  8.1 0.0 collective-permute-done.near_ref
  8.1 4.4 %collective-permute-done.1.far_ref = f32[4,128]{1,0:T(4,128)S(1)} collective-permute-done((f32[4,128]{1,0:T(4,128)S(1)}, f32[4,128]{1,0:T(4,128)S(1)}, u32[]{:S(2)}, u32[]{:S(2)}) %collective-permute-start.1) | collective-permute-done | bytes 2080 | tf_op jit(solution)/shard_map/ppermute | solution.py:598
  12.4 4.1 %shard_map.142 = (f32[256,128]{1,0:T(8,128)S(1)}, f32[128,128]{1,0:T(8,128)S(1)}, f32[128,128]{1,0:T(8,128)S(1)}, f32[6,8,3072]{2,1,0:T(8,128)S(1)}, f32[64,128]...) custom-call(f32[4,128]{1,0:T(4,128)S(1)} %shard_map.140.own_ref, ...), custom_call_target="tpu_custom_call" | custom-call | flops 1000000000 | bytes 3571712 | tf_op jit(solution)/shard_map/pallas_call | solution.py:553
  16.5 0.1 collective-permute-start.2
  16.6 4.2 %collective-permute-start.3 = (f32[128,128]{1,0:T(8,128)S(1)}, f32[128,128]{1,0:T(8,128)S(1)}, u32[]{:S(2)}, u32[]{:S(2)}) collective-permute-start(f32[128,128]{1,0:T(8,128)S(1)} %get-tuple-element.38), channel_id=1, source_target_pairs={{1,2},{2,1},{3,4},{4,3},{5,6},{6,5},{7,8},{8,7},{9,10},{10,9},{11,... | collective-permute-start | bytes 196616 | tf_op jit(solution)/shard_map/ppermute | solution.py:598
  20.8 2.9 %shard_map.143 = (f32[128,3072]{1,0:T(8,128)S(1)}, f32[128,3072]{1,0:T(8,128)S(1)}) custom-call(f32[6,8,3072]{2,1,0:T(8,128)S(1)} %get-tuple-element.39.geom_ref, bf16[2,64,32]{2,1,0:T(8,128)(2,1)S(1)} %get-tuple-element.31.win_ref, bf16[2,64,192]{2,1,0:T(8,128)(2,1)S(1)} %get-tuple-element.32.wmid_ref, bf16[2,128,192]{2,1,0:T(8,128)(2,1)S(1)} %get-tuple-element.33.wout_ref), custom_call_target="tpu_custom_call" | custom-call | flops 2000000000 | bytes 3891200 | tf_op jit(solution)/shard_map/pallas_call | solution.py:553
  23.8 0.0 collective-permute-done.2.near_ref
  23.8 3.8 %collective-permute-done.3.far_ref = f32[128,128]{1,0:T(8,128)S(1)} collective-permute-done((f32[128,128]{1,0:T(8,128)S(1)}, f32[128,128]{1,0:T(8,128)S(1)}, u32[]{:S(2)}, u32[]{:S(2)}) %collective-permute-start.3) | collective-permute-done | bytes 65568 | tf_op jit(solution)/shard_map/ppermute | solution.py:598
  27.6 3.6 %shard_map.144 = (f32[1,128]{1,0:T(1,128)}, f32[256,128]{1,0:T(8,128)S(1)}, f32[128,128]{1,0:T(8,128)S(1)}, f32[128,128]{1,0:T(8,128)S(1)}, f32[8,256]{1,0:T(8,128)S(1)}) custom-call(f32[256,128]{1,0:T(8,128)S(1)} %get-tuple-element.36.feats_ref, f32[128,128]{1,0:T(8,128)S(1)} %collective-permute-done.2.near_ref, ...), custom_call_target="tpu_custom_call" | custom-call | flops 1000000000 | bytes 5874688 | tf_op jit(solution)/shard_map/pallas_call | solution.py:553
  31.2 0.0 collective-permute-start.4
  31.2 4.4 %collective-permute-start.5 = (f32[128,128]{1,0:T(8,128)S(1)}, f32[128,128]{1,0:T(8,128)S(1)}, u32[]{:S(2)}, u32[]{:S(2)}) collective-permute-start(f32[128,128]{1,0:T(8,128)S(1)} %get-tuple-element.47), channel_id=1, source_target_pairs={{1,2},{2,1},{3,4},{4,3},{5,6},{6,5},{7,8},{8,7},{9,10},{10,9},{11,... | collective-permute-start | bytes 196616 | tf_op jit(solution)/shard_map/ppermute | solution.py:598
  35.7 2.9 %shard_map.145.edge_ref = f32[192,3072]{1,0:T(8,128)S(1)} custom-call(f32[6,8,3072]{2,1,0:T(8,128)S(1)} %get-tuple-element.39.geom_ref, f32[64,3072]{1,0:T(8,128)S(1)} %get-tuple-element.48.hfar_ref, bf16[2,64,32]{2,1,0:T(8,128)(2,1)S(1)} %get-tuple-element.31.win_ref, bf16[2,64,192]{2,1,0:T(8,128)(2,1)S(1)} %get-tuple-element.32.wmid_ref, ...), custom_call_target="tpu_custom_call" | custom-call | flops 2000000000 | bytes 3891200 | tf_op jit(solution)/shard_map/pallas_call | solution.py:553
  38.6 0.0 collective-permute-done.4.near_ref
  38.6 3.6 %collective-permute-done.5.far_ref = f32[128,128]{1,0:T(8,128)S(1)} collective-permute-done((f32[128,128]{1,0:T(8,128)S(1)}, f32[128,128]{1,0:T(8,128)S(1)}, u32[]{:S(2)}, u32[]{:S(2)}) %collective-permute-start.5) | collective-permute-done | bytes 65568 | tf_op jit(solution)/shard_map/ppermute | solution.py:598
  42.2 1.4 %shard_map.146 = (f32[8,128]{1,0:T(8,128)S(1)}, f32[8,128]{1,0:T(8,128)S(1)}) custom-call(f32[256,128]{1,0:T(8,128)S(1)} %get-tuple-element.45.gown_ref, f32[128,128]{1,0:T(8,128)S(1)} %collective-permute-done.4.near_ref, f32[128,128]{1,0:T(8,128)S(1)} %collective-permute-done.5.far_ref, bf16[256,3072]{1,0:T(8,128)(2,1)S(1)} %get-tuple-element.28.sel_ref, ...), custom_call_target="tpu_custom_call" | custom-call | flops 1000000000 | bytes 4997120 | tf_op jit(solution)/shard_map/pallas_call | solution.py:553
  43.6 4.2 %collective-permute-start.7 = (f32[8,128]{1,0:T(8,128)S(1)}, f32[8,128]{1,0:T(8,128)S(1)}, u32[]{:S(2)}, u32[]{:S(2)}) collective-permute-start(f32[8,128]{1,0:T(8,128)S(1)} %get-tuple-element.53), channel_id=1, source_target_pairs={{1,2},{2,1},{3,4},{4,3},{5,6},{6,5},{7,8},{8,7},{9,10},{10,9},{11,... | collective-permute-start | bytes 12296 | tf_op jit(solution)/shard_map/ppermute | solution.py:598
  47.8 0.1 collective-permute-start.6
  48.0 6.0 %collective-permute-done.7 = f32[8,128]{1,0:T(8,128)S(1)} collective-permute-done((f32[8,128]{1,0:T(8,128)S(1)}, f32[8,128]{1,0:T(8,128)S(1)}, u32[]{:S(2)}, u32[]{:S(2)}) %collective-permute-start.7) | collective-permute-done | bytes 4128 | tf_op jit(solution)/shard_map/ppermute | solution.py:598
  53.9 0.0 collective-permute-done.6
  53.9 0.6 %add_negate_fusion = f32[3,128]{1,0:T(4,128)} fusion(f32[8,128]{1,0:T(8,128)S(1)} %collective-permute-done.7, f32[8,128]{1,0:T(8,128)S(1)} %collective-permute-done.6, f32[8,128]{1,0:T(8,128)S(1)} %get-tuple-element.52, pred[128]{0:T(512)(128)(4,1)S(1)} %compare_compare_fusion), kind=kLoop, calls=%fused_computation | loop fusion | flops 1152 | bytes 6272 | tf_op jit(solution)/shard_map/neg | solution.py:686
  (1 shorter events, 0.0 us)
Async XLA Ops:
  1.3 6.7 %collective-permute-start = (f32[4,128]{1,0:T(4,128)S(1)}, f32[4,128]{1,0:T(4,128)S(1)}, u32[]{:S(2)}, u32[]{:S(2)}) collective-permute-start(f32[4,128]{1,0:T(4,128)S(1)} %shard_map.140.own_ref), channel_id=1, source_target_pairs={{0,1},{1,0},{2,3},{3,2},{4,5},{5,4},{6,7},{7,6},{8,9},{9,8},{10,11... | collective-permute-start | bytes 6152 | tf_op jit(solution)/shard_map/ppermute | solution.py:595
  2.1 10.3 %collective-permute-start.1 = (f32[4,128]{1,0:T(4,128)S(1)}, f32[4,128]{1,0:T(4,128)S(1)}, u32[]{:S(2)}, u32[]{:S(2)}) collective-permute-start(f32[4,128]{1,0:T(4,128)S(1)} %shard_map.140.own_ref), channel_id=1, source_target_pairs={{1,2},{2,1},{3,4},{4,3},{5,6},{6,5},{7,8},{8,7},{9,10},{10,9},{11,... | collective-permute-start | bytes 6152 | tf_op jit(solution)/shard_map/ppermute | solution.py:598
  16.5 7.3 %collective-permute-start.2 = (f32[128,128]{1,0:T(8,128)S(1)}, f32[128,128]{1,0:T(8,128)S(1)}, u32[]{:S(2)}, u32[]{:S(2)}) collective-permute-start(f32[128,128]{1,0:T(8,128)S(1)} %get-tuple-element.37), channel_id=1, source_target_pairs={{0,1},{1,0},{2,3},{3,2},{4,5},{5,4},{6,7},{7,6},{8,9},{9,8},{10,11... | collective-permute-start | bytes 196616 | tf_op jit(solution)/shard_map/ppermute | solution.py:595
  16.6 11.0 %collective-permute-start.3 = (f32[128,128]{1,0:T(8,128)S(1)}, f32[128,128]{1,0:T(8,128)S(1)}, u32[]{:S(2)}, u32[]{:S(2)}) collective-permute-start(f32[128,128]{1,0:T(8,128)S(1)} %get-tuple-element.38), channel_id=1, source_target_pairs={{1,2},{2,1},{3,4},{4,3},{5,6},{6,5},{7,8},{8,7},{9,10},{10,9},{11,... | collective-permute-start | bytes 196616 | tf_op jit(solution)/shard_map/ppermute | solution.py:598
  31.2 7.4 %collective-permute-start.4 = (f32[128,128]{1,0:T(8,128)S(1)}, f32[128,128]{1,0:T(8,128)S(1)}, u32[]{:S(2)}, u32[]{:S(2)}) collective-permute-start(f32[128,128]{1,0:T(8,128)S(1)} %get-tuple-element.46), channel_id=1, source_target_pairs={{0,1},{1,0},{2,3},{3,2},{4,5},{5,4},{6,7},{7,6},{8,9},{9,8},{10,11... | collective-permute-start | bytes 196616 | tf_op jit(solution)/shard_map/ppermute | solution.py:595
  31.2 11.0 %collective-permute-start.5 = (f32[128,128]{1,0:T(8,128)S(1)}, f32[128,128]{1,0:T(8,128)S(1)}, u32[]{:S(2)}, u32[]{:S(2)}) collective-permute-start(f32[128,128]{1,0:T(8,128)S(1)} %get-tuple-element.47), channel_id=1, source_target_pairs={{1,2},{2,1},{3,4},{4,3},{5,6},{6,5},{7,8},{8,7},{9,10},{10,9},{11,... | collective-permute-start | bytes 196616 | tf_op jit(solution)/shard_map/ppermute | solution.py:598
  43.6 10.4 %collective-permute-start.7 = (f32[8,128]{1,0:T(8,128)S(1)}, f32[8,128]{1,0:T(8,128)S(1)}, u32[]{:S(2)}, u32[]{:S(2)}) collective-permute-start(f32[8,128]{1,0:T(8,128)S(1)} %get-tuple-element.53), channel_id=1, source_target_pairs={{1,2},{2,1},{3,4},{4,3},{5,6},{6,5},{7,8},{8,7},{9,10},{10,9},{11,... | collective-permute-start | bytes 12296 | tf_op jit(solution)/shard_map/ppermute | solution.py:598
  47.8 6.1 %collective-permute-start.6 = (f32[8,128]{1,0:T(8,128)S(1)}, f32[8,128]{1,0:T(8,128)S(1)}, u32[]{:S(2)}, u32[]{:S(2)}) collective-permute-start(f32[8,128]{1,0:T(8,128)S(1)} %get-tuple-element.53), channel_id=1, source_target_pairs={{0,1},{1,0},{2,3},{3,2},{4,5},{5,4},{6,7},{7,6},{8,9},{9,8},{10,11... | collective-permute-start | bytes 12296 | tf_op jit(solution)/shard_map/ppermute | solution.py:595

commit v3 on v2

--- a/solution.py
+++ b/solution.py
@@ -12,7 +12,7 @@
 F32 = jnp.float32
 BF16 = jnp.bfloat16
 HALF = 64
-CHUNK = 4
+CHUNK = 24
 MIB = 1024 * 1024
 
 

time: 54.8 us -> 52.7 us (0.962)
  Pallas kernels: 17.3 us -> 12.3 us
  waiting for transfers between devices: 17.8 us -> 20.9 us
    pallas_call x7, Pallas kernels: 17.3 us -> 12.3 us  [call(): pl.pallas_call(kernel, out_shape=out_shapes, in_specs=[pl.BlockSpec(memor...]
    ppermute x4, waiting for transfers between devices: 17.8 us -> 20.8 us  [swap_far(): return lax.ppermute(x, 'space', far_route)]
  transfers between devices with their start and end apart: 8 -> 8, of which waited for: 4 -> 4; matrix products, arithmetic and copies ran while one was open for 0% -> 0% of each run, Pallas kernels for 14% -> 9%
where the time goes in v3:
time: 52.7 us; the launch traced here: 52.4 us
  waiting for transfers between devices  20.9 us (40%)
  starting transfers between devices  17.9 us (34%)
  Pallas kernels  12.3 us (23%)
  between operations  0.74 us (1%)
  other arithmetic  0.59 us (1%)
    ppermute x4, waiting for transfers between devices, swap_far(): return lax.ppermute(x, 'space', far_route)  20.8 us
    ppermute x4, starting transfers between devices, swap_far(): return lax.ppermute(x, 'space', far_route)  16.9 us
    pallas_call x7, Pallas kernels, call(): pl.pallas_call(kernel, out_shape=out_shapes, in_specs=[pl.BlockSpec(memor...  12.3 us
  transfers between devices with their start and end apart: 8, of which 4 were waited for; matrix products, arithmetic and copies ran while one was open for 0% of the time, Pallas kernels for 9%

profile of v3, /device:TPU:127, one launch (start us, length us, event | category | flops | bytes accessed | tf_op | source)
XLA Modules:
  0.0 52.4 jit_solution(13893490800531997578)
XLA Ops:
  0.6 0.7 %shard_map.140.own_ref = f32[4,128]{1,0:T(4,128)S(1)} custom-call(f32[3,128]{1,0:T(4,128)} %pos_hbm.1, s32[1,128]{1,0:T(1,128)} %bitcast.3), custom_call_target="tpu_custom_call" | custom-call | bytes 4096 | tf_op jit(solution)/shard_map/pallas_call | solution.py:553
  1.3 0.8 %collective-permute-start = (f32[4,128]{1,0:T(4,128)S(1)}, f32[4,128]{1,0:T(4,128)S(1)}, u32[]{:S(2)}, u32[]{:S(2)}) collective-permute-start(f32[4,128]{1,0:T(4,128)S(1)} %shard_map.140.own_ref), channel_id=1, source_target_pairs={{0,1},{1,0},{2,3},{3,2},{4,5},{5,4},{6,7},{7,6},{8,9},{9,8},{10,11... | collective-permute-start | bytes 6152 | tf_op jit(solution)/shard_map/ppermute | solution.py:595
  2.1 4.2 %collective-permute-start.1 = (f32[4,128]{1,0:T(4,128)S(1)}, f32[4,128]{1,0:T(4,128)S(1)}, u32[]{:S(2)}, u32[]{:S(2)}) collective-permute-start(f32[4,128]{1,0:T(4,128)S(1)} %shard_map.140.own_ref), channel_id=1, source_target_pairs={{1,2},{2,1},{3,4},{4,3},{5,6},{6,5},{7,8},{8,7},{9,10},{10,9},{11,... | collective-permute-start | bytes 6152 | tf_op jit(solution)/shard_map/ppermute | solution.py:598
  6.3 1.7 %shard_map.141 = (bf16[256,3072]{1,0:T(8,128)(2,1)S(1)}, bf16[2,64,32]{2,1,0:T(8,128)(2,1)S(1)}, bf16[2,64,192]{2,1,0:T(8,128)(2,1)S(1)}, bf16[2,128,192]{2,1,0:...) custom-call(s32[24,128]{1,0:T(8,128)} %nb_hbm.1, ...), custom_call_target="tpu_custom_call" | custom-call | flops 100000000 | bytes 2045440 | tf_op jit(solution)/shard_map/pallas_call | solution.py:553
  8.1 0.0 collective-permute-done.near_ref
  8.1 4.4 %collective-permute-done.1.far_ref = f32[4,128]{1,0:T(4,128)S(1)} collective-permute-done((f32[4,128]{1,0:T(4,128)S(1)}, f32[4,128]{1,0:T(4,128)S(1)}, u32[]{:S(2)}, u32[]{:S(2)}) %collective-permute-start.1) | collective-permute-done | bytes 2080 | tf_op jit(solution)/shard_map/ppermute | solution.py:598
  12.4 1.9 %shard_map.142 = (f32[256,128]{1,0:T(8,128)S(1)}, f32[128,128]{1,0:T(8,128)S(1)}, f32[128,128]{1,0:T(8,128)S(1)}, f32[6,8,3072]{2,1,0:T(8,128)S(1)}, f32[64,128]...) custom-call(f32[4,128]{1,0:T(4,128)S(1)} %shard_map.140.own_ref, ...), custom_call_target="tpu_custom_call" | custom-call | flops 1000000000 | bytes 3571712 | tf_op jit(solution)/shard_map/pallas_call | solution.py:553
  14.4 0.1 collective-permute-start.2
  14.4 4.2 %collective-permute-start.3 = (f32[128,128]{1,0:T(8,128)S(1)}, f32[128,128]{1,0:T(8,128)S(1)}, u32[]{:S(2)}, u32[]{:S(2)}) collective-permute-start(f32[128,128]{1,0:T(8,128)S(1)} %get-tuple-element.38), channel_id=1, source_target_pairs={{1,2},{2,1},{3,4},{4,3},{5,6},{6,5},{7,8},{8,7},{9,10},{10,9},{11,... | collective-permute-start | bytes 196616 | tf_op jit(solution)/shard_map/ppermute | solution.py:598
  18.7 1.5 %shard_map.143 = (f32[128,3072]{1,0:T(8,128)S(1)}, f32[128,3072]{1,0:T(8,128)S(1)}) custom-call(f32[6,8,3072]{2,1,0:T(8,128)S(1)} %get-tuple-element.39.geom_ref, bf16[2,64,32]{2,1,0:T(8,128)(2,1)S(1)} %get-tuple-element.31.win_ref, bf16[2,64,192]{2,1,0:T(8,128)(2,1)S(1)} %get-tuple-element.32.wmid_ref, bf16[2,128,192]{2,1,0:T(8,128)(2,1)S(1)} %get-tuple-element.33.wout_ref), custom_call_target="tpu_custom_call" | custom-call | flops 2000000000 | bytes 3891200 | tf_op jit(solution)/shard_map/pallas_call | solution.py:553
  20.2 0.0 collective-permute-done.2.near_ref
  20.2 5.2 %collective-permute-done.3.far_ref = f32[128,128]{1,0:T(8,128)S(1)} collective-permute-done((f32[128,128]{1,0:T(8,128)S(1)}, f32[128,128]{1,0:T(8,128)S(1)}, u32[]{:S(2)}, u32[]{:S(2)}) %collective-permute-start.3) | collective-permute-done | bytes 65568 | tf_op jit(solution)/shard_map/ppermute | solution.py:598
  25.5 3.7 %shard_map.144 = (f32[1,128]{1,0:T(1,128)}, f32[256,128]{1,0:T(8,128)S(1)}, f32[128,128]{1,0:T(8,128)S(1)}, f32[128,128]{1,0:T(8,128)S(1)}, f32[8,256]{1,0:T(8,128)S(1)}) custom-call(f32[256,128]{1,0:T(8,128)S(1)} %get-tuple-element.36.feats_ref, f32[128,128]{1,0:T(8,128)S(1)} %collective-permute-done.2.near_ref, ...), custom_call_target="tpu_custom_call" | custom-call | flops 1000000000 | bytes 5874688 | tf_op jit(solution)/shard_map/pallas_call | solution.py:553
  29.1 0.0 collective-permute-start.4
  29.1 4.2 %collective-permute-start.5 = (f32[128,128]{1,0:T(8,128)S(1)}, f32[128,128]{1,0:T(8,128)S(1)}, u32[]{:S(2)}, u32[]{:S(2)}) collective-permute-start(f32[128,128]{1,0:T(8,128)S(1)} %get-tuple-element.47), channel_id=1, source_target_pairs={{1,2},{2,1},{3,4},{4,3},{5,6},{6,5},{7,8},{8,7},{9,10},{10,9},{11,... | collective-permute-start | bytes 196616 | tf_op jit(solution)/shard_map/ppermute | solution.py:598
  33.4 1.5 %shard_map.145.edge_ref = f32[192,3072]{1,0:T(8,128)S(1)} custom-call(f32[6,8,3072]{2,1,0:T(8,128)S(1)} %get-tuple-element.39.geom_ref, f32[64,3072]{1,0:T(8,128)S(1)} %get-tuple-element.48.hfar_ref, bf16[2,64,32]{2,1,0:T(8,128)(2,1)S(1)} %get-tuple-element.31.win_ref, bf16[2,64,192]{2,1,0:T(8,128)(2,1)S(1)} %get-tuple-element.32.wmid_ref, ...), custom_call_target="tpu_custom_call" | custom-call | flops 2000000000 | bytes 3891200 | tf_op jit(solution)/shard_map/pallas_call | solution.py:553
  34.9 0.0 collective-permute-done.4.near_ref
  34.9 5.3 %collective-permute-done.5.far_ref = f32[128,128]{1,0:T(8,128)S(1)} collective-permute-done((f32[128,128]{1,0:T(8,128)S(1)}, f32[128,128]{1,0:T(8,128)S(1)}, u32[]{:S(2)}, u32[]{:S(2)}) %collective-permute-start.5) | collective-permute-done | bytes 65568 | tf_op jit(solution)/shard_map/ppermute | solution.py:598
  40.1 1.3 %shard_map.146 = (f32[8,128]{1,0:T(8,128)S(1)}, f32[8,128]{1,0:T(8,128)S(1)}) custom-call(f32[256,128]{1,0:T(8,128)S(1)} %get-tuple-element.45.gown_ref, f32[128,128]{1,0:T(8,128)S(1)} %collective-permute-done.4.near_ref, f32[128,128]{1,0:T(8,128)S(1)} %collective-permute-done.5.far_ref, bf16[256,3072]{1,0:T(8,128)(2,1)S(1)} %get-tuple-element.28.sel_ref, ...), custom_call_target="tpu_custom_call" | custom-call | flops 1000000000 | bytes 4997120 | tf_op jit(solution)/shard_map/pallas_call | solution.py:553
  41.5 4.2 %collective-permute-start.7 = (f32[8,128]{1,0:T(8,128)S(1)}, f32[8,128]{1,0:T(8,128)S(1)}, u32[]{:S(2)}, u32[]{:S(2)}) collective-permute-start(f32[8,128]{1,0:T(8,128)S(1)} %get-tuple-element.53), channel_id=1, source_target_pairs={{1,2},{2,1},{3,4},{4,3},{5,6},{6,5},{7,8},{8,7},{9,10},{10,9},{11,... | collective-permute-start | bytes 12296 | tf_op jit(solution)/shard_map/ppermute | solution.py:598
  45.7 0.1 collective-permute-start.6
  45.8 6.0 %collective-permute-done.7 = f32[8,128]{1,0:T(8,128)S(1)} collective-permute-done((f32[8,128]{1,0:T(8,128)S(1)}, f32[8,128]{1,0:T(8,128)S(1)}, u32[]{:S(2)}, u32[]{:S(2)}) %collective-permute-start.7) | collective-permute-done | bytes 4128 | tf_op jit(solution)/shard_map/ppermute | solution.py:598
  51.8 0.0 collective-permute-done.6
  51.8 0.6 %add_negate_fusion = f32[3,128]{1,0:T(4,128)} fusion(f32[8,128]{1,0:T(8,128)S(1)} %collective-permute-done.7, f32[8,128]{1,0:T(8,128)S(1)} %collective-permute-done.6, f32[8,128]{1,0:T(8,128)S(1)} %get-tuple-element.52, pred[128]{0:T(512)(128)(4,1)S(1)} %compare_compare_fusion), kind=kLoop, calls=%fused_computation | loop fusion | flops 1152 | bytes 6272 | tf_op jit(solution)/shard_map/neg | solution.py:686
  (1 shorter events, 0.0 us)
Async XLA Ops:
  1.3 6.7 %collective-permute-start = (f32[4,128]{1,0:T(4,128)S(1)}, f32[4,128]{1,0:T(4,128)S(1)}, u32[]{:S(2)}, u32[]{:S(2)}) collective-permute-start(f32[4,128]{1,0:T(4,128)S(1)} %shard_map.140.own_ref), channel_id=1, source_target_pairs={{0,1},{1,0},{2,3},{3,2},{4,5},{5,4},{6,7},{7,6},{8,9},{9,8},{10,11... | collective-permute-start | bytes 6152 | tf_op jit(solution)/shard_map/ppermute | solution.py:595
  2.1 10.3 %collective-permute-start.1 = (f32[4,128]{1,0:T(4,128)S(1)}, f32[4,128]{1,0:T(4,128)S(1)}, u32[]{:S(2)}, u32[]{:S(2)}) collective-permute-start(f32[4,128]{1,0:T(4,128)S(1)} %shard_map.140.own_ref), channel_id=1, source_target_pairs={{1,2},{2,1},{3,4},{4,3},{5,6},{6,5},{7,8},{8,7},{9,10},{10,9},{11,... | collective-permute-start | bytes 6152 | tf_op jit(solution)/shard_map/ppermute | solution.py:598
  14.4 5.9 %collective-permute-start.2 = (f32[128,128]{1,0:T(8,128)S(1)}, f32[128,128]{1,0:T(8,128)S(1)}, u32[]{:S(2)}, u32[]{:S(2)}) collective-permute-start(f32[128,128]{1,0:T(8,128)S(1)} %get-tuple-element.37), channel_id=1, source_target_pairs={{0,1},{1,0},{2,3},{3,2},{4,5},{5,4},{6,7},{7,6},{8,9},{9,8},{10,11... | collective-permute-start | bytes 196616 | tf_op jit(solution)/shard_map/ppermute | solution.py:595
  14.4 11.0 %collective-permute-start.3 = (f32[128,128]{1,0:T(8,128)S(1)}, f32[128,128]{1,0:T(8,128)S(1)}, u32[]{:S(2)}, u32[]{:S(2)}) collective-permute-start(f32[128,128]{1,0:T(8,128)S(1)} %get-tuple-element.38), channel_id=1, source_target_pairs={{1,2},{2,1},{3,4},{4,3},{5,6},{6,5},{7,8},{8,7},{9,10},{10,9},{11,... | collective-permute-start | bytes 196616 | tf_op jit(solution)/shard_map/ppermute | solution.py:598
  29.1 5.7 %collective-permute-start.4 = (f32[128,128]{1,0:T(8,128)S(1)}, f32[128,128]{1,0:T(8,128)S(1)}, u32[]{:S(2)}, u32[]{:S(2)}) collective-permute-start(f32[128,128]{1,0:T(8,128)S(1)} %get-tuple-element.46), channel_id=1, source_target_pairs={{0,1},{1,0},{2,3},{3,2},{4,5},{5,4},{6,7},{7,6},{8,9},{9,8},{10,11... | collective-permute-start | bytes 196616 | tf_op jit(solution)/shard_map/ppermute | solution.py:595
  29.1 11.0 %collective-permute-start.5 = (f32[128,128]{1,0:T(8,128)S(1)}, f32[128,128]{1,0:T(8,128)S(1)}, u32[]{:S(2)}, u32[]{:S(2)}) collective-permute-start(f32[128,128]{1,0:T(8,128)S(1)} %get-tuple-element.47), channel_id=1, source_target_pairs={{1,2},{2,1},{3,4},{4,3},{5,6},{6,5},{7,8},{8,7},{9,10},{10,9},{11,... | collective-permute-start | bytes 196616 | tf_op jit(solution)/shard_map/ppermute | solution.py:598
  41.5 10.3 %collective-permute-start.7 = (f32[8,128]{1,0:T(8,128)S(1)}, f32[8,128]{1,0:T(8,128)S(1)}, u32[]{:S(2)}, u32[]{:S(2)}) collective-permute-start(f32[8,128]{1,0:T(8,128)S(1)} %get-tuple-element.53), channel_id=1, source_target_pairs={{1,2},{2,1},{3,4},{4,3},{5,6},{6,5},{7,8},{8,7},{9,10},{10,9},{11,... | collective-permute-start | bytes 12296 | tf_op jit(solution)/shard_map/ppermute | solution.py:598
  45.7 6.1 %collective-permute-start.6 = (f32[8,128]{1,0:T(8,128)S(1)}, f32[8,128]{1,0:T(8,128)S(1)}, u32[]{:S(2)}, u32[]{:S(2)}) collective-permute-start(f32[8,128]{1,0:T(8,128)S(1)} %get-tuple-element.53), channel_id=1, source_target_pairs={{0,1},{1,0},{2,3},{3,2},{4,5},{5,4},{6,7},{7,6},{8,9},{9,8},{10,11... | collective-permute-start | bytes 12296 | tf_op jit(solution)/shard_map/ppermute | solution.py:595

commit v4 on v1

v4 whole, which is shorter than its diff:
```python
import jax
import jax.numpy as jnp
from jax import lax
from jax.experimental import pallas as pl
from jax.experimental.pallas import tpu as pltpu
from jax.sharding import PartitionSpec as P

RADIUS = 5.0
SOFTEN = 0.25
F32 = jnp.float32
BF16 = jnp.bfloat16
HALF = 64
MIB = 1024 * 1024


def hdot(a, b, dims=(((1,), (0,)), ((), ()))):
    return lax.dot_general(
        a, b, dims, precision=lax.Precision.HIGHEST, preferred_element_type=F32
    )


def hdot_t(a, b):
    return hdot(a, b, (((0,), (0,)), ((), ())))


def bdot(a, b):
    return jnp.dot(a, b, preferred_element_type=F32)


def bdot_nt(a, b):
    return lax.dot_general(a, b, (((1,), (1,)), ((), ())), preferred_element_type=F32)


def high(x):
    return x.astype(BF16).astype(F32)


def split_rows(x):
    hi = x.astype(BF16)
    lo = (x - hi.astype(F32)).astype(BF16)
    return hi, lo


def stack3(x):
    hi, lo = split_rows(x)
    return jnp.concatenate([hi, lo, hi], axis=0)


def sigmoid(v):
    return 0.5 + 0.5 * jnp.tanh(0.5 * v)


def roll64(x):
    return pltpu.roll(x, HALF, 1)


def lane_low(rows):
    return lax.broadcasted_iota(jnp.int32, (rows, 128), 1) < HALF


def parity_odd(rows):
    odd = lax.rem(lax.axis_index("space"), 2)
    return jnp.full((rows, 128), odd, jnp.int32) > 0


def far_lanes(rows):
    return parity_odd(rows) == lane_low(rows)


def copy_in(moves, sems):
    copies = [
        pltpu.make_async_copy(src, dst, sems.at[i]) for i, (src, dst) in enumerate(moves)
    ]
    for c in copies:
        c.start()
    for c in copies:
        c.wait()


def pack_kernel(pos_hbm, kind_hbm, own_ref, pos_ref, kind_ref, sems):
    copy_in([(pos_hbm, pos_ref), (kind_hbm, kind_ref)], sems)
    own_ref[0:3, :] = pos_ref[...]
    own_ref[3:4, :] = (kind_ref[...] + 1).astype(F32)


def remap_kernel(nb_hbm, gi_hbm, counts_hbm, out_ref, nb_ref, gi_ref, counts_ref, hot_ref, sems):
    copy_in([(nb_hbm, nb_ref), (gi_hbm, gi_ref), (counts_hbm, counts_ref)], sems)
    slots, atoms = nb_ref.shape
    rows = lax.broadcasted_iota(jnp.int32, (atoms, atoms), 0) + atoms
    for k in range(slots):
        nb = jnp.broadcast_to(nb_ref[k : k + 1, :], (atoms, atoms))
        hot_ref[:, pl.ds(k * atoms, atoms)] = (rows == nb).astype(F32).astype(BF16)
    place = jnp.concatenate(
        [jnp.broadcast_to(gi_ref[i : i + 1, :], (16, HALF)).astype(F32) for i in range(2)], axis=1
    )
    ghost = bdot(place.astype(BF16), hot_ref[...])
    for k in range(slots):
        nb = nb_ref[k : k + 1, :]
        there = ghost[0:1, k * atoms : (k + 1) * atoms] + F32(atoms)
        out_ref[k : k + 1, :] = jnp.where(nb < atoms, nb.astype(F32), there)
    out_ref[slots : slots + 1, :] = counts_ref[...].astype(F32)
    out_ref[slots + 1 :, :] = jnp.zeros((out_ref.shape[0] - slots - 1, atoms), F32)


def build_selector(rows_f32, base, slots, sel_ref):
    atoms = rows_f32.shape[1]
    rows = lax.broadcasted_iota(jnp.int32, (2 * atoms, atoms), 0).astype(F32)
    for k in range(slots):
        nb = jnp.broadcast_to(rows_f32[base + k : base + k + 1, :], (2 * atoms, atoms))
        sel_ref[:, pl.ds(k * atoms, atoms)] = (rows == nb).astype(F32).astype(BF16)


def prep_kernel(
    rin_hbm,
    rmid_hbm,
    rout_hbm,
    embed_hbm,
    mix_one_hbm,
    vec_hbm,
    mix_two_hbm,
    read_hbm,
    edges_ref,
    sel_ref,
    win_ref,
    wmid_ref,
    wout_ref,
    embed_ref,
    mix_one_ref,
    vec_ref,
    mix_two_ref,
    read_ref,
    rin_ref,
    rmid_ref,
    rout_ref,
    sems,
):
    copy_in(
        [
            (rin_hbm, rin_ref),
            (rmid_hbm, rmid_ref),
            (rout_hbm, rout_ref),
            (embed_hbm, embed_ref),
            (mix_one_hbm, mix_one_ref),
            (vec_hbm, vec_ref),
            (mix_two_hbm, mix_two_ref),
            (read_hbm, read_ref),
        ],
        sems,
    )
    build_selector(edges_ref[...], 0, sel_ref.shape[1] // edges_ref.shape[1], sel_ref)
    for layer in range(2):
        w = rin_ref[layer]
        h = high(w)
        lo = w - h
        win_ref[layer] = jnp.concatenate([h, h, lo, lo], axis=0).T.astype(BF16)
        w = rmid_ref[layer]
        h = high(w)
        wmid_ref[layer] = jnp.concatenate([h, h, w - h], axis=0).T.astype(BF16)
        w = rout_ref[layer]
        h = high(w)
        wout_ref[layer] = jnp.concatenate([h, h, w - h], axis=0).T.astype(BF16)


def basis_rows(b):
    h = high(b)
    lo = b - h
    return jnp.concatenate([h, lo, h, lo], axis=0).astype(BF16)


def radial(win, wmid, wout, b):
    v1 = bdot(win, basis_rows(b))
    z1 = v1 * sigmoid(v1)
    v2 = bdot(wmid, stack3(z1))
    z2 = v2 * sigmoid(v2)
    return bdot(wout, stack3(z2))


def silu_pair(v, t):
    s = sigmoid(v)
    z = v * s
    return z, (s + z * (1.0 - s)) * t


def radial_pair(win, wmid, wout, b, db):
    z1, t1 = silu_pair(bdot(win, basis_rows(b)), bdot(win, basis_rows(db)))
    z2, t2 = silu_pair(bdot(wmid, stack3(z1)), bdot(wmid, stack3(t1)))
    return bdot(wout, stack3(z2)), bdot(wout, stack3(t2))


def tile8(x, times):
    return jnp.concatenate([x] * times, axis=0)


def spread_rows(row, rows):
    return jnp.broadcast_to(row, (rows, row.shape[1]))


def geometry(far, own, valid):
    vec = [f - o for f, o in zip(far, own)]
    r2 = vec[0] * vec[0] + vec[1] * vec[1] + vec[2] * vec[2] + SOFTEN
    inv = lax.rsqrt(r2)
    inv = inv * (1.5 - 0.5 * r2 * inv * inv)
    rho = r2 * inv
    unit = [v * inv for v in vec]
    x = jnp.minimum(rho * (1.0 / RADIUS), 1.0)
    y = 1.0 - x
    x2 = x * x
    env = y * y * y * (1.0 + x * (3.0 + x * (6.0 + x * (10.0 + x * 15.0))))
    denv = (-105.0 / RADIUS) * x2 * x2 * y * y
    f = RADIUS * inv * env * valid
    df = RADIUS * inv * (denv - env * inv) * valid
    n = (lax.broadcasted_iota(jnp.int32, rho.shape, 0) + 1).astype(F32)
    turns = n * x
    whole = jnp.floor(turns + 0.5)
    frac = (turns - whole) * jnp.pi
    parity = whole - 2.0 * jnp.floor(0.5 * whole)
    sign = 1.0 - 2.0 * parity
    q = frac * frac
    sin = frac * (
        1.0
        + q * (-1 / 6 + q * (1 / 120 + q * (-1 / 5040 + q * (1 / 362880 + q * (-1 / 39916800)))))
    )
    cos = 1.0 + q * (
        -1 / 2
        + q * (1 / 24 + q * (-1 / 720 + q * (1 / 40320 + q * (-1 / 3628800 + q * (1 / 479001600)))))
    )
    sin = sin * sign
    cos = cos * sign
    return unit, inv, sin * f, sin * df + (n * (jnp.pi / RADIUS)) * cos * f


def forward_one(
    domain,
    table,
    counts,
    sel,
    embed,
    win,
    wmid,
    wout,
    mix_ref,
    vec,
    tab_ref,
    htab_ref,
    geom_ref,
    basis_ref,
    pre_ref,
    b_ref,
):
    atoms = table.shape[1] // 2
    slots = sel.shape[1] // atoms
    species, width = embed.shape
    for c in range(3):
        p = jnp.broadcast_to(table[c : c + 1], (8, 2 * atoms))
        h = p.astype(BF16)
        rest = p - h.astype(F32)
        m = rest.astype(BF16)
        lo = (rest - m.astype(F32)).astype(BF16)
        part = jnp.concatenate([h.astype(F32), m.astype(F32), lo.astype(F32)], axis=0)
        tab_ref[domain, c * 24 : c * 24 + 24, :] = part
    kind = jnp.broadcast_to(table[3:4], (species, 2 * atoms))
    onehot = (
        kind == (lax.broadcasted_iota(jnp.int32, (species, 2 * atoms), 0) + 1).astype(F32)
    ).astype(F32)
    h0 = hdot_t(embed, onehot)
    h0_hi = high(h0)
    tab_ref[domain, 72 : 72 + width, :] = h0_hi
    tab_ref[domain, 72 + width : 72 + 2 * width, :] = h0 - h0_hi
    tab = tab_ref[domain].astype(BF16)
    htab_ref[domain] = tab_ref[domain, 72 : 72 + 2 * width, :].astype(BF16)
    own_rep = [
        jnp.concatenate([jnp.broadcast_to(table[c : c + 1, :atoms], (8, atoms))] * slots, axis=1)
        for c in range(3)
    ]
    counts = jnp.broadcast_to(counts, (8, atoms))
    g = bdot(tab, sel)
    far = [
        g[24 * c : 24 * c + 8] + g[24 * c + 8 : 24 * c + 16] + g[24 * c + 16 : 24 * c + 24]
        for c in range(3)
    ]
    h_far = g[72 : 72 + width] + g[72 + width : 72 + 2 * width]
    valid = jnp.concatenate([(counts > F32(k)).astype(F32) for k in range(slots)], axis=1)
    unit, inv, b, db = geometry(far, own_rep, valid)
    for i, x in enumerate(unit + [inv]):
        geom_ref[domain, i : i + 1] = x[0:1]
    basis_ref[domain, 0] = b
    basis_ref[domain, 1] = db
    w = radial(win, wmid, wout, b)
    wa = w[:width] * h_far
    wb = w[width:] * h_far
    a_sum = jnp.zeros((width, atoms), F32)
    b_sum = [jnp.zeros((width, atoms), F32) for _ in range(3)]
    for k in range(slots):
        s = slice(k * atoms, (k + 1) * atoms)
        a_sum = a_sum + wa[:, s]
        for c in range(3):
            b_sum[c] = b_sum[c] + wb[:, s] * tile8(unit[c][:, s], width // 8)
    scale = 1.0 / jnp.sqrt(F32(slots))
    a_sum = a_sum * scale
    b_all = jnp.concatenate([x * scale for x in b_sum], axis=1)
    sq = b_all * b_all
    q = sq[:, :atoms] + sq[:, atoms : 2 * atoms] + sq[:, 2 * atoms :]
    pre = hdot_t(mix_ref[0], a_sum) + hdot_t(mix_ref[1], h0[:, :atoms]) + hdot_t(mix_ref[2], q)
    pre_ref[domain] = pre
    b_ref[domain] = b_all
    s1 = pre * sigmoid(pre)
    v1 = hdot_t(vec, b_all)
    lo_part = jnp.concatenate([s1, v1[:, :atoms]], axis=0)
    hi_part = jnp.concatenate([v1[:, atoms : 2 * atoms], v1[:, 2 * atoms :]], axis=0)
    return lo_part, hi_part


def layer_one_kernel(
    own_ref,
    near_ref,
    edges_ref,
    far_ref,
    sel_ref,
    embed_ref,
    win_ref,
    wmid_ref,
    wout_ref,
    mix_ref,
    vec_ref,
    feats_ref,
    near_out,
    htab_ref,
    geom_ref,
    basis_ref,
    pre_ref,
    b_ref,
    sel_far_ref,
    tab_ref,
):
    atoms = own_ref.shape[1]
    slots = sel_ref.shape[1] // atoms
    width = embed_ref.shape[1]
    ours = far_lanes(4)
    own = own_ref[...]
    there = far_ref[...]
    build_selector(there, 8, slots, sel_far_ref)
    tables = [
        jnp.concatenate([own, jnp.where(ours, there[0:4], near_ref[...])], axis=1),
        jnp.concatenate([there[0:4], jnp.where(ours, there[4:8], own)], axis=1),
    ]
    counts = [edges_ref[slots : slots + 1, :], there[8 + slots : 9 + slots]]
    for domain in range(2):
        lo_part, hi_part = forward_one(
            domain,
            tables[domain],
            counts[domain],
            (sel_ref, sel_far_ref)[domain][...],
            embed_ref[...],
            win_ref[0],
            wmid_ref[0],
            wout_ref[0],
            mix_ref,
            vec_ref[...],
            tab_ref,
            htab_ref,
            geom_ref,
            basis_ref,
            pre_ref,
            b_ref,
        )
        feats_ref[domain, 0 : 2 * width] = lo_part
        feats_ref[domain, 2 * width :] = hi_part
        if domain == 0:
            low_lanes, high_lanes = packed(lo_part, hi_part)
            near_out[...] = jnp.where(parity_odd(2 * width), low_lanes, high_lanes)


def packed(lo_part, hi_part):
    low = lane_low(lo_part.shape[0])
    return (
        jnp.where(low, lo_part, roll64(hi_part)),
        jnp.where(low, roll64(lo_part), hi_part),
    )


def unpacked(tile, high_half):
    other = roll64(tile)
    return jnp.where(high_half, other, tile), jnp.where(high_half, tile, other)


def radial_two_kernel(basis_ref, win_ref, wmid_ref, wout_ref, w_ref, dw_ref):
    w, dw = radial_pair(win_ref[1], wmid_ref[1], wout_ref[1], basis_ref[0, 0], basis_ref[0, 1])
    w_ref[...] = w
    dw_ref[...] = dw


def edge_gradient(unit, inv, drho, du):
    dot = unit[0] * du[0] + unit[1] * du[1] + unit[2] * du[2]
    radial_part = drho - dot * inv
    return [unit[c] * radial_part + du[c] * inv for c in range(3)]


def sum_rows(x):
    return jnp.sum(x, axis=0, keepdims=True)


def position_rows(grads):
    g = jnp.concatenate([jnp.broadcast_to(x, (8, x.shape[1])) for x in grads], axis=0)
    x = jnp.concatenate([g[0:1], g[8:9], g[16:17], jnp.zeros((5, g.shape[1]), F32)], axis=0)
    h = high(x)
    return jnp.concatenate([h, x - h], axis=0).astype(BF16)


def layer_two_kernel(
    feats_ref,
    near_ref,
    sel_ref,
    geom_ref,
    w_ref,
    dw_ref,
    mix_ref,
    read_ref,
    energy_ref,
    gown_ref,
    gghost_ref,
    near_out,
    far_out,
    gpos_ref,
    gpos_ghost_ref,
    far_scr,
    along_scr,
):
    atoms = feats_ref.shape[2]
    width = mix_ref.shape[1]
    slots = sel_ref.shape[1] // atoms
    rows = 2 * width
    odd = parity_odd(rows)
    ours = far_lanes(rows)
    near_lo, near_hi = unpacked(near_ref[...], odd)
    g_lo = jnp.where(ours, feats_ref[1, 0:rows], near_lo)
    g_hi = jnp.where(ours, feats_ref[1, rows:], near_hi)
    feats = feats_ref[0]
    table = jnp.concatenate([feats, jnp.concatenate([g_lo, g_hi], axis=0)], axis=1)
    t_hi, t_lo = split_rows(table)
    g = bdot(jnp.concatenate([t_hi, t_lo], axis=0), sel_ref[...])
    f = g[: 4 * width] + g[4 * width :]
    far_scr[...] = f
    unit = [geom_ref[0, c : c + 1] for c in range(3)]
    along = f[width : 2 * width] * spread_rows(unit[0], width)
    along = along + f[2 * width : 3 * width] * spread_rows(unit[1], width)
    along = along + f[3 * width :] * spread_rows(unit[2], width)
    along_scr[...] = along
    msg = w_ref[0:width] * f[:width] + w_ref[width:] * along
    m = jnp.zeros((width, atoms), F32)
    for k in range(slots):
        m = m + msg[:, k * atoms : (k + 1) * atoms]
    scale = 1.0 / jnp.sqrt(F32(slots))
    s1 = feats[:width]
    pre = hdot_t(mix_ref[0], m * scale) + hdot_t(mix_ref[1], s1)
    sg = sigmoid(pre)
    s2 = pre * sg
    energy_ref[...] = hdot(read_ref[0:1], s1) + hdot(read_ref[1:2], s2)
    read = read_ref[...].T
    r_one = jnp.broadcast_to(read[:, 0:1], (width, atoms))
    r_two = jnp.broadcast_to(read[:, 1:2], (width, atoms))
    gpre = r_two * (sg + s2 * (1.0 - sg))
    gm = hdot(mix_ref[0], gpre) * scale
    gs_own = r_one + hdot(mix_ref[1], gpre)
    gm_rep = jnp.concatenate([gm] * slots, axis=1)
    ga = w_ref[0:width] * gm_rep
    gb = w_ref[width:] * gm_rep
    gv = [gb * spread_rows(unit[c], width) for c in range(3)]
    drho = gm_rep * (dw_ref[0:width] * far_scr[0:width] + dw_ref[width:] * along_scr[...])
    du = [sum_rows(gb * far_scr[(c + 1) * width : (c + 2) * width]) for c in range(3)]
    gp = edge_gradient(unit, geom_ref[0, 3:4], sum_rows(drho), du)
    hi, lo = split_rows(jnp.concatenate([ga] + gv, axis=0))
    acc = bdot_nt(jnp.concatenate([hi, lo, position_rows(gp)], axis=0), sel_ref[...])
    grads = acc[: 4 * width] + acc[4 * width : 8 * width]
    own = grads[:, :atoms]
    gown_ref[0:width] = own[0:width] + gs_own
    gown_ref[width:] = own[width:]
    ghost = grads[:, atoms:]
    gghost_ref[...] = ghost
    to_upper, to_lower = packed(ghost[:rows], ghost[rows:])
    near_out[...] = jnp.where(odd, to_lower, to_upper)
    far_out[...] = jnp.where(odd, to_upper, to_lower)
    pos = acc[8 * width : 8 * width + 8] + acc[8 * width + 8 :]
    gpos_ref[...] = pos[:, :atoms] - centre_rows(gp, slots, atoms)
    gpos_ghost_ref[...] = pos[:, atoms:]


def centre_rows(gp, slots, atoms):
    total = [jnp.zeros((1, atoms), F32) for _ in range(3)]
    for k in range(slots):
        for c in range(3):
            total[c] = total[c] + gp[c][:, k * atoms : (k + 1) * atoms]
    return jnp.concatenate(total + [jnp.zeros((5, atoms), F32)], axis=0)


def join_kernel(gown_ref, near_ref, far_ref, gpos_ghost_ref, out_ref):
    rows = near_ref.shape[0]
    odd = parity_odd(rows)
    ours = far_lanes(rows)
    zero = jnp.zeros(near_ref.shape, F32)
    lo, hi = unpacked(near_ref[...], jnp.logical_not(odd))
    out_ref[0:rows] = gown_ref[0:rows] + jnp.where(ours, lo, zero)
    out_ref[rows : 2 * rows] = gown_ref[rows:] + jnp.where(ours, hi, zero)
    out_ref[2 * rows : 3 * rows] = far_ref[...]
    out_ref[3 * rows :] = gpos_ghost_ref[...]


def tangent_one_kernel(
    basis_ref, htab_ref, sel_ref, there_ref, win_ref, wmid_ref, wout_ref, out_ref, sel_ghost_ref, sel_scr
):
    atoms = there_ref.shape[1]
    width = htab_ref.shape[1] // 2
    slots = sel_ref.shape[1] // atoms
    build_selector(there_ref[...], 8, slots, sel_scr)
    sel_ghost_ref[...] = sel_scr[atoms:]
    for domain in range(2):
        w, dw = radial_pair(
            win_ref[0], wmid_ref[0], wout_ref[0], basis_ref[domain, 0], basis_ref[domain, 1]
        )
        g = bdot(htab_ref[domain], (sel_ref, sel_scr)[domain][...])
        h = g[:width] + g[width:]
        out_ref[domain, 0:width] = dw[:width] * h
        out_ref[domain, width : 2 * width] = dw[width:] * h
        out_ref[domain, 2 * width :] = w[width:] * h


def backward_one(g_lo, g_hi, pre, b_all, mix_ref, vec, geom_ref, domain, edge_ref, slots):
    width, atoms = pre.shape
    scale = 1.0 / jnp.sqrt(F32(slots))
    sg = sigmoid(pre)
    gpre = g_lo[:width] * (sg + pre * sg * (1.0 - sg))
    ga = hdot(mix_ref[0], gpre) * scale
    gq = hdot(mix_ref[2], gpre)
    gv = jnp.concatenate([g_lo[width:], g_hi[:width], g_hi[width:]], axis=1)
    gb_all = hdot(vec, gv) + 2.0 * b_all * jnp.concatenate([gq] * 3, axis=1)
    gb = [gb_all[:, c * atoms : (c + 1) * atoms] * scale for c in range(3)]
    ga_rep = jnp.concatenate([ga] * slots, axis=1)
    gb_rep = [jnp.concatenate([g] * slots, axis=1) for g in gb]
    unit = [geom_ref[domain, c : c + 1] for c in range(3)]
    gbu = gb_rep[0] * spread_rows(unit[0], width)
    gbu = gbu + gb_rep[1] * spread_rows(unit[1], width)
    gbu = gbu + gb_rep[2] * spread_rows(unit[2], width)
    drho = edge_ref[domain, 0:width] * ga_rep + edge_ref[domain, width : 2 * width] * gbu
    carried = edge_ref[domain, 2 * width :]
    du = [sum_rows(carried * gb_rep[c]) for c in range(3)]
    return edge_gradient(unit, geom_ref[domain, 3:4], sum_rows(drho), du)


def back_one_kernel(
    sent_ref,
    far_ref,
    gghost_ref,
    sel_ref,
    sel_ghost_ref,
    geom_ref,
    edge_ref,
    pre_ref,
    b_ref,
    mix_ref,
    vec_ref,
    gpos_ref,
    gown_out,
    ghost_out,
):
    atoms = gpos_ref.shape[1]
    width = mix_ref.shape[1]
    slots = sel_ref.shape[1] // atoms
    rows = 2 * width
    odd = parity_odd(rows)
    ours = far_lanes(rows)
    zero = jnp.zeros((rows, atoms), F32)
    lo, hi = unpacked(far_ref[2 * rows : 3 * rows], odd)
    g_lo = sent_ref[0:rows] + jnp.where(ours, zero, lo)
    g_hi = sent_ref[rows : 2 * rows] + jnp.where(ours, zero, hi)
    vec = vec_ref[...]
    gp = backward_one(
        g_lo, g_hi, pre_ref[0], b_ref[0], mix_ref, vec, geom_ref, 0, edge_ref, slots
    )
    acc = bdot_nt(position_rows(gp), sel_ref[...])
    pos = acc[0:8] + acc[8:16]
    ghost_out[...] = pos[:, atoms:] + sent_ref[3 * rows :]
    f_lo = far_ref[0:rows] + jnp.where(ours, gghost_ref[0:rows], zero)
    f_hi = far_ref[rows : 2 * rows] + jnp.where(ours, gghost_ref[rows:], zero)
    gf = backward_one(
        f_lo, f_hi, pre_ref[1], b_ref[1], mix_ref, vec, geom_ref, 1, edge_ref, slots
    )
    acc = bdot_nt(position_rows(gf), sel_ghost_ref[...])
    there = acc[0:8] + acc[8:16] + far_ref[3 * rows :]
    there = jnp.where(far_lanes(8), jnp.zeros((8, atoms), F32), there)
    gown_out[...] = gpos_ref[...] + pos[:, :atoms] - centre_rows(gp, slots, atoms) + there


def call(kernel, out_shapes, args, scratch=(), flops=0, transcendentals=0, far_away=0):
    args = [
        pltpu.with_memory_space_constraint(x, pltpu.HBM) if i < far_away else x
        for i, x in enumerate(args)
    ]
    spaces = [pltpu.HBM] * far_away + [pltpu.VMEM] * (len(args) - far_away)
    moved = sum(x.size * x.dtype.itemsize for x in list(args) + list(out_shapes))
    return pl.pallas_call(
        kernel,
        out_shape=out_shapes,
        in_specs=[pl.BlockSpec(memory_space=space) for space in spaces],
        out_specs=[pl.BlockSpec(memory_space=pltpu.VMEM)] * len(out_shapes),
        scratch_shapes=list(scratch),
        cost_estimate=pl.CostEstimate(
            flops=flops, bytes_accessed=moved, transcendentals=transcendentals
        ),
        compiler_params=pltpu.CompilerParams(vmem_limit_bytes=36 * MIB),
    )(*args)


def shape(dims, dtype=F32):
    return jax.ShapeDtypeStruct(dims, dtype)


def body(
    positions,
    species,
    neighbours,
    counts,
    ghost_index,
    embed,
    radial_in,
    radial_mid,
    radial_out,
    mix_one,
    vec_mix,
    mix_two,
    readout,
):
    atoms = positions.shape[1]
    slots = neighbours.shape[0]
    edges = slots * atoms
    nbasis, hidden = radial_in.shape[1:]
    width = embed.shape[1]
    rows = 2 * width
    devices = lax.axis_size("space")
    near_route = [(i, i ^ 1) for i in range(devices)]
    far_route = [(i, ((i + 1) ^ 1) - 1) for i in range(1, devices - 1)]

    def swap_near(x):
        return lax.ppermute(x, "space", near_route)

    def swap_far(x):
        return lax.ppermute(x, "space", far_route)

    def scratch_of(args):
        return [pltpu.VMEM(x.shape, x.dtype) for x in args]

    (own,) = call(
        pack_kernel,
        [shape((4, atoms))],
        [positions, species[None]],
        scratch=scratch_of([positions, species[None]]) + [pltpu.SemaphoreType.DMA((2,))],
        far_away=2,
    )
    near = swap_near(own)
    lists = [neighbours, ghost_index, counts[None]]
    (edge_rows,) = call(
        remap_kernel,
        [shape((slots + 8, atoms))],
        lists,
        scratch=scratch_of(lists)
        + [pltpu.VMEM((atoms, edges), BF16), pltpu.SemaphoreType.DMA((3,))],
        flops=10**8,
        far_away=3,
    )
    there = swap_far(jnp.concatenate([own, near, edge_rows], axis=0))
    weights = [radial_in, radial_mid, radial_out]
    passed = [embed, mix_one, vec_mix, mix_two, readout]
    moved = weights + passed
    sel, win, wmid, wout, embed, mix_one, vec_mix, mix_two, readout = call(
        prep_kernel,
        [
            shape((2 * atoms, edges), BF16),
            shape((2, hidden, 4 * nbasis), BF16),
            shape((2, hidden, 3 * hidden), BF16),
            shape((2, 2 * width, 3 * hidden), BF16),
        ]
        + [shape(x.shape, x.dtype) for x in passed],
        moved + [edge_rows],
        scratch=scratch_of(weights) + [pltpu.SemaphoreType.DMA((len(moved),))],
        flops=10**8,
        far_away=len(moved),
    )
    feats, near_f, htab, geom, basis, pre, b_all = call(
        layer_one_kernel,
        [
            shape((2, 4 * width, atoms)),
            shape((rows, atoms)),
            shape((2, 2 * width, 2 * atoms), BF16),
            shape((2, 8, edges)),
            shape((2, 2, 8, edges)),
            shape((2, width, atoms)),
            shape((2, width, 3 * atoms)),
        ],
        [own, near, edge_rows, there, sel, embed, win, wmid, wout, mix_one, vec_mix],
        scratch=[
            pltpu.VMEM((2 * atoms, edges), BF16),
            pltpu.VMEM((2, 72 + 2 * width, 2 * atoms), F32),
        ],
        flops=2 * 10**9,
    )
    near_f = swap_near(near_f)
    w, dw = call(
        radial_two_kernel,
        [shape((2 * width, edges)), shape((2 * width, edges))],
        [basis, win, wmid, wout],
        flops=2 * 10**9,
    )
    energy, g_own, g_ghost, near_g, far_g, gpos, gpos_ghost = call(
        layer_two_kernel,
        [
            shape((1, atoms)),
            shape((4 * width, atoms)),
            shape((4 * width, atoms)),
            shape((rows, atoms)),
            shape((rows, atoms)),
            shape((8, atoms)),
            shape((8, atoms)),
        ],
        [feats, near_f, sel, geom, w, dw, mix_two, readout],
        scratch=[pltpu.VMEM((4 * width, edges), F32), pltpu.VMEM((width, edges), F32)],
        flops=10**9,
    )
    near_g = swap_near(near_g)

    (sent,) = call(
        join_kernel, [shape((3 * rows + 8, atoms))], [g_own, near_g, far_g, gpos_ghost]
    )
    come = swap_far(sent)
    edge, sel_ghost = call(
        tangent_one_kernel,
        [shape((2, 3 * width, edges)), shape((atoms, edges), BF16)],
        [basis, htab, sel, there, win, wmid, wout],
        scratch=[pltpu.VMEM((2 * atoms, edges), BF16)],
        flops=4 * 10**9,
    )
    centre, ghost = call(
        back_one_kernel,
        [shape((8, atoms)), shape((8, atoms))],
        [
            sent,
            come,
            g_ghost,
            sel,
            sel_ghost,
            geom,
            edge,
            pre,
            b_all,
            mix_one,
            vec_mix,
            gpos,
        ],
        flops=10**9,
    )
    near_p = swap_near(ghost)
    odd = lax.rem(lax.axis_index("space"), 2) == 1
    low = lax.broadcasted_iota(jnp.int32, (3, atoms), 1) < HALF
    back = jnp.where(low == odd, near_p[:3], 0.0)
    return (energy[0], -(centre[:3] + back))


def solution(mesh):
    placed = (
        P(None, "space"),
        P("space"),
        P(None, "space"),
        P("space"),
        P(None, "space"),
        P(),
        P(),
        P(),
        P(),
        P(),
        P(),
        P(),
        P(),
    )
    return jax.shard_map(
        body, mesh=mesh, in_specs=placed, out_specs=(P("space"), P(None, "space")), check_vma=False
    )
```

time: 58.9 us -> 42 us (0.71)
  starting transfers between devices: 20.5 us -> 9.97 us
  local copies, waits for them, and re-layouts: 6.86 us -> 0 us
  Pallas kernels: 15.4 us -> 19.5 us
  waiting for transfers between devices: 12.7 us -> 10.9 us
  other arithmetic: 1.94 us -> 0.63 us
    ppermute x4 -> x2, starting transfers between devices: 19.6 us -> 8.68 us  [swap_far(): return lax.ppermute(x, 'space', far_route)]
    unnamed x24 -> x0, local copies, waits for them, and re-layouts: 6.1 us -> none
    pallas_call x6 -> x9, Pallas kernels: 15.4 us -> 19.5 us  [call(): pl.pallas_call(kernel, out_shape=out_shapes, in_specs=[pl.BlockSpec(memor...]
    ppermute x4 -> x2, waiting for transfers between devices: 12.6 us -> 8.79 us  [swap_far(): return lax.ppermute(x, 'space', far_route)]
    ppermute x4, waiting for transfers between devices: 0.01 us -> 2.06 us  [swap_near(): return lax.ppermute(x, 'space', near_route)]
    reshape x1 -> x0, local copies, waits for them, and re-layouts: 0.76 us -> none  [body(): ghost_index.reshape(1, atoms)]
    concatenate x1, other arithmetic: 0.69 us -> 0.01 us  [body(): there = swap_far(jnp.concatenate([own, near, edge_rows], axis=0))]
    broadcast_in_dim x1 -> x0, other arithmetic: 0.66 us -> none  [body(): own = jnp.concatenate([positions, (species + 1).astype(F32)[None]], axis=0)]
  transfers between devices with their start and end apart: 8 -> 6, of which waited for: 4 -> 4; matrix products, arithmetic and copies ran while one was open for 1% -> 0% of each run, Pallas kernels for 11% -> 20%
where the time goes in v4:
time: 42 us; the launch traced here: 41.7 us
  Pallas kernels  19.5 us (46%)
  waiting for transfers between devices  10.9 us (26%)
  starting transfers between devices  9.97 us (24%)
  between operations  0.73 us (2%)
  other arithmetic  0.63 us (2%)
    pallas_call x9, Pallas kernels, call(): pl.pallas_call(kernel, out_shape=out_shapes, in_specs=[pl.BlockSpec(memor...  19.5 us
    ppermute x2, waiting for transfers between devices, swap_far(): return lax.ppermute(x, 'space', far_route)  8.79 us
    ppermute x2, starting transfers between devices, swap_far(): return lax.ppermute(x, 'space', far_route)  8.68 us
    ppermute x4, waiting for transfers between devices, swap_near(): return lax.ppermute(x, 'space', near_route)  2.06 us
    ppermute x4, starting transfers between devices, swap_near(): return lax.ppermute(x, 'space', near_route)  1.29 us
  transfers between devices with their start and end apart: 6, of which 4 were waited for; matrix products, arithmetic and copies ran while one was open for 0% of the time, Pallas kernels for 20%

profile of v4, /device:TPU:127, one launch (start us, length us, event | category | flops | bytes accessed | tf_op | source)
XLA Modules:
  0.0 41.7 jit_solution(1980816010848671168)
XLA Ops:
  0.6 0.7 %shard_map.140.own_ref = f32[4,128]{1,0:T(4,128)S(1)} custom-call(f32[3,128]{1,0:T(4,128)} %pos_hbm.1, s32[1,128]{1,0:T(1,128)} %bitcast.3), custom_call_target="tpu_custom_call" | custom-call | bytes 4096 | tf_op jit(solution)/shard_map/pallas_call | solution.py:599
  1.3 0.8 %collective-permute-start = (f32[4,128]{1,0:T(4,128)S(1)}, f32[4,128]{1,0:T(4,128)S(1)}, u32[]{:S(2)}, u32[]{:S(2)}) collective-permute-start(f32[4,128]{1,0:T(4,128)S(1)} %shard_map.140.own_ref), channel_id=1, source_target_pairs={{0,1},{1,0},{2,3},{3,2},{4,5},{5,4},{6,7},{7,6},{8,9},{9,8},{10,11... | collective-permute-start | bytes 6152 | tf_op jit(solution)/shard_map/ppermute | solution.py:642
  2.1 1.1 %shard_map.141.edges_ref = f32[32,128]{1,0:T(8,128)S(1)} custom-call(s32[24,128]{1,0:T(8,128)} %nb_hbm.1, s32[2,64]{1,0:T(2,128)} %gi_hbm.1, s32[1,128]{1,0:T(1,128)} %bitcast.4), custom_call_target="tpu_custom_call" | custom-call | flops 100000000 | bytes 29696 | tf_op jit(solution)/shard_map/pallas_call | solution.py:599
  3.2 0.0 collective-permute-done.near_ref
  3.3 4.2 %collective-permute-start.1 = (f32[40,128]{1,0:T(8,128)S(1)}, f32[40,128]{1,0:T(8,128)S(1)}, u32[]{:S(2)}, u32[]{:S(2)}) collective-permute-start(f32[40,128]{1,0:T(8,128)S(1)} %pad_maximum_fusion), channel_id=1, source_target_pairs={{1,2},{2,1},{3,4},{4,3},{5,6},{6,5},{7,8},{8,7},{9,10},{10,9},{11,... | collective-permute-start | bytes 61448 | tf_op jit(solution)/shard_map/ppermute | solution.py:645
  7.5 1.7 %shard_map.142 = (bf16[256,3072]{1,0:T(8,128)(2,1)S(1)}, bf16[2,64,32]{2,1,0:T(8,128)(2,1)S(1)}, bf16[2,64,192]{2,1,0:T(8,128)(2,1)S(1)}, bf16[2,128,192]{2,1,0:...) custom-call(f32[2,8,64]{2,1,0:T(8,128)} %rin_hbm.1, ...), custom_call_target="tpu_custom_call" | custom-call | flops 100000000 | bytes 2048000 | tf_op jit(solution)/shard_map/pallas_call | solution.py:599
  9.2 4.6 %collective-permute-done.1.far_ref.there_ref = f32[40,128]{1,0:T(8,128)S(1)} collective-permute-done((f32[40,128]{1,0:T(8,128)S(1)}, f32[40,128]{1,0:T(8,128)S(1)}, u32[]{:S(2)}, u32[]{:S(2)}) %collective-permute-start.1) | collective-permute-done | bytes 20512 | tf_op jit(solution)/shard_map/ppermute | solution.py:645
  13.8 3.9 %shard_map.143 = (f32[2,256,128]{2,1,0:T(8,128)S(1)}, f32[128,128]{1,0:T(8,128)S(1)}, bf16[2,128,256]{2,1,0:T(8,128)(2,1)S(1)}, f32[2,8,3072]{2,1,0:T(8,128)S(1)...) custom-call(f32[4,128]{1,0:T(4,128)S(1)} %shard_map.140.own_ref, ...), custom_call_target="tpu_custom_call" | custom-call | flops 2000000000 | bytes 3147264 | tf_op jit(solution)/shard_map/pallas_call | solution.py:599
  17.6 0.1 collective-permute-start.2
  17.7 1.5 %shard_map.144 = (f32[128,3072]{1,0:T(8,128)S(1)}, f32[128,3072]{1,0:T(8,128)S(1)}) custom-call(f32[2,2,8,3072]{3,2,1,0:T(8,128)S(1)} %get-tuple-element.41.basis_ref, bf16[2,64,32]{2,1,0:T(8,128)(2,1)S(1)} %get-tuple-element.33.win_ref, bf16[2,64,192]{2,1,0:T(8,128)(2,1)S(1)} %get-tuple-element.34.wmid_ref, bf16[2,128,192]{2,1,0:T(8,128)(2,1)S(1)} %get-tuple-element.35.wout_ref), custom_call_target="tpu_custom_call" | custom-call | flops 2000000000 | bytes 3694592 | tf_op jit(solution)/shard_map/pallas_call | solution.py:599
  19.2 0.0 collective-permute-done.2.near_ref
  19.2 3.7 %shard_map.145 = (f32[1,128]{1,0:T(1,128)}, f32[256,128]{1,0:T(8,128)S(1)}, f32[256,128]{1,0:T(8,128)S(1)}, f32[128,128]{1,0:T(8,128)S(1)}, f32[128,128]{1,0:T(8...) custom-call(f32[2,256,128]{2,1,0:T(8,128)S(1)} %get-tuple-element.38.feats_ref, ...), custom_call_target="tpu_custom_call" | custom-call | flops 1000000000 | bytes 5678080 | tf_op jit(solution)/shard_map/pallas_call | solution.py:599
  23.0 0.5 %collective-permute-start.3 = (f32[128,128]{1,0:T(8,128)S(1)}, f32[128,128]{1,0:T(8,128)S(1)}, u32[]{:S(2)}, u32[]{:S(2)}) collective-permute-start(f32[128,128]{1,0:T(8,128)S(1)} %get-tuple-element.48), channel_id=1, source_target_pairs={{0,1},{1,0},{2,3},{3,2},{4,5},{5,4},{6,7},{7,6},{8,9},{9,8},{10,11... | collective-permute-start | bytes 196616 | tf_op jit(solution)/shard_map/ppermute | solution.py:642
  23.5 0.9 %collective-permute-done.3.near_ref = f32[128,128]{1,0:T(8,128)S(1)} collective-permute-done((f32[128,128]{1,0:T(8,128)S(1)}, f32[128,128]{1,0:T(8,128)S(1)}, u32[]{:S(2)}, u32[]{:S(2)}) %collective-permute-start.3) | collective-permute-done | bytes 65568 | tf_op jit(solution)/shard_map/ppermute | solution.py:642
  24.4 0.1 shard_map.146.sent_ref
  24.5 4.4 %collective-permute-start.4 = (f32[392,128]{1,0:T(8,128)S(1)}, f32[392,128]{1,0:T(8,128)S(1)}, u32[]{:S(2)}, u32[]{:S(2)}) collective-permute-start(f32[392,128]{1,0:T(8,128)S(1)} %shard_map.146.sent_ref), channel_id=1, source_target_pairs={{1,2},{2,1},{3,4},{4,3},{5,6},{6,5},{7,8},{8,7},{9,10},{10,9},{11,... | collective-permute-start | bytes 602120 | tf_op jit(solution)/shard_map/ppermute | solution.py:645
  28.9 3.8 %shard_map.147 = (f32[2,192,3072]{2,1,0:T(8,128)S(1)}, bf16[128,3072]{1,0:T(8,128)(2,1)S(1)}) custom-call(f32[2,2,8,3072]{3,2,1,0:T(8,128)S(1)} %get-tuple-element.41.basis_ref, bf16[2,128,256]{2,1,0:T(8,128)(2,1)S(1)} %get-tuple-element.52.htab_ref, bf16[256,3072]{1,0:T(8,128)(2,1)S(1)} %get-tuple-element.31.sel_ref, ...), custom_call_target="tpu_custom_call" | custom-call | flops 4000000000 | bytes 7778304 | tf_op jit(solution)/shard_map/pallas_call | solution.py:599
  32.7 4.2 %collective-permute-done.4.far_ref = f32[392,128]{1,0:T(8,128)S(1)} collective-permute-done((f32[392,128]{1,0:T(8,128)S(1)}, f32[392,128]{1,0:T(8,128)S(1)}, u32[]{:S(2)}, u32[]{:S(2)}) %collective-permute-start.4) | collective-permute-done | bytes 200736 | tf_op jit(solution)/shard_map/ppermute | solution.py:645
  36.9 3.0 %shard_map.148 = (f32[8,128]{1,0:T(8,128)S(1)}, f32[8,128]{1,0:T(8,128)S(1)}) custom-call(f32[392,128]{1,0:T(8,128)S(1)} %shard_map.146.sent_ref, f32[392,128]{1,0:T(8,128)S(1)} %collective-permute-done.4.far_ref, f32[256,128]{1,0:T(8,128)S(1)} %get-tuple-element.51.gghost_ref, bf16[256,3072]{1,0:T(8,128)(2,1)S(1)} %get-tuple-element.31.sel_ref, ...), custom_call_target="tpu_custom_call" | custom-call | flops 1000000000 | bytes 8146944 | tf_op jit(solution)/shard_map/pallas_call | solution.py:599
  39.9 0.0 collective-permute-start.5
  40.0 1.2 %collective-permute-done.5 = f32[8,128]{1,0:T(8,128)S(1)} collective-permute-done((f32[8,128]{1,0:T(8,128)S(1)}, f32[8,128]{1,0:T(8,128)S(1)}, u32[]{:S(2)}, u32[]{:S(2)}) %collective-permute-start.5) | collective-permute-done | bytes 4128 | tf_op jit(solution)/shard_map/ppermute | solution.py:642
  41.1 0.6 %add_negate_fusion = f32[3,128]{1,0:T(4,128)} fusion(f32[8,128]{1,0:T(8,128)S(1)} %collective-permute-done.5, f32[8,128]{1,0:T(8,128)S(1)} %get-tuple-element.58, pred[128]{0:T(512)(128)(4,1)S(1)} %compare_compare_fusion), kind=kLoop, calls=%fused_computation.1 | loop fusion | flops 1152 | bytes 4736 | tf_op jit(solution)/shard_map/neg | solution.py:762
  (2 shorter events, 0.0 us)
Async XLA Ops:
  1.3 1.9 %collective-permute-start = (f32[4,128]{1,0:T(4,128)S(1)}, f32[4,128]{1,0:T(4,128)S(1)}, u32[]{:S(2)}, u32[]{:S(2)}) collective-permute-start(f32[4,128]{1,0:T(4,128)S(1)} %shard_map.140.own_ref), channel_id=1, source_target_pairs={{0,1},{1,0},{2,3},{3,2},{4,5},{5,4},{6,7},{7,6},{8,9},{9,8},{10,11... | collective-permute-start | bytes 6152 | tf_op jit(solution)/shard_map/ppermute | solution.py:642
  3.3 10.5 %collective-permute-start.1 = (f32[40,128]{1,0:T(8,128)S(1)}, f32[40,128]{1,0:T(8,128)S(1)}, u32[]{:S(2)}, u32[]{:S(2)}) collective-permute-start(f32[40,128]{1,0:T(8,128)S(1)} %pad_maximum_fusion), channel_id=1, source_target_pairs={{1,2},{2,1},{3,4},{4,3},{5,6},{6,5},{7,8},{8,7},{9,10},{10,9},{11,... | collective-permute-start | bytes 61448 | tf_op jit(solution)/shard_map/ppermute | solution.py:645
  17.6 1.6 %collective-permute-start.2 = (f32[128,128]{1,0:T(8,128)S(1)}, f32[128,128]{1,0:T(8,128)S(1)}, u32[]{:S(2)}, u32[]{:S(2)}) collective-permute-start(f32[128,128]{1,0:T(8,128)S(1)} %get-tuple-element.39), channel_id=1, source_target_pairs={{0,1},{1,0},{2,3},{3,2},{4,5},{5,4},{6,7},{7,6},{8,9},{9,8},{10,11... | collective-permute-start | bytes 196616 | tf_op jit(solution)/shard_map/ppermute | solution.py:642
  23.0 1.4 %collective-permute-start.3 = (f32[128,128]{1,0:T(8,128)S(1)}, f32[128,128]{1,0:T(8,128)S(1)}, u32[]{:S(2)}, u32[]{:S(2)}) collective-permute-start(f32[128,128]{1,0:T(8,128)S(1)} %get-tuple-element.48), channel_id=1, source_target_pairs={{0,1},{1,0},{2,3},{3,2},{4,5},{5,4},{6,7},{7,6},{8,9},{9,8},{10,11... | collective-permute-start | bytes 196616 | tf_op jit(solution)/shard_map/ppermute | solution.py:642
  24.5 12.5 %collective-permute-start.4 = (f32[392,128]{1,0:T(8,128)S(1)}, f32[392,128]{1,0:T(8,128)S(1)}, u32[]{:S(2)}, u32[]{:S(2)}) collective-permute-start(f32[392,128]{1,0:T(8,128)S(1)} %shard_map.146.sent_ref), channel_id=1, source_target_pairs={{1,2},{2,1},{3,4},{4,3},{5,6},{6,5},{7,8},{8,7},{9,10},{10,9},{11,... | collective-permute-start | bytes 602120 | tf_op jit(solution)/shard_map/ppermute | solution.py:645
  39.9 1.2 %collective-permute-start.5 = (f32[8,128]{1,0:T(8,128)S(1)}, f32[8,128]{1,0:T(8,128)S(1)}, u32[]{:S(2)}, u32[]{:S(2)}) collective-permute-start(f32[8,128]{1,0:T(8,128)S(1)} %get-tuple-element.59), channel_id=1, source_target_pairs={{0,1},{1,0},{2,3},{3,2},{4,5},{5,4},{6,7},{7,6},{8,9},{9,8},{10,11... | collective-permute-start | bytes 12296 | tf_op jit(solution)/shard_map/ppermute | solution.py:642

commit v5 on v4

v5 whole, which is shorter than its diff:
```python
import jax
import jax.numpy as jnp
from jax import lax
from jax.experimental import pallas as pl
from jax.experimental.pallas import tpu as pltpu
from jax.sharding import PartitionSpec as P

RADIUS = 5.0
SOFTEN = 0.25
F32 = jnp.float32
BF16 = jnp.bfloat16
HALF = 64
MIB = 1024 * 1024


def hdot(a, b, dims=(((1,), (0,)), ((), ()))):
    return lax.dot_general(
        a, b, dims, precision=lax.Precision.HIGHEST, preferred_element_type=F32
    )


def hdot_t(a, b):
    return hdot(a, b, (((0,), (0,)), ((), ())))


def bdot(a, b):
    return jnp.dot(a, b, preferred_element_type=F32)


def bdot_nt(a, b):
    return lax.dot_general(a, b, (((1,), (1,)), ((), ())), preferred_element_type=F32)


def high(x):
    return x.astype(BF16).astype(F32)


def split(x):
    hi = x.astype(BF16)
    return hi, (x - hi.astype(F32)).astype(BF16)


def stack3(x):
    hi, lo = split(x)
    return jnp.concatenate([hi, lo, hi], axis=0)


def slot(k):
    return slice(k * 128, (k + 1) * 128)


def sigmoid(v):
    return 0.5 + 0.5 * jnp.tanh(0.5 * v)


def roll64(x):
    return pltpu.roll(x, HALF, 1)


def lane_low(rows):
    return lax.broadcasted_iota(jnp.int32, (rows, 128), 1) < HALF


def parity_odd(rows):
    odd = lax.rem(lax.axis_index("space"), 2)
    return jnp.full((rows, 128), odd, jnp.int32) > 0


def far_lanes(rows):
    return parity_odd(rows) == lane_low(rows)


def copy_in(moves, sems):
    copies = [
        pltpu.make_async_copy(src, dst, sems.at[i]) for i, (src, dst) in enumerate(moves)
    ]
    for c in copies:
        c.start()
    for c in copies:
        c.wait()


def pack_kernel(
    pos_hbm, kind_hbm, nb_hbm, gi_hbm, counts_hbm, own_ref, nb_ref, gi_ref, counts_ref, pos_ref, kind_ref, sems
):
    copy_in(
        [
            (pos_hbm, pos_ref),
            (kind_hbm, kind_ref),
            (nb_hbm, nb_ref),
            (gi_hbm, gi_ref),
            (counts_hbm, counts_ref),
        ],
        sems,
    )
    own_ref[0:3, :] = pos_ref[...]
    own_ref[3:4, :] = (kind_ref[...] + 1).astype(F32)


def remap_kernel(nb_ref, gi_ref, counts_ref, out_ref, hot_ref):
    slots, atoms = nb_ref.shape
    rows = lax.broadcasted_iota(jnp.int32, (atoms, atoms), 0) + atoms
    for k in range(slots):
        nb = jnp.broadcast_to(nb_ref[k : k + 1, :], (atoms, atoms))
        hot_ref[:, slot(k)] = (rows == nb).astype(F32).astype(BF16)
    place = jnp.concatenate(
        [jnp.broadcast_to(gi_ref[i : i + 1, :], (16, HALF)).astype(F32) for i in range(2)], axis=1
    )
    ghost = bdot(place.astype(BF16), hot_ref[...])
    for k in range(slots):
        nb = nb_ref[k : k + 1, :]
        out_ref[k : k + 1, :] = jnp.where(
            nb < atoms, nb.astype(F32), ghost[0:1, slot(k)] + F32(atoms)
        )
    out_ref[slots : slots + 1, :] = counts_ref[...].astype(F32)
    out_ref[slots + 1 :, :] = jnp.zeros((out_ref.shape[0] - slots - 1, atoms), F32)


def build_selector(rows_f32, sel_ref):
    count, atoms = rows_f32.shape
    rows = lax.broadcasted_iota(jnp.int32, (2 * atoms, atoms), 0).astype(F32)
    for k in range(count):
        nb = jnp.broadcast_to(rows_f32[k : k + 1, :], (2 * atoms, atoms))
        sel_ref[:, slot(k)] = (rows == nb).astype(F32).astype(BF16)


def prep_kernel(
    rin_hbm,
    rmid_hbm,
    rout_hbm,
    embed_hbm,
    mix_one_hbm,
    vec_hbm,
    mix_two_hbm,
    read_hbm,
    edges_ref,
    sel_ref,
    win_ref,
    wmid_ref,
    wout_ref,
    embed_ref,
    mix_one_ref,
    vec_ref,
    mix_two_ref,
    read_ref,
    rin_ref,
    rmid_ref,
    rout_ref,
    sems,
):
    copy_in(
        [
            (rin_hbm, rin_ref),
            (rmid_hbm, rmid_ref),
            (rout_hbm, rout_ref),
            (embed_hbm, embed_ref),
            (mix_one_hbm, mix_one_ref),
            (vec_hbm, vec_ref),
            (mix_two_hbm, mix_two_ref),
            (read_hbm, read_ref),
        ],
        sems,
    )
    build_selector(edges_ref[0 : sel_ref.shape[1] // edges_ref.shape[1], :], sel_ref)
    for layer in range(2):
        w = rin_ref[layer]
        h = high(w)
        lo = w - h
        win_ref[layer] = jnp.concatenate([h, h, lo, lo], axis=0).T.astype(BF16)
        w = rmid_ref[layer]
        h = high(w)
        wmid_ref[layer] = jnp.concatenate([h, h, w - h], axis=0).T.astype(BF16)
        w = rout_ref[layer]
        h = high(w)
        wout_ref[layer] = jnp.concatenate([h, h, w - h], axis=0).T.astype(BF16)


def basis_rows(b):
    h = high(b)
    lo = b - h
    return jnp.concatenate([h, lo, h, lo], axis=0).astype(BF16)


def radial(win, wmid, wout, b):
    v1 = bdot(win, basis_rows(b))
    v2 = bdot(wmid, stack3(v1 * sigmoid(v1)))
    return bdot(wout, stack3(v2 * sigmoid(v2)))


def silu_pair(v, t):
    s = sigmoid(v)
    z = v * s
    return z, (s + z * (1.0 - s)) * t


def radial_pair(win, wmid, wout, b, db):
    z1, t1 = silu_pair(bdot(win, basis_rows(b)), bdot(win, basis_rows(db)))
    z2, t2 = silu_pair(bdot(wmid, stack3(z1)), bdot(wmid, stack3(t1)))
    return bdot(wout, stack3(z2)), bdot(wout, stack3(t2))


def spread_rows(row, rows):
    return jnp.broadcast_to(row, (rows, row.shape[1]))


def geometry(far, own, valid):
    vec = [f - o for f, o in zip(far, own)]
    r2 = vec[0] * vec[0] + vec[1] * vec[1] + vec[2] * vec[2] + SOFTEN
    inv = lax.rsqrt(r2)
    inv = inv * (1.5 - 0.5 * r2 * inv * inv)
    rho = r2 * inv
    unit = [v * inv for v in vec]
    x = jnp.minimum(rho * (1.0 / RADIUS), 1.0)
    y = 1.0 - x
    x2 = x * x
    env = y * y * y * (1.0 + x * (3.0 + x * (6.0 + x * (10.0 + x * 15.0))))
    denv = (-105.0 / RADIUS) * x2 * x2 * y * y
    f = RADIUS * inv * env * valid
    df = RADIUS * inv * (denv - env * inv) * valid
    n = (lax.broadcasted_iota(jnp.int32, rho.shape, 0) + 1).astype(F32)
    turns = n * x
    whole = jnp.floor(turns + 0.5)
    frac = (turns - whole) * jnp.pi
    parity = whole - 2.0 * jnp.floor(0.5 * whole)
    sign = 1.0 - 2.0 * parity
    q = frac * frac
    sin = frac * (
        1.0
        + q * (-1 / 6 + q * (1 / 120 + q * (-1 / 5040 + q * (1 / 362880 + q * (-1 / 39916800)))))
    )
    cos = 1.0 + q * (
        -1 / 2
        + q * (1 / 24 + q * (-1 / 720 + q * (1 / 40320 + q * (-1 / 3628800 + q * (1 / 479001600)))))
    )
    sin = sin * sign
    cos = cos * sign
    return unit, inv, sin * f, sin * df + (n * (jnp.pi / RADIUS)) * cos * f


def make_table(table, embed, tab_ref):
    species, width = embed.shape
    columns = table.shape[1]
    parts = []
    for c in range(3):
        p = jnp.broadcast_to(table[c : c + 1], (8, columns))
        h = high(p)
        m = high(p - h)
        parts += [h, m, p - h - m]
    kind = jnp.broadcast_to(table[3:4], (species, columns))
    onehot = (
        kind == (lax.broadcasted_iota(jnp.int32, (species, columns), 0) + 1).astype(F32)
    ).astype(F32)
    h0 = hdot_t(embed, onehot)
    h0_hi = high(h0)
    zero = jnp.zeros((8, columns), F32)
    tab_ref[...] = jnp.concatenate([h0_hi, h0 - h0_hi] + parts + [zero], axis=0).astype(BF16)
    return h0


def gathered(g, width):
    base = 2 * width
    far = [
        g[base + 24 * c : base + 24 * c + 8]
        + g[base + 24 * c + 8 : base + 24 * c + 16]
        + g[base + 24 * c + 16 : base + 24 * c + 24]
        for c in range(3)
    ]
    return far, g[:width] + g[width:base]


def edge_geometry(far, own, counts, tiles):
    centre = [jnp.concatenate([spread_rows(own[c : c + 1], 8)] * tiles, axis=1) for c in range(3)]
    valid = jnp.concatenate([(counts > F32(k)).astype(F32) for k in range(tiles)], axis=1)
    return geometry(far, centre, valid)


def messages(w, h, unit, width, tiles):
    atoms = 128
    wa = w[:width] * h
    wb = w[width:] * h
    a_sum = jnp.zeros((width, atoms), F32)
    b_sum = [jnp.zeros((width, atoms), F32) for _ in range(3)]
    for k in range(tiles):
        a_sum = a_sum + wa[:, slot(k)]
        for c in range(3):
            b_sum[c] = b_sum[c] + wb[:, slot(k)] * tile8(unit[c][:, slot(k)], width // 8)
    return a_sum, b_sum


def tile8(x, times):
    return jnp.concatenate([x] * times, axis=0)


def mixed_pre(a, b_all, h0_own, mix_ref):
    atoms = a.shape[1]
    sq = b_all * b_all
    q = sq[:, :atoms] + sq[:, atoms : 2 * atoms] + sq[:, 2 * atoms :]
    return hdot_t(mix_ref[0], a) + hdot_t(mix_ref[1], h0_own) + hdot_t(mix_ref[2], q)


def features(pre, b_all, vec):
    atoms = pre.shape[1]
    v1 = hdot_t(vec, b_all)
    return (
        jnp.concatenate([pre * sigmoid(pre), v1[:, :atoms]], axis=0),
        jnp.concatenate([v1[:, atoms : 2 * atoms], v1[:, 2 * atoms :]], axis=0),
    )


def doubled(x):
    rows = x.shape[0]
    low = lane_low(rows)
    other = roll64(x)
    return jnp.where(low == parity_odd(rows), x, other)


def layer_one_kernel(
    own_ref,
    near_ref,
    edges_ref,
    far_ref,
    sel_ref,
    embed_ref,
    win_ref,
    wmid_ref,
    wout_ref,
    mix_ref,
    vec_ref,
    feats_ref,
    far_feats_ref,
    near_out,
    htab_ref,
    ftab_ref,
    geom_ref,
    basis_ref,
    pre_ref,
    b_ref,
    sel_far_ref,
    tab_ref,
):
    atoms = own_ref.shape[1]
    slots = sel_ref.shape[1] // atoms
    tiles = slots // 2
    width = embed_ref.shape[1]
    embed = embed_ref[...]
    scale = 1.0 / jnp.sqrt(F32(slots))
    ours = far_lanes(4)
    own = own_ref[...]
    there = far_ref[...]
    low12 = lane_low(tiles)
    lists = there[8 : 8 + slots]
    first = lists[:tiles]
    second = lists[tiles:]
    odd12 = parity_odd(tiles)
    build_selector(
        jnp.where(
            low12,
            jnp.where(odd12, first, roll64(first)),
            jnp.where(odd12, roll64(second), second),
        ),
        sel_far_ref,
    )
    h0 = make_table(
        jnp.concatenate([own, jnp.where(ours, there[0:4], near_ref[...])], axis=1), embed, tab_ref
    )
    h0_far = make_table(
        jnp.concatenate([there[0:4], jnp.where(ours, there[4:8], own)], axis=1), embed, ftab_ref
    )
    htab_ref[...] = tab_ref[0 : 2 * width, :]
    g = bdot(tab_ref[...], sel_ref[...])
    gf = bdot(ftab_ref[...], sel_far_ref[...])

    far, h_far = gathered(g, width)
    counts = spread_rows(edges_ref[slots : slots + 1, :], 8)
    unit, inv, b, db = edge_geometry(far, own, counts, slots)
    for i, x in enumerate(unit + [inv]):
        geom_ref[i : i + 1, :] = x[0:1]
    basis_ref[0] = b
    basis_ref[1] = db
    far, far_h = gathered(gf, width)
    half = doubled(there)
    counts = spread_rows(half[8 + slots : 9 + slots], 8) - jnp.where(
        lane_low(8), F32(0), F32(tiles)
    )
    far_unit, _, far_b, _ = edge_geometry(far, half, counts, tiles)

    win, wmid, wout = win_ref[0], wmid_ref[0], wout_ref[0]
    w = radial(win, wmid, wout, b)
    wf = radial(win, wmid, wout, far_b)
    a, b = messages(w, h_far, unit, width, slots)
    b_all = jnp.concatenate(b, axis=1) * scale
    pre = mixed_pre(a * scale, b_all, h0[:, :atoms], mix_ref)
    pre_ref[...] = pre
    b_ref[...] = b_all
    vec = vec_ref[...]
    lo_part, hi_part = features(pre, b_all, vec)
    feats_ref[0 : 2 * width] = lo_part
    feats_ref[2 * width :] = hi_part
    low_lanes, high_lanes = packed(lo_part, hi_part)
    near_out[...] = jnp.where(parity_odd(2 * width), low_lanes, high_lanes)

    a, b = messages(wf, far_h, far_unit, width, tiles)
    a = (a + roll64(a)) * scale
    b_all = jnp.concatenate([x + roll64(x) for x in b], axis=1) * scale
    pre = mixed_pre(a, b_all, doubled(h0_far[:, :atoms]), mix_ref)
    lo_part, hi_part = features(pre, b_all, vec)
    far_feats_ref[0 : 2 * width] = lo_part
    far_feats_ref[2 * width :] = hi_part


def packed(lo_part, hi_part):
    low = lane_low(lo_part.shape[0])
    return (
        jnp.where(low, lo_part, roll64(hi_part)),
        jnp.where(low, roll64(lo_part), hi_part),
    )


def unpacked(tile, high_half):
    other = roll64(tile)
    return jnp.where(high_half, other, tile), jnp.where(high_half, tile, other)


def radial_two_kernel(basis_ref, win_ref, wmid_ref, wout_ref, w_ref, dw_ref):
    w, dw = radial_pair(win_ref[1], wmid_ref[1], wout_ref[1], basis_ref[0], basis_ref[1])
    w_ref[...] = w
    dw_ref[...] = dw


def edge_gradient(unit, inv, drho, du):
    dot = unit[0] * du[0] + unit[1] * du[1] + unit[2] * du[2]
    radial_part = drho - dot * inv
    return [unit[c] * radial_part + du[c] * inv for c in range(3)]


def sum_groups(x):
    total = x[0:8]
    for i in range(1, x.shape[0] // 8):
        total = total + x[8 * i : 8 * i + 8]
    return total


def put_positions(ref, base, grads):
    x = jnp.concatenate(list(grads), axis=0)
    hi, lo = split(x)
    ref[base : base + 24] = hi
    ref[base + 24 : base + 48] = lo


def rows8(x):
    sums = [jnp.sum(x[8 * c : 8 * c + 8], axis=0, keepdims=True) for c in range(3)]
    return jnp.concatenate(sums + [jnp.zeros((5, x.shape[1]), F32)], axis=0)


def centre_sum(grads, slots):
    x = jnp.concatenate(list(grads), axis=0)
    total = x[:, slot(0)]
    for k in range(1, slots):
        total = total + x[:, slot(k)]
    return total


def layer_two_kernel(
    feats_ref,
    far_feats_ref,
    near_ref,
    sel_ref,
    geom_ref,
    w_ref,
    dw_ref,
    mix_ref,
    read_ref,
    energy_ref,
    gown_ref,
    gghost_ref,
    near_out,
    far_out,
    gpos_ref,
    gpos_ghost_ref,
    grad_scr,
):
    atoms = feats_ref.shape[1]
    width = mix_ref.shape[1]
    slots = sel_ref.shape[1] // atoms
    rows = 2 * width
    odd = parity_odd(rows)
    ours = far_lanes(rows)
    near_lo, near_hi = unpacked(near_ref[...], odd)
    g_lo = jnp.where(ours, far_feats_ref[0:rows], near_lo)
    g_hi = jnp.where(ours, far_feats_ref[rows:], near_hi)
    feats = feats_ref[...]
    table = jnp.concatenate([feats, jnp.concatenate([g_lo, g_hi], axis=0)], axis=1)
    t_hi, t_lo = split(table)
    g = bdot(jnp.concatenate([t_hi, t_lo], axis=0), sel_ref[...])

    f = g[: 4 * width] + g[4 * width :]
    unit = [geom_ref[c : c + 1, :] for c in range(3)]
    along = f[width : 2 * width] * spread_rows(unit[0], width)
    along = along + f[2 * width : 3 * width] * spread_rows(unit[1], width)
    along = along + f[3 * width :] * spread_rows(unit[2], width)
    msg = w_ref[0:width] * f[:width] + w_ref[width:] * along
    m = jnp.zeros((width, atoms), F32)
    for k in range(slots):
        m = m + msg[:, slot(k)]
    scale = 1.0 / jnp.sqrt(F32(slots))
    s1 = feats[:width]
    pre = hdot_t(mix_ref[0], m * scale) + hdot_t(mix_ref[1], s1)
    sg = sigmoid(pre)
    s2 = pre * sg
    energy_ref[...] = hdot(read_ref[0:1], s1) + hdot(read_ref[1:2], s2)
    read = read_ref[...].T
    r_one = jnp.broadcast_to(read[:, 0:1], (width, atoms))
    r_two = jnp.broadcast_to(read[:, 1:2], (width, atoms))
    gpre = r_two * (sg + s2 * (1.0 - sg))
    gm = hdot(mix_ref[0], gpre) * scale
    gs_own = r_one + hdot(mix_ref[1], gpre)
    gm_rep = jnp.concatenate([gm] * slots, axis=1)
    ga = w_ref[0:width] * gm_rep
    gb = w_ref[width:] * gm_rep
    for i, x in enumerate([ga] + [gb * spread_rows(u, width) for u in unit]):
        hi, lo = split(x)
        grad_scr[i * width : (i + 1) * width] = hi
        grad_scr[(4 + i) * width : (5 + i) * width] = lo
    drho = gm_rep * (dw_ref[0:width] * f[:width] + dw_ref[width:] * along)
    du = [sum_groups(gb * f[(c + 1) * width : (c + 2) * width]) for c in range(3)]
    gp = edge_gradient(
        [spread_rows(u, 8) for u in unit],
        spread_rows(geom_ref[3:4, :], 8),
        sum_groups(drho),
        du,
    )
    put_positions(grad_scr, 8 * width, gp)
    centre = centre_sum(gp, slots)
    acc = bdot_nt(grad_scr[...], sel_ref[...])
    grads = acc[: 4 * width] + acc[4 * width : 8 * width]
    own = grads[:, :atoms]
    gown_ref[0:width] = own[0:width] + gs_own
    gown_ref[width:] = own[width:]
    ghost = grads[:, atoms:]
    gghost_ref[...] = ghost
    to_upper, to_lower = packed(ghost[:rows], ghost[rows:])
    near_out[...] = jnp.where(odd, to_lower, to_upper)
    far_out[...] = jnp.where(odd, to_upper, to_lower)
    pos = acc[8 * width : 8 * width + 24] + acc[8 * width + 24 :]
    gpos_ref[...] = rows8(pos[:, :atoms] - centre)
    gpos_ghost_ref[...] = rows8(pos[:, atoms:])


def join_kernel(gown_ref, near_ref, far_ref, gpos_ghost_ref, out_ref):
    rows = near_ref.shape[0]
    odd = parity_odd(rows)
    ours = far_lanes(rows)
    zero = jnp.zeros(near_ref.shape, F32)
    lo, hi = unpacked(near_ref[...], jnp.logical_not(odd))
    out_ref[0:rows] = gown_ref[0:rows] + jnp.where(ours, lo, zero)
    out_ref[rows : 2 * rows] = gown_ref[rows:] + jnp.where(ours, hi, zero)
    out_ref[2 * rows : 3 * rows] = far_ref[...]
    out_ref[3 * rows :] = gpos_ghost_ref[...]


def tangent_one_kernel(
    basis_ref,
    htab_ref,
    ftab_ref,
    sel_ref,
    there_ref,
    win_ref,
    wmid_ref,
    wout_ref,
    mix_ref,
    embed_ref,
    edge_ref,
    sel_ghost_ref,
    geom_ref,
    pre_ref,
    b_ref,
    sel_scr,
):
    atoms = there_ref.shape[1]
    width = htab_ref.shape[0] // 2
    slots = sel_ref.shape[1] // atoms
    win, wmid, wout = win_ref[0], wmid_ref[0], wout_ref[0]

    def store(domain, w, dw, h):
        edge_ref[domain, 0:width] = dw[:width] * h
        edge_ref[domain, width : 2 * width] = dw[width:] * h
        edge_ref[domain, 2 * width :] = w[width:] * h

    w, dw = radial_pair(win, wmid, wout, basis_ref[0], basis_ref[1])
    g = bdot(htab_ref[...], sel_ref[...])
    store(0, w, dw, g[:width] + g[width:])

    there = there_ref[...]
    build_selector(there[8 : 8 + slots], sel_scr)
    sel_ghost_ref[...] = sel_scr[atoms:]
    far, h = gathered(bdot(ftab_ref[...], sel_scr[...]), width)
    counts = spread_rows(there[8 + slots : 9 + slots], 8)
    unit, inv, b, db = edge_geometry(far, there, counts, slots)
    for i, x in enumerate(unit + [inv]):
        geom_ref[i : i + 1, :] = x[0:1]
    w, dw = radial_pair(win, wmid, wout, b, db)
    store(1, w, dw, h)
    a, b = messages(w, h, unit, width, slots)
    scale = 1.0 / jnp.sqrt(F32(slots))
    b_all = jnp.concatenate(b, axis=1) * scale
    species = embed_ref.shape[0]
    kind = jnp.broadcast_to(there[3:4], (species, atoms))
    onehot = (
        kind == (lax.broadcasted_iota(jnp.int32, (species, atoms), 0) + 1).astype(F32)
    ).astype(F32)
    pre_ref[...] = mixed_pre(a * scale, b_all, hdot_t(embed_ref[...], onehot), mix_ref)
    b_ref[...] = b_all


def back_one_kernel(
    sent_ref,
    far_ref,
    gghost_ref,
    sel_ref,
    sel_ghost_ref,
    geom_ref,
    far_geom_ref,
    edge_ref,
    pre_ref,
    far_pre_ref,
    b_ref,
    far_b_ref,
    mix_ref,
    vec_ref,
    gpos_ref,
    gown_out,
    ghost_out,
    pos_scr,
    far_pos_scr,
):
    atoms = gpos_ref.shape[1]
    width = mix_ref.shape[1]
    slots = sel_ref.shape[1] // atoms
    rows = 2 * width
    odd = parity_odd(rows)
    ours = far_lanes(rows)
    zero = jnp.zeros((rows, atoms), F32)
    scale = 1.0 / jnp.sqrt(F32(slots))
    lo, hi = unpacked(far_ref[2 * rows : 3 * rows], odd)
    g_lo = sent_ref[0:rows] + jnp.where(ours, zero, lo)
    g_hi = sent_ref[rows : 2 * rows] + jnp.where(ours, zero, hi)
    f_lo = far_ref[0:rows] + jnp.where(ours, gghost_ref[0:rows], zero)
    f_hi = far_ref[rows : 2 * rows] + jnp.where(ours, gghost_ref[rows:], zero)
    pre = jnp.concatenate([pre_ref[...], far_pre_ref[...]], axis=1)
    sg = sigmoid(pre)
    gpre = jnp.concatenate([g_lo[:width], f_lo[:width]], axis=1) * (sg + pre * sg * (1.0 - sg))
    ga = hdot(mix_ref[0], gpre) * scale
    gq = hdot(mix_ref[2], gpre) * (2.0 * scale)
    gv = jnp.concatenate(
        [g_lo[width:], g_hi[:width], g_hi[width:], f_lo[width:], f_hi[:width], f_hi[width:]],
        axis=1,
    )
    gb_all = hdot(vec_ref[...], gv) * scale
    b_of = [b_ref, far_b_ref]
    geom_of = [geom_ref, far_geom_ref]
    scr_of = [pos_scr, far_pos_scr]
    for domain in range(2):
        ga_d = ga[:, slot(domain)]
        gq_d = gq[:, slot(domain)]
        gb = [
            gb_all[:, slot(3 * domain + c)] + b_of[domain][:, slot(c)] * gq_d for c in range(3)
        ]
        geom = geom_of[domain]
        total = jnp.zeros((24, atoms), F32)
        for k in range(slots):
            unit = [spread_rows(geom[c : c + 1, slot(k)], 8) for c in range(3)]
            u = [tile8(x, width // 8) for x in unit]
            gbu = gb[0] * u[0] + gb[1] * u[1] + gb[2] * u[2]
            drho = (
                edge_ref[domain, 0:width, slot(k)] * ga_d
                + edge_ref[domain, width : 2 * width, slot(k)] * gbu
            )
            carried = edge_ref[domain, 2 * width :, slot(k)]
            du = [sum_groups(carried * gb[c]) for c in range(3)]
            gp = edge_gradient(unit, spread_rows(geom[3:4, slot(k)], 8), sum_groups(drho), du)
            x = jnp.concatenate(gp, axis=0)
            if domain == 0:
                total = total + x
            hi, lo = split(x)
            scr_of[domain][0:24, slot(k)] = hi
            scr_of[domain][24:48, slot(k)] = lo
        if domain == 0:
            centre = total
    acc = bdot_nt(pos_scr[...], sel_ref[...])
    pos = acc[0:24] + acc[24:48]
    ghost_out[...] = rows8(pos[:, atoms:]) + sent_ref[3 * rows :]
    acc = bdot_nt(far_pos_scr[...], sel_ghost_ref[...])
    there = rows8(acc[0:24] + acc[24:48]) + far_ref[3 * rows :]
    there = jnp.where(far_lanes(8), jnp.zeros((8, atoms), F32), there)
    gown_out[...] = gpos_ref[...] + rows8(pos[:, :atoms] - centre) + there


def call(kernel, out_shapes, args, scratch=(), flops=0, transcendentals=0, far_away=0):
    args = [
        pltpu.with_memory_space_constraint(x, pltpu.HBM) if i < far_away else x
        for i, x in enumerate(args)
    ]
    spaces = [pltpu.HBM] * far_away + [pltpu.VMEM] * (len(args) - far_away)
    moved = sum(x.size * x.dtype.itemsize for x in list(args) + list(out_shapes))
    return pl.pallas_call(
        kernel,
        out_shape=out_shapes,
        in_specs=[pl.BlockSpec(memory_space=space) for space in spaces],
        out_specs=[pl.BlockSpec(memory_space=pltpu.VMEM)] * len(out_shapes),
        scratch_shapes=list(scratch),
        cost_estimate=pl.CostEstimate(
            flops=flops, bytes_accessed=moved, transcendentals=transcendentals
        ),
        compiler_params=pltpu.CompilerParams(vmem_limit_bytes=36 * MIB),
    )(*args)


def shape(dims, dtype=F32):
    return jax.ShapeDtypeStruct(dims, dtype)


def body(
    positions,
    species,
    neighbours,
    counts,
    ghost_index,
    embed,
    radial_in,
    radial_mid,
    radial_out,
    mix_one,
    vec_mix,
    mix_two,
    readout,
):
    atoms = positions.shape[1]
    slots = neighbours.shape[0]
    edges = slots * atoms
    nbasis, hidden = radial_in.shape[1:]
    width = embed.shape[1]
    rows = 2 * width
    devices = lax.axis_size("space")
    near_route = [(i, i ^ 1) for i in range(devices)]
    far_route = [(i, ((i + 1) ^ 1) - 1) for i in range(1, devices - 1)]

    def swap_near(x):
        return lax.ppermute(x, "space", near_route)

    def swap_far(x):
        return lax.ppermute(x, "space", far_route)

    def scratch_of(args):
        return [pltpu.VMEM(x.shape, x.dtype) for x in args]

    def shapes_of(args):
        return [shape(x.shape, x.dtype) for x in args]

    atom_rows = [positions, species[None]]
    lists = [neighbours, ghost_index, counts[None]]
    own, *lists = call(
        pack_kernel,
        [shape((4, atoms))] + shapes_of(lists),
        atom_rows + lists,
        scratch=scratch_of(atom_rows) + [pltpu.SemaphoreType.DMA((5,))],
        far_away=5,
    )
    near = swap_near(own)
    (edge_rows,) = call(
        remap_kernel,
        [shape((slots + 8, atoms))],
        lists,
        scratch=[pltpu.VMEM((atoms, edges), BF16)],
        flops=10**8,
    )
    there = swap_far(jnp.concatenate([own, near, edge_rows], axis=0))
    weights = [radial_in, radial_mid, radial_out]
    passed = [embed, mix_one, vec_mix, mix_two, readout]
    moved = weights + passed
    sel, win, wmid, wout, embed, mix_one, vec_mix, mix_two, readout = call(
        prep_kernel,
        [
            shape((2 * atoms, edges), BF16),
            shape((2, hidden, 4 * nbasis), BF16),
            shape((2, hidden, 3 * hidden), BF16),
            shape((2, 2 * width, 3 * hidden), BF16),
        ]
        + shapes_of(passed),
        moved + [edge_rows],
        scratch=scratch_of(weights) + [pltpu.SemaphoreType.DMA((len(moved),))],
        flops=10**8,
        far_away=len(moved),
    )
    table_rows = 2 * width + 80
    feats, far_feats, near_f, htab, ftab, geom, basis, pre, b_all = call(
        layer_one_kernel,
        [
            shape((4 * width, atoms)),
            shape((4 * width, atoms)),
            shape((rows, atoms)),
            shape((2 * width, 2 * atoms), BF16),
            shape((table_rows, 2 * atoms), BF16),
            shape((8, edges)),
            shape((2, nbasis, edges)),
            shape((width, atoms)),
            shape((width, 3 * atoms)),
        ],
        [own, near, edge_rows, there, sel, embed, win, wmid, wout, mix_one, vec_mix],
        scratch=[
            pltpu.VMEM((2 * atoms, edges // 2), BF16),
            pltpu.VMEM((table_rows, 2 * atoms), BF16),
        ],
        flops=2 * 10**9,
    )
    near_f = swap_near(near_f)
    w, dw = call(
        radial_two_kernel,
        [shape((2 * width, edges)), shape((2 * width, edges))],
        [basis, win, wmid, wout],
        flops=2 * 10**9,
    )
    energy, g_own, g_ghost, near_g, far_g, gpos, gpos_ghost = call(
        layer_two_kernel,
        [
            shape((1, atoms)),
            shape((4 * width, atoms)),
            shape((4 * width, atoms)),
            shape((rows, atoms)),
            shape((rows, atoms)),
            shape((8, atoms)),
            shape((8, atoms)),
        ],
        [feats, far_feats, near_f, sel, geom, w, dw, mix_two, readout],
        scratch=[pltpu.VMEM((8 * width + 48, edges), BF16)],
        flops=10**9,
    )
    near_g = swap_near(near_g)
    (sent,) = call(
        join_kernel, [shape((3 * rows + 8, atoms))], [g_own, near_g, far_g, gpos_ghost]
    )
    come = swap_far(sent)
    edge, sel_ghost, far_geom, far_pre, far_b = call(
        tangent_one_kernel,
        [
            shape((2, 3 * width, edges)),
            shape((atoms, edges), BF16),
            shape((8, edges)),
            shape((width, atoms)),
            shape((width, 3 * atoms)),
        ],
        [basis, htab, ftab, sel, there, win, wmid, wout, mix_one, embed],
        scratch=[pltpu.VMEM((2 * atoms, edges), BF16)],
        flops=4 * 10**9,
    )
    centre, ghost = call(
        back_one_kernel,
        [shape((8, atoms)), shape((8, atoms))],
        [
            sent,
            come,
            g_ghost,
            sel,
            sel_ghost,
            geom,
            far_geom,
            edge,
            pre,
            far_pre,
            b_all,
            far_b,
            mix_one,
            vec_mix,
            gpos,
        ],
        scratch=[pltpu.VMEM((48, edges), BF16), pltpu.VMEM((48, edges), BF16)],
        flops=10**9,
    )
    near_p = swap_near(ghost)
    odd = lax.rem(lax.axis_index("space"), 2) == 1
    low = lax.broadcasted_iota(jnp.int32, (3, atoms), 1) < HALF
    back = jnp.where(low == odd, near_p[:3], 0.0)
    return (energy[0], -(centre[:3] + back))


def solution(mesh):
    placed = (
        P(None, "space"),
        P("space"),
        P(None, "space"),
        P("space"),
        P(None, "space"),
        P(),
        P(),
        P(),
        P(),
        P(),
        P(),
        P(),
        P(),
    )
    return jax.shard_map(
        body, mesh=mesh, in_specs=placed, out_specs=(P("space"), P(None, "space")), check_vma=False
    )
```

time: 42 us -> 40 us (0.952)
  Pallas kernels: 19.5 us -> 17.8 us
  waiting for transfers between devices: 10.9 us -> 9.94 us
  starting transfers between devices: 9.97 us -> 10.7 us
    pallas_call x9, Pallas kernels: 19.5 us -> 17.8 us  [call(): pl.pallas_call(kernel, out_shape=out_shapes, in_specs=[pl.BlockSpec(memor...]
    ppermute x2, waiting for transfers between devices: 8.79 us -> 7.46 us  [swap_far(): return lax.ppermute(x, 'space', far_route)]
    ppermute x2, starting transfers between devices: 8.68 us -> 9.27 us  [swap_far(): return lax.ppermute(x, 'space', far_route)]
  transfers between devices with their start and end apart: 6 -> 6, of which waited for: 4 -> 5; matrix products, arithmetic and copies ran while one was open for 0% -> 0% of each run, Pallas kernels for 20% -> 20%
where the time goes in v5:
time: 40 us; the launch traced here: 39.7 us
  Pallas kernels  17.8 us (44%)
  starting transfers between devices  10.7 us (27%)
  waiting for transfers between devices  9.94 us (25%)
  between operations  0.72 us (2%)
  other arithmetic  0.6 us (2%)
    pallas_call x9, Pallas kernels, call(): pl.pallas_call(kernel, out_shape=out_shapes, in_specs=[pl.BlockSpec(memor...  17.8 us
    ppermute x2, starting transfers between devices, swap_far(): return lax.ppermute(x, 'space', far_route)  9.27 us
    ppermute x2, waiting for transfers between devices, swap_far(): return lax.ppermute(x, 'space', far_route)  7.46 us
    ppermute x4, waiting for transfers between devices, swap_near(): return lax.ppermute(x, 'space', near_route)  2.47 us
    ppermute x4, starting transfers between devices, swap_near(): return lax.ppermute(x, 'space', near_route)  1.45 us
  transfers between devices with their start and end apart: 6, of which 5 were waited for; matrix products, arithmetic and copies ran while one was open for 0% of the time, Pallas kernels for 20%

profile of v5, /device:TPU:127, one launch (start us, length us, event | category | flops | bytes accessed | tf_op | source)
XLA Modules:
  0.0 39.7 jit_solution(13523676751902704827)
XLA Ops:
  0.6 0.8 %shard_map.140 = (f32[4,128]{1,0:T(4,128)S(1)}, s32[24,128]{1,0:T(8,128)S(1)}, s32[2,64]{1,0:T(2,128)S(1)}, s32[1,128]{1,0:T(1,128)S(1)}) custom-call(f32[3,128]{1,0:T(4,128)} %pos_hbm.1, s32[1,128]{1,0:T(1,128)} %bitcast.3, s32[24,128]{1,0:T(8,128)} %nb_hbm.1, s32[2,64]{1,0:T(2,128)} %gi_hbm.1, s32[1,128]{1,0:T(1,128)} %bitcast.4), custom_call_target="tpu_custom_call" | custom-call | bytes 30720 | tf_op jit(solution)/shard_map/pallas_call | solution.py:705
  1.4 0.8 %collective-permute-start = (f32[4,128]{1,0:T(4,128)S(1)}, f32[4,128]{1,0:T(4,128)S(1)}, u32[]{:S(2)}, u32[]{:S(2)}) collective-permute-start(f32[4,128]{1,0:T(4,128)S(1)} %get-tuple-element.40.own_ref), channel_id=1, source_target_pairs={{0,1},{1,0},{2,3},{3,2},{4,5},{5,4},{6,7},{7,6},{8,9},{9,8},{10,11... | collective-permute-start | bytes 6152 | tf_op jit(solution)/shard_map/ppermute | solution.py:748
  2.2 0.4 shard_map.141.edges_ref
  2.6 0.4 %collective-permute-done.near_ref = f32[4,128]{1,0:T(4,128)S(1)} collective-permute-done((f32[4,128]{1,0:T(4,128)S(1)}, f32[4,128]{1,0:T(4,128)S(1)}, u32[]{:S(2)}, u32[]{:S(2)}) %collective-permute-start) | collective-permute-done | bytes 2080 | tf_op jit(solution)/shard_map/ppermute | solution.py:748
  3.0 4.5 %collective-permute-start.1 = (f32[40,128]{1,0:T(8,128)S(1)}, f32[40,128]{1,0:T(8,128)S(1)}, u32[]{:S(2)}, u32[]{:S(2)}) collective-permute-start(f32[40,128]{1,0:T(8,128)S(1)} %pad_maximum_fusion), channel_id=1, source_target_pairs={{1,2},{2,1},{3,4},{4,3},{5,6},{6,5},{7,8},{8,7},{9,10},{10,9},{11,... | collective-permute-start | bytes 61448 | tf_op jit(solution)/shard_map/ppermute | solution.py:751
  7.6 1.7 %shard_map.142 = (bf16[256,3072]{1,0:T(8,128)(2,1)S(1)}, bf16[2,64,32]{2,1,0:T(8,128)(2,1)S(1)}, bf16[2,64,192]{2,1,0:T(8,128)(2,1)S(1)}, bf16[2,128,192]{2,1,0:...) custom-call(f32[2,8,64]{2,1,0:T(8,128)} %rin_hbm.1, ...), custom_call_target="tpu_custom_call" | custom-call | flops 100000000 | bytes 2048000 | tf_op jit(solution)/shard_map/pallas_call | solution.py:705
  9.3 4.2 %collective-permute-done.1.far_ref.there_ref = f32[40,128]{1,0:T(8,128)S(1)} collective-permute-done((f32[40,128]{1,0:T(8,128)S(1)}, f32[40,128]{1,0:T(8,128)S(1)}, u32[]{:S(2)}, u32[]{:S(2)}) %collective-permute-start.1) | collective-permute-done | bytes 20512 | tf_op jit(solution)/shard_map/ppermute | solution.py:751
  13.5 3.1 %shard_map.143 = (f32[256,128]{1,0:T(8,128)S(1)}, f32[256,128]{1,0:T(8,128)S(1)}, f32[128,128]{1,0:T(8,128)S(1)}, bf16[128,256]{1,0:T(8,128)(2,1)S(1)}, bf16[208...) custom-call(f32[4,128]{1,0:T(4,128)S(1)} %get-tuple-element.40.own_r, ...), custom_call_target="tpu_custom_call" | custom-call | flops 2000000000 | bytes 2762240 | tf_op jit(solution)/shard_map/pallas_call | solution.py:705
  16.6 0.1 collective-permute-start.2
  16.7 1.5 %shard_map.144 = (f32[128,3072]{1,0:T(8,128)S(1)}, f32[128,3072]{1,0:T(8,128)S(1)}) custom-call(f32[2,8,3072]{2,1,0:T(8,128)S(1)} %get-tuple-element.55.basis_ref, bf16[2,64,32]{2,1,0:T(8,128)(2,1)S(1)} %get-tuple-element.46.win_ref, bf16[2,64,192]{2,1,0:T(8,128)(2,1)S(1)} %get-tuple-element.47.wmid_ref, bf16[2,128,192]{2,1,0:T(8,128)(2,1)S(1)} %get-tuple-element.48.wout_ref), custom_call_target="tpu_custom_call" | custom-call | flops 2000000000 | bytes 3497984 | tf_op jit(solution)/shard_map/pallas_call | solution.py:705
  18.2 0.0 collective-permute-done.2.near_ref
  18.3 3.6 %shard_map.145 = (f32[1,128]{1,0:T(1,128)}, f32[256,128]{1,0:T(8,128)S(1)}, f32[256,128]{1,0:T(8,128)S(1)}, f32[128,128]{1,0:T(8,128)S(1)}, f32[128,128]{1,0:T(8...) custom-call(f32[256,128]{1,0:T(8,128)S(1)} %get-tuple-element.51.feats_ref, ...), custom_call_target="tpu_custom_call" | custom-call | flops 1000000000 | bytes 5579776 | tf_op jit(solution)/shard_map/pallas_call | solution.py:705
  21.9 0.5 %collective-permute-start.3 = (f32[128,128]{1,0:T(8,128)S(1)}, f32[128,128]{1,0:T(8,128)S(1)}, u32[]{:S(2)}, u32[]{:S(2)}) collective-permute-start(f32[128,128]{1,0:T(8,128)S(1)} %get-tuple-element.62), channel_id=1, source_target_pairs={{0,1},{1,0},{2,3},{3,2},{4,5},{5,4},{6,7},{7,6},{8,9},{9,8},{10,11... | collective-permute-start | bytes 196616 | tf_op jit(solution)/shard_map/ppermute | solution.py:748
  22.4 0.9 %collective-permute-done.3.near_ref = f32[128,128]{1,0:T(8,128)S(1)} collective-permute-done((f32[128,128]{1,0:T(8,128)S(1)}, f32[128,128]{1,0:T(8,128)S(1)}, u32[]{:S(2)}, u32[]{:S(2)}) %collective-permute-start.3) | collective-permute-done | bytes 65568 | tf_op jit(solution)/shard_map/ppermute | solution.py:748
  23.3 0.1 shard_map.146.sent_ref
  23.4 4.7 %collective-permute-start.4 = (f32[392,128]{1,0:T(8,128)S(1)}, f32[392,128]{1,0:T(8,128)S(1)}, u32[]{:S(2)}, u32[]{:S(2)}) collective-permute-start(f32[392,128]{1,0:T(8,128)S(1)} %shard_map.146.sent_ref), channel_id=1, source_target_pairs={{1,2},{2,1},{3,4},{4,3},{5,6},{6,5},{7,8},{8,7},{9,10},{10,9},{11,... | collective-permute-start | bytes 602120 | tf_op jit(solution)/shard_map/ppermute | solution.py:751
  28.1 4.5 %shard_map.147 = (f32[2,192,3072]{2,1,0:T(8,128)S(1)}, bf16[128,3072]{1,0:T(8,128)(2,1)S(1)}, f32[8,3072]{1,0:T(8,128)S(1)}, f32[64,128]{1,0:T(8,128)S(1)}, f32[64,384]{1,0:T(8,128)S(1)}) custom-call(f32[2,8,3072]{2,1,0:T(8,128)S(1)} %get-tuple-element.55.basis_ref, bf16[128,256]{1,0:T(8,128)(2,1)S(1)} %get-tuple-element.66.htab_ref, ...), custom_call_target="tpu_custom_call" | custom-call | flops 4000000000 | bytes 7902720 | tf_op jit(solution)/shard_map/pallas_call | solution.py:705
  32.6 3.2 %collective-permute-done.4.far_ref = f32[392,128]{1,0:T(8,128)S(1)} collective-permute-done((f32[392,128]{1,0:T(8,128)S(1)}, f32[392,128]{1,0:T(8,128)S(1)}, u32[]{:S(2)}, u32[]{:S(2)}) %collective-permute-start.4) | collective-permute-done | bytes 200736 | tf_op jit(solution)/shard_map/ppermute | solution.py:751
  35.8 2.1 %shard_map.148 = (f32[8,128]{1,0:T(8,128)S(1)}, f32[8,128]{1,0:T(8,128)S(1)}) custom-call(f32[392,128]{1,0:T(8,128)S(1)} %shard_map.146.sent_ref, f32[392,128]{1,0:T(8,128)S(1)} %collective-permute-done.4.far_ref, f32[256,128]{1,0:T(8,128)S(1)} %get-tuple-element.65.gghost_ref, bf16[256,3072]{1,0:T(8,128)(2,1)S(1)} %get-tuple-element.44.sel_ref, ...), custom_call_target="tpu_custom_call" | custom-call | flops 1000000000 | bytes 8146944 | tf_op jit(solution)/shard_map/pallas_call | solution.py:705
  37.9 0.1 collective-permute-start.5
  38.0 1.1 %collective-permute-done.5 = f32[8,128]{1,0:T(8,128)S(1)} collective-permute-done((f32[8,128]{1,0:T(8,128)S(1)}, f32[8,128]{1,0:T(8,128)S(1)}, u32[]{:S(2)}, u32[]{:S(2)}) %collective-permute-start.5) | collective-permute-done | bytes 4128 | tf_op jit(solution)/shard_map/ppermute | solution.py:748
  39.2 0.6 %add_negate_fusion = f32[3,128]{1,0:T(4,128)} fusion(f32[8,128]{1,0:T(8,128)S(1)} %collective-permute-done.5, f32[8,128]{1,0:T(8,128)S(1)} %get-tuple-element.76, pred[128]{0:T(512)(128)(4,1)S(1)} %compare_compare_fusion), kind=kLoop, calls=%fused_computation.1 | loop fusion | flops 1152 | bytes 4736 | tf_op jit(solution)/shard_map/neg | solution.py:882
  (2 shorter events, 0.0 us)
Async XLA Ops:
  1.4 1.6 %collective-permute-start = (f32[4,128]{1,0:T(4,128)S(1)}, f32[4,128]{1,0:T(4,128)S(1)}, u32[]{:S(2)}, u32[]{:S(2)}) collective-permute-start(f32[4,128]{1,0:T(4,128)S(1)} %get-tuple-element.40.own_ref), channel_id=1, source_target_pairs={{0,1},{1,0},{2,3},{3,2},{4,5},{5,4},{6,7},{7,6},{8,9},{9,8},{10,11... | collective-permute-start | bytes 6152 | tf_op jit(solution)/shard_map/ppermute | solution.py:748
  3.0 10.5 %collective-permute-start.1 = (f32[40,128]{1,0:T(8,128)S(1)}, f32[40,128]{1,0:T(8,128)S(1)}, u32[]{:S(2)}, u32[]{:S(2)}) collective-permute-start(f32[40,128]{1,0:T(8,128)S(1)} %pad_maximum_fusion), channel_id=1, source_target_pairs={{1,2},{2,1},{3,4},{4,3},{5,6},{6,5},{7,8},{8,7},{9,10},{10,9},{11,... | collective-permute-start | bytes 61448 | tf_op jit(solution)/shard_map/ppermute | solution.py:751
  16.6 1.6 %collective-permute-start.2 = (f32[128,128]{1,0:T(8,128)S(1)}, f32[128,128]{1,0:T(8,128)S(1)}, u32[]{:S(2)}, u32[]{:S(2)}) collective-permute-start(f32[128,128]{1,0:T(8,128)S(1)} %get-tuple-element.53), channel_id=1, source_target_pairs={{0,1},{1,0},{2,3},{3,2},{4,5},{5,4},{6,7},{7,6},{8,9},{9,8},{10,11... | collective-permute-start | bytes 196616 | tf_op jit(solution)/shard_map/ppermute | solution.py:748
  21.9 1.4 %collective-permute-start.3 = (f32[128,128]{1,0:T(8,128)S(1)}, f32[128,128]{1,0:T(8,128)S(1)}, u32[]{:S(2)}, u32[]{:S(2)}) collective-permute-start(f32[128,128]{1,0:T(8,128)S(1)} %get-tuple-element.62), channel_id=1, source_target_pairs={{0,1},{1,0},{2,3},{3,2},{4,5},{5,4},{6,7},{7,6},{8,9},{9,8},{10,11... | collective-permute-start | bytes 196616 | tf_op jit(solution)/shard_map/ppermute | solution.py:748
  23.4 12.5 %collective-permute-start.4 = (f32[392,128]{1,0:T(8,128)S(1)}, f32[392,128]{1,0:T(8,128)S(1)}, u32[]{:S(2)}, u32[]{:S(2)}) collective-permute-start(f32[392,128]{1,0:T(8,128)S(1)} %shard_map.146.sent_ref), channel_id=1, source_target_pairs={{1,2},{2,1},{3,4},{4,3},{5,6},{6,5},{7,8},{8,7},{9,10},{10,9},{11,... | collective-permute-start | bytes 602120 | tf_op jit(solution)/shard_map/ppermute | solution.py:751
  37.9 1.3 %collective-permute-start.5 = (f32[8,128]{1,0:T(8,128)S(1)}, f32[8,128]{1,0:T(8,128)S(1)}, u32[]{:S(2)}, u32[]{:S(2)}) collective-permute-start(f32[8,128]{1,0:T(8,128)S(1)} %get-tuple-element.77), channel_id=1, source_target_pairs={{0,1},{1,0},{2,3},{3,2},{4,5},{5,4},{6,7},{7,6},{8,9},{9,8},{10,11... | collective-permute-start | bytes 12296 | tf_op jit(solution)/shard_map/ppermute | solution.py:748

commit v6 on v5

--- a/solution.py
+++ b/solution.py
@@ -80,24 +80,7 @@
         c.wait()
 
 
-def pack_kernel(
-    pos_hbm, kind_hbm, nb_hbm, gi_hbm, counts_hbm, own_ref, nb_ref, gi_ref, counts_ref, pos_ref, kind_ref, sems
-):
-    copy_in(
-        [
-            (pos_hbm, pos_ref),
-            (kind_hbm, kind_ref),
-            (nb_hbm, nb_ref),
-            (gi_hbm, gi_ref),
-            (counts_hbm, counts_ref),
-        ],
-        sems,
-    )
-    own_ref[0:3, :] = pos_ref[...]
-    own_ref[3:4, :] = (kind_ref[...] + 1).astype(F32)
-
-
-def remap_kernel(nb_ref, gi_ref, counts_ref, out_ref, hot_ref):
+def put_lists(nb_ref, gi_ref, counts_ref, out_ref, hot_ref):
     slots, atoms = nb_ref.shape
     rows = lax.broadcasted_iota(jnp.int32, (atoms, atoms), 0) + atoms
     for k in range(slots):
@@ -125,6 +108,11 @@
 
 
 def prep_kernel(
+    pos_hbm,
+    kind_hbm,
+    nb_hbm,
+    gi_hbm,
+    counts_hbm,
     rin_hbm,
     rmid_hbm,
     rout_hbm,
@@ -133,6 +121,7 @@
     vec_hbm,
     mix_two_hbm,
     read_hbm,
+    own_ref,
     edges_ref,
     sel_ref,
     win_ref,
@@ -143,13 +132,24 @@
     vec_ref,
     mix_two_ref,
     read_ref,
+    pos_ref,
+    kind_ref,
+    nb_ref,
+    gi_ref,
+    counts_ref,
     rin_ref,
     rmid_ref,
     rout_ref,
+    hot_ref,
     sems,
 ):
     copy_in(
         [
+            (pos_hbm, pos_ref),
+            (kind_hbm, kind_ref),
+            (nb_hbm, nb_ref),
+            (gi_hbm, gi_ref),
+            (counts_hbm, counts_ref),
             (rin_hbm, rin_ref),
             (rmid_hbm, rmid_ref),
             (rout_hbm, rout_ref),
@@ -161,7 +161,10 @@
         ],
         sems,
     )
-    build_selector(edges_ref[0 : sel_ref.shape[1] // edges_ref.shape[1], :], sel_ref)
+    own_ref[0:3, :] = pos_ref[...]
+    own_ref[3:4, :] = (kind_ref[...] + 1).astype(F32)
+    put_lists(nb_ref, gi_ref, counts_ref, edges_ref, hot_ref)
+    build_selector(edges_ref[0 : nb_ref.shape[0], :], sel_ref)
     for layer in range(2):
         w = rin_ref[layer]
         h = high(w)
@@ -315,10 +318,8 @@
 
 
 def layer_one_kernel(
-    own_ref,
-    near_ref,
-    edges_ref,
-    far_ref,
+    sent_ref,
+    come_ref,
     sel_ref,
     embed_ref,
     win_ref,
@@ -335,18 +336,24 @@
     basis_ref,
     pre_ref,
     b_ref,
+    there_ref,
     sel_far_ref,
     tab_ref,
 ):
-    atoms = own_ref.shape[1]
+    atoms = sent_ref.shape[1]
     slots = sel_ref.shape[1] // atoms
     tiles = slots // 2
     width = embed_ref.shape[1]
     embed = embed_ref[...]
     scale = 1.0 / jnp.sqrt(F32(slots))
     ours = far_lanes(4)
-    own = own_ref[...]
-    there = far_ref[...]
+    own = sent_ref[0:4]
+    near = sent_ref[4:8]
+    me = jnp.full(sent_ref.shape, lax.axis_index("space"), jnp.int32)
+    has = jnp.logical_and(me > 0, me < lax.axis_size("space") - 1)
+    there = jnp.where(parity_odd(sent_ref.shape[0]), come_ref[1], come_ref[0])
+    there = jnp.where(has, there, jnp.zeros(sent_ref.shape, F32))
+    there_ref[...] = there
     low12 = lane_low(tiles)
     lists = there[8 : 8 + slots]
     first = lists[:tiles]
@@ -361,7 +368,7 @@
         sel_far_ref,
     )
     h0 = make_table(
-        jnp.concatenate([own, jnp.where(ours, there[0:4], near_ref[...])], axis=1), embed, tab_ref
+        jnp.concatenate([own, jnp.where(ours, there[0:4], near)], axis=1), embed, tab_ref
     )
     h0_far = make_table(
         jnp.concatenate([there[0:4], jnp.where(ours, there[4:8], own)], axis=1), embed, ftab_ref
@@ -371,7 +378,7 @@
     gf = bdot(ftab_ref[...], sel_far_ref[...])
 
     far, h_far = gathered(g, width)
-    counts = spread_rows(edges_ref[slots : slots + 1, :], 8)
+    counts = spread_rows(sent_ref[8 + slots : 9 + slots, :], 8)
     unit, inv, b, db = edge_geometry(far, own, counts, slots)
     for i, x in enumerate(unit + [inv]):
         geom_ref[i : i + 1, :] = x[0:1]
@@ -756,43 +763,35 @@
     def shapes_of(args):
         return [shape(x.shape, x.dtype) for x in args]
 
-    atom_rows = [positions, species[None]]
-    lists = [neighbours, ghost_index, counts[None]]
-    own, *lists = call(
-        pack_kernel,
-        [shape((4, atoms))] + shapes_of(lists),
-        atom_rows + lists,
-        scratch=scratch_of(atom_rows) + [pltpu.SemaphoreType.DMA((5,))],
-        far_away=5,
-    )
-    near = swap_near(own)
-    (edge_rows,) = call(
-        remap_kernel,
-        [shape((slots + 8, atoms))],
-        lists,
-        scratch=[pltpu.VMEM((atoms, edges), BF16)],
-        flops=10**8,
-    )
-    there = swap_far(jnp.concatenate([own, near, edge_rows], axis=0))
+    near_pos = swap_near(positions)
+    near_kind = swap_near(species)
+    local = [positions, species[None], neighbours, ghost_index, counts[None]]
     weights = [radial_in, radial_mid, radial_out]
     passed = [embed, mix_one, vec_mix, mix_two, readout]
-    moved = weights + passed
-    sel, win, wmid, wout, embed, mix_one, vec_mix, mix_two, readout = call(
+    moved = local + weights + passed
+    own, edge_rows, sel, win, wmid, wout, embed, mix_one, vec_mix, mix_two, readout = call(
         prep_kernel,
         [
+            shape((4, atoms)),
+            shape((slots + 8, atoms)),
             shape((2 * atoms, edges), BF16),
             shape((2, hidden, 4 * nbasis), BF16),
             shape((2, hidden, 3 * hidden), BF16),
             shape((2, 2 * width, 3 * hidden), BF16),
         ]
         + shapes_of(passed),
-        moved + [edge_rows],
-        scratch=scratch_of(weights) + [pltpu.SemaphoreType.DMA((len(moved),))],
+        moved,
+        scratch=scratch_of(local + weights)
+        + [pltpu.VMEM((atoms, edges), BF16), pltpu.SemaphoreType.DMA((len(moved),))],
         flops=10**8,
         far_away=len(moved),
     )
+    near_rows = [near_pos, (near_kind + 1).astype(F32)[None]]
+    sent = jnp.concatenate([own] + near_rows + [edge_rows], axis=0)
+    pairs = [[i, (i + 1) % devices] for i in range(1, devices, 2)]
+    come = lax.all_gather(sent, "space", axis_index_groups=pairs)
     table_rows = 2 * width + 80
-    feats, far_feats, near_f, htab, ftab, geom, basis, pre, b_all = call(
+    feats, far_feats, near_f, htab, ftab, geom, basis, pre, b_all, there = call(
         layer_one_kernel,
         [
             shape((4 * width, atoms)),
@@ -804,8 +803,9 @@
             shape((2, nbasis, edges)),
             shape((width, atoms)),
             shape((width, 3 * atoms)),
+            shape((slots + 16, atoms)),
         ],
-        [own, near, edge_rows, there, sel, embed, win, wmid, wout, mix_one, vec_mix],
+        [sent, come, sel, embed, win, wmid, wout, mix_one, vec_mix],
         scratch=[
             pltpu.VMEM((2 * atoms, edges // 2), BF16),
             pltpu.VMEM((table_rows, 2 * atoms), BF16),

time: 40 us -> 39.3 us (0.982)
  blocking collectives: 0 us -> 9.31 us
  waiting for transfers between devices: 9.94 us -> 5.15 us
  starting transfers between devices: 10.7 us -> 6.34 us
  Pallas kernels: 17.8 us -> 16.9 us
    all_gather x0 -> x1, blocking collectives: none -> 9.31 us  [body(): come = lax.all_gather(sent, 'space', axis_index_groups=pairs)]
    ppermute x2 -> x1, starting transfers between devices: 9.27 us -> 4.81 us  [swap_far(): return lax.ppermute(x, 'space', far_route)]
    ppermute x2 -> x1, waiting for transfers between devices: 7.46 us -> 3.1 us  [swap_far(): return lax.ppermute(x, 'space', far_route)]
    pallas_call x9 -> x7, Pallas kernels: 17.8 us -> 16.9 us  [call(): pl.pallas_call(kernel, out_shape=out_shapes, in_specs=[pl.BlockSpec(memor...]
    ppermute x4 -> x5, waiting for transfers between devices: 2.47 us -> 2.05 us  [swap_near(): return lax.ppermute(x, 'space', near_route)]
    ppermute x4 -> x5, starting transfers between devices: 1.45 us -> 1.54 us  [swap_near(): return lax.ppermute(x, 'space', near_route)]
  transfers between devices with their start and end apart: 6 -> 6, of which waited for: 5 -> 3; matrix products, arithmetic and copies ran while one was open for 0% -> 0% of each run, Pallas kernels for 20% -> 21%
where the time goes in v6:
time: 39.3 us; the launch traced here: 39.1 us
  Pallas kernels  16.9 us (43%)
  blocking collectives  9.31 us (24%)
  starting transfers between devices  6.34 us (16%)
  waiting for transfers between devices  5.15 us (13%)
  between operations  0.74 us (2%)
  other arithmetic  0.61 us (2%)
    pallas_call x7, Pallas kernels, call(): pl.pallas_call(kernel, out_shape=out_shapes, in_specs=[pl.BlockSpec(memor...  16.9 us
    all_gather x1, blocking collectives, body(): come = lax.all_gather(sent, 'space', axis_index_groups=pairs)  9.31 us
    ppermute x1, starting transfers between devices, swap_far(): return lax.ppermute(x, 'space', far_route)  4.81 us
    ppermute x1, waiting for transfers between devices, swap_far(): return lax.ppermute(x, 'space', far_route)  3.1 us
    ppermute x5, waiting for transfers between devices, swap_near(): return lax.ppermute(x, 'space', near_route)  2.05 us
    ppermute x5, starting transfers between devices, swap_near(): return lax.ppermute(x, 'space', near_route)  1.54 us
  transfers between devices with their start and end apart: 6, of which 3 were waited for; matrix products, arithmetic and copies ran while one was open for 0% of the time, Pallas kernels for 21%

profile of v6, /device:TPU:127, one launch (start us, length us, event | category | flops | bytes accessed | tf_op | source)
XLA Modules:
  0.0 39.1 jit_solution(655728988088436014)
XLA Ops:
  0.6 0.8 %collective-permute-start.1 = (s32[128]{0:T(128)}, s32[128]{0:T(128)S(1)}, u32[]{:S(2)}, u32[]{:S(2)}) collective-permute-start(s32[128]{0:T(128)} %param.14), channel_id=1, source_target_pairs={{0,1},{1,0},{2,3},{3,2},{4,5},{5,4},{6,7},{7,6},{8,9},{9,8},{10,11... | collective-permute-start | bytes 1544 | tf_op jit(solution)/shard_map/ppermute | solution.py:755
  1.4 0.1 collective-permute-start
  1.5 2.0 %shard_map.140 = (f32[4,128]{1,0:T(4,128)S(1)}, f32[32,128]{1,0:T(8,128)S(1)}, bf16[256,3072]{1,0:T(8,128)(2,1)S(1)}, bf16[2,64,32]{2,1,0:T(8,128)(2,1)S(1)}, bf...) custom-call(f32[3,128]{1,0:T(4,128)} %pos_hbm.1, ...), custom_call_target="tpu_custom_call" | custom-call | flops 100000000 | bytes 2065408 | tf_op jit(solution)/shard_map/pallas_call | solution.py:712
  3.5 0.0 collective-permute-done.1
  3.5 0.0 collective-permute-done
  3.6 9.3 %all-gather = f32[80,128]{1,0:T(8,128)S(1)} all-gather(f32[40,128]{1,0:T(8,128)S(1)} %pad_maximum_fusion.sent_ref), channel_id=2, replica_groups={{1,2},{3,4},{5,6},{7,8},{9,10},{11,12},{13,14},{15,16},{17,18},{19,20},..., dimensions={0}, use_global_device_ids=true | all-gather | bytes 61440 | tf_op jit(solution)/shard_map/all_gather | solution.py:792
  12.9 3.1 %shard_map.141 = (f32[256,128]{1,0:T(8,128)S(1)}, f32[256,128]{1,0:T(8,128)S(1)}, f32[128,128]{1,0:T(8,128)S(1)}, bf16[128,256]{1,0:T(8,128)(2,1)S(1)}, bf16[208...) custom-call(f32[40,128]{1,0:T(8,128)S(1)} %pad_maximum_fusion.sent_r, ...), custom_call_target="tpu_custom_call" | custom-call | flops 2000000000 | bytes 2803200 | tf_op jit(solution)/shard_map/pallas_call | solution.py:712
  16.0 0.1 collective-permute-start.2
  16.1 1.5 %shard_map.142 = (f32[128,3072]{1,0:T(8,128)S(1)}, f32[128,3072]{1,0:T(8,128)S(1)}) custom-call(f32[2,8,3072]{2,1,0:T(8,128)S(1)} %get-tuple-element.52.basis_ref, bf16[2,64,32]{2,1,0:T(8,128)(2,1)S(1)} %get-tuple-element.43.win_ref, bf16[2,64,192]{2,1,0:T(8,128)(2,1)S(1)} %get-tuple-element.44.wmid_ref, bf16[2,128,192]{2,1,0:T(8,128)(2,1)S(1)} %get-tuple-element.45.wout_ref), custom_call_target="tpu_custom_call" | custom-call | flops 2000000000 | bytes 3497984 | tf_op jit(solution)/shard_map/pallas_call | solution.py:712
  17.6 0.0 collective-permute-done.2.near_ref
  17.6 3.6 %shard_map.143 = (f32[1,128]{1,0:T(1,128)}, f32[256,128]{1,0:T(8,128)S(1)}, f32[256,128]{1,0:T(8,128)S(1)}, f32[128,128]{1,0:T(8,128)S(1)}, f32[128,128]{1,0:T(8...) custom-call(f32[256,128]{1,0:T(8,128)S(1)} %get-tuple-element.48.feats_ref, ...), custom_call_target="tpu_custom_call" | custom-call | flops 1000000000 | bytes 5579776 | tf_op jit(solution)/shard_map/pallas_call | solution.py:712
  21.2 0.5 %collective-permute-start.3 = (f32[128,128]{1,0:T(8,128)S(1)}, f32[128,128]{1,0:T(8,128)S(1)}, u32[]{:S(2)}, u32[]{:S(2)}) collective-permute-start(f32[128,128]{1,0:T(8,128)S(1)} %get-tuple-element.59), channel_id=1, source_target_pairs={{0,1},{1,0},{2,3},{3,2},{4,5},{5,4},{6,7},{7,6},{8,9},{9,8},{10,11... | collective-permute-start | bytes 196616 | tf_op jit(solution)/shard_map/ppermute | solution.py:755
  21.7 0.9 %collective-permute-done.3.near_ref = f32[128,128]{1,0:T(8,128)S(1)} collective-permute-done((f32[128,128]{1,0:T(8,128)S(1)}, f32[128,128]{1,0:T(8,128)S(1)}, u32[]{:S(2)}, u32[]{:S(2)}) %collective-permute-start.3) | collective-permute-done | bytes 65568 | tf_op jit(solution)/shard_map/ppermute | solution.py:755
  22.6 0.1 shard_map.144.sent_ref
  22.7 4.8 %collective-permute-start.4 = (f32[392,128]{1,0:T(8,128)S(1)}, f32[392,128]{1,0:T(8,128)S(1)}, u32[]{:S(2)}, u32[]{:S(2)}) collective-permute-start(f32[392,128]{1,0:T(8,128)S(1)} %shard_map.144.sent_ref), channel_id=1, source_target_pairs={{1,2},{2,1},{3,4},{4,3},{5,6},{6,5},{7,8},{8,7},{9,10},{10,9},{11,... | collective-permute-start | bytes 602120 | tf_op jit(solution)/shard_map/ppermute | solution.py:758
  27.5 4.5 %shard_map.145 = (f32[2,192,3072]{2,1,0:T(8,128)S(1)}, bf16[128,3072]{1,0:T(8,128)(2,1)S(1)}, f32[8,3072]{1,0:T(8,128)S(1)}, f32[64,128]{1,0:T(8,128)S(1)}, f32[64,384]{1,0:T(8,128)S(1)}) custom-call(f32[2,8,3072]{2,1,0:T(8,128)S(1)} %get-tuple-element.52.basis_ref, bf16[128,256]{1,0:T(8,128)(2,1)S(1)} %get-tuple-element.63.htab_ref, ...), custom_call_target="tpu_custom_call" | custom-call | flops 4000000000 | bytes 7902720 | tf_op jit(solution)/shard_map/pallas_call | solution.py:712
  32.1 3.1 %collective-permute-done.4.far_ref = f32[392,128]{1,0:T(8,128)S(1)} collective-permute-done((f32[392,128]{1,0:T(8,128)S(1)}, f32[392,128]{1,0:T(8,128)S(1)}, u32[]{:S(2)}, u32[]{:S(2)}) %collective-permute-start.4) | collective-permute-done | bytes 200736 | tf_op jit(solution)/shard_map/ppermute | solution.py:758
  35.2 2.1 %shard_map.146 = (f32[8,128]{1,0:T(8,128)S(1)}, f32[8,128]{1,0:T(8,128)S(1)}) custom-call(f32[392,128]{1,0:T(8,128)S(1)} %shard_map.144.sent_ref, f32[392,128]{1,0:T(8,128)S(1)} %collective-permute-done.4.far_ref, f32[256,128]{1,0:T(8,128)S(1)} %get-tuple-element.62.gghost_ref, bf16[256,3072]{1,0:T(8,128)(2,1)S(1)} %get-tuple-element.41.sel_ref, ...), custom_call_target="tpu_custom_call" | custom-call | flops 1000000000 | bytes 8146944 | tf_op jit(solution)/shard_map/pallas_call | solution.py:712
  37.2 0.1 collective-permute-start.5
  37.4 1.1 %collective-permute-done.5 = f32[8,128]{1,0:T(8,128)S(1)} collective-permute-done((f32[8,128]{1,0:T(8,128)S(1)}, f32[8,128]{1,0:T(8,128)S(1)}, u32[]{:S(2)}, u32[]{:S(2)}) %collective-permute-start.5) | collective-permute-done | bytes 4128 | tf_op jit(solution)/shard_map/ppermute | solution.py:755
  38.5 0.6 %add_negate_fusion = f32[3,128]{1,0:T(4,128)} fusion(f32[8,128]{1,0:T(8,128)S(1)} %collective-permute-done.5, f32[8,128]{1,0:T(8,128)S(1)} %get-tuple-element.74, pred[128]{0:T(512)(128)(4,1)S(1)} %compare_compare_fusion), kind=kLoop, calls=%fused_computation.1 | loop fusion | flops 1152 | bytes 4736 | tf_op jit(solution)/shard_map/neg | solution.py:882
  (3 shorter events, 0.0 us)
Async XLA Ops:
  0.6 2.9 %collective-permute-start.1 = (s32[128]{0:T(128)}, s32[128]{0:T(128)S(1)}, u32[]{:S(2)}, u32[]{:S(2)}) collective-permute-start(s32[128]{0:T(128)} %param.14), channel_id=1, source_target_pairs={{0,1},{1,0},{2,3},{3,2},{4,5},{5,4},{6,7},{7,6},{8,9},{9,8},{10,11... | collective-permute-start | bytes 1544 | tf_op jit(solution)/shard_map/ppermute | solution.py:755
  1.4 2.1 %collective-permute-start = (f32[3,128]{1,0:T(4,128)}, f32[3,128]{1,0:T(4,128)S(1)}, u32[]{:S(2)}, u32[]{:S(2)}) collective-permute-start(f32[3,128]{1,0:T(4,128)} %pos_hbm.1), channel_id=1, source_target_pairs={{0,1},{1,0},{2,3},{3,2},{4,5},{5,4},{6,7},{7,6},{8,9},{9,8},{10,11... | collective-permute-start | bytes 4616 | tf_op jit(solution)/shard_map/ppermute | solution.py:755
  16.0 1.6 %collective-permute-start.2 = (f32[128,128]{1,0:T(8,128)S(1)}, f32[128,128]{1,0:T(8,128)S(1)}, u32[]{:S(2)}, u32[]{:S(2)}) collective-permute-start(f32[128,128]{1,0:T(8,128)S(1)} %get-tuple-element.50), channel_id=1, source_target_pairs={{0,1},{1,0},{2,3},{3,2},{4,5},{5,4},{6,7},{7,6},{8,9},{9,8},{10,11... | collective-permute-start | bytes 196616 | tf_op jit(solution)/shard_map/ppermute | solution.py:755
  21.2 1.4 %collective-permute-start.3 = (f32[128,128]{1,0:T(8,128)S(1)}, f32[128,128]{1,0:T(8,128)S(1)}, u32[]{:S(2)}, u32[]{:S(2)}) collective-permute-start(f32[128,128]{1,0:T(8,128)S(1)} %get-tuple-element.59), channel_id=1, source_target_pairs={{0,1},{1,0},{2,3},{3,2},{4,5},{5,4},{6,7},{7,6},{8,9},{9,8},{10,11... | collective-permute-start | bytes 196616 | tf_op jit(solution)/shard_map/ppermute | solution.py:755
  22.7 12.5 %collective-permute-start.4 = (f32[392,128]{1,0:T(8,128)S(1)}, f32[392,128]{1,0:T(8,128)S(1)}, u32[]{:S(2)}, u32[]{:S(2)}) collective-permute-start(f32[392,128]{1,0:T(8,128)S(1)} %shard_map.144.sent_ref), channel_id=1, source_target_pairs={{1,2},{2,1},{3,4},{4,3},{5,6},{6,5},{7,8},{8,7},{9,10},{10,9},{11,... | collective-permute-start | bytes 602120 | tf_op jit(solution)/shard_map/ppermute | solution.py:758
  37.2 1.3 %collective-permute-start.5 = (f32[8,128]{1,0:T(8,128)S(1)}, f32[8,128]{1,0:T(8,128)S(1)}, u32[]{:S(2)}, u32[]{:S(2)}) collective-permute-start(f32[8,128]{1,0:T(8,128)S(1)} %get-tuple-element.75), channel_id=1, source_target_pairs={{0,1},{1,0},{2,3},{3,2},{4,5},{5,4},{6,7},{7,6},{8,9},{9,8},{10,11... | collective-permute-start | bytes 12296 | tf_op jit(solution)/shard_map/ppermute | solution.py:755

commit v7 on v6

--- a/solution.py
+++ b/solution.py
@@ -82,10 +82,13 @@
 
 def put_lists(nb_ref, gi_ref, counts_ref, out_ref, hot_ref):
     slots, atoms = nb_ref.shape
-    rows = lax.broadcasted_iota(jnp.int32, (atoms, atoms), 0) + atoms
+    rows = (lax.broadcasted_iota(jnp.int32, (atoms, atoms), 0) + atoms).astype(F32).astype(BF16)
+    one = jnp.ones((atoms, atoms), BF16)
+    zero = jnp.zeros((atoms, atoms), BF16)
     for k in range(slots):
-        nb = jnp.broadcast_to(nb_ref[k : k + 1, :], (atoms, atoms))
-        hot_ref[:, slot(k)] = (rows == nb).astype(F32).astype(BF16)
+        nb = jnp.broadcast_to(nb_ref[k : k + 1, :].astype(F32), (16, atoms)).astype(BF16)
+        nb = jnp.concatenate([nb] * (atoms // 16), axis=0)
+        hot_ref[:, slot(k)] = jnp.where(rows == nb, one, zero)
     place = jnp.concatenate(
         [jnp.broadcast_to(gi_ref[i : i + 1, :], (16, HALF)).astype(F32) for i in range(2)], axis=1
     )
@@ -101,10 +104,13 @@
 
 def build_selector(rows_f32, sel_ref):
     count, atoms = rows_f32.shape
-    rows = lax.broadcasted_iota(jnp.int32, (2 * atoms, atoms), 0).astype(F32)
+    rows = lax.broadcasted_iota(jnp.int32, (2 * atoms, atoms), 0).astype(F32).astype(BF16)
+    one = jnp.ones((2 * atoms, atoms), BF16)
+    zero = jnp.zeros((2 * atoms, atoms), BF16)
     for k in range(count):
-        nb = jnp.broadcast_to(rows_f32[k : k + 1, :], (2 * atoms, atoms))
-        sel_ref[:, slot(k)] = (rows == nb).astype(F32).astype(BF16)
+        nb = jnp.broadcast_to(rows_f32[k : k + 1, :], (16, atoms)).astype(BF16)
+        nb = jnp.concatenate([nb] * (atoms // 8), axis=0)
+        sel_ref[:, slot(k)] = jnp.where(rows == nb, one, zero)
 
 
 def prep_kernel(
@@ -240,35 +246,43 @@
     return unit, inv, sin * f, sin * df + (n * (jnp.pi / RADIUS)) * cos * f
 
 
-def make_table(table, embed, tab_ref):
-    species, width = embed.shape
-    columns = table.shape[1]
+def kinds(row, species):
+    n = row.shape[1]
+    numbers = (lax.broadcasted_iota(jnp.int32, (8, n), 0) + 1).astype(F32)
+    return jnp.logical_and(spread_rows(row, 8) == numbers, numbers <= F32(species)).astype(F32)
+
+
+def make_table(table, species, tab_ref):
     parts = []
     for c in range(3):
-        p = jnp.broadcast_to(table[c : c + 1], (8, columns))
+        p = table[c : c + 1]
         h = high(p)
         m = high(p - h)
         parts += [h, m, p - h - m]
-    kind = jnp.broadcast_to(table[3:4], (species, columns))
-    onehot = (
-        kind == (lax.broadcasted_iota(jnp.int32, (species, columns), 0) + 1).astype(F32)
-    ).astype(F32)
-    h0 = hdot_t(embed, onehot)
-    h0_hi = high(h0)
-    zero = jnp.zeros((8, columns), F32)
-    tab_ref[...] = jnp.concatenate([h0_hi, h0 - h0_hi] + parts + [zero], axis=0).astype(BF16)
-    return h0
-
-
-def gathered(g, width):
-    base = 2 * width
-    far = [
-        g[base + 24 * c : base + 24 * c + 8]
-        + g[base + 24 * c + 8 : base + 24 * c + 16]
-        + g[base + 24 * c + 16 : base + 24 * c + 24]
+    pad = jnp.zeros((7, table.shape[1]), F32)
+    rows = parts + [pad, kinds(table[3:4], species), pad, pad[0:1]]
+    tab_ref[...] = jnp.concatenate(rows, axis=0).astype(BF16)
+
+
+def embed_rows(embed):
+    species, width = embed.shape
+    e = jnp.concatenate([embed, jnp.zeros((8 - species, width), F32)], axis=0)
+    h = high(e)
+    return jnp.concatenate([h, e - h], axis=0).T.astype(BF16)
+
+
+def far_kinds(g, emb):
+    hot = g[16:24]
+    return bdot(emb, jnp.concatenate([hot, hot], axis=0).astype(BF16))
+
+
+def far_positions(g):
+    return [
+        spread_rows(g[3 * c : 3 * c + 1], 8)
+        + spread_rows(g[3 * c + 1 : 3 * c + 2], 8)
+        + spread_rows(g[3 * c + 2 : 3 * c + 3], 8)
         for c in range(3)
     ]
-    return far, g[:width] + g[width:base]
 
 
 def edge_geometry(far, own, counts, tiles):
@@ -330,15 +344,15 @@
     feats_ref,
     far_feats_ref,
     near_out,
-    htab_ref,
+    tab_ref,
     ftab_ref,
+    emb_ref,
     geom_ref,
     basis_ref,
     pre_ref,
     b_ref,
     there_ref,
     sel_far_ref,
-    tab_ref,
 ):
     atoms = sent_ref.shape[1]
     slots = sel_ref.shape[1] // atoms
@@ -367,52 +381,79 @@
         ),
         sel_far_ref,
     )
-    h0 = make_table(
-        jnp.concatenate([own, jnp.where(ours, there[0:4], near)], axis=1), embed, tab_ref
-    )
-    h0_far = make_table(
-        jnp.concatenate([there[0:4], jnp.where(ours, there[4:8], own)], axis=1), embed, ftab_ref
-    )
-    htab_ref[...] = tab_ref[0 : 2 * width, :]
+    species = embed.shape[0]
+    make_table(
+        jnp.concatenate([own, jnp.where(ours, there[0:4], near)], axis=1), species, tab_ref
+    )
+    make_table(
+        jnp.concatenate([there[0:4], jnp.where(ours, there[4:8], own)], axis=1), species, ftab_ref
+    )
+    emb = embed_rows(embed)
+    emb_ref[...] = emb
+    h0 = hdot_t(embed, kinds(own[3:4], species)[:species])
+    h0_far = hdot_t(embed, kinds(doubled(there[0:8])[3:4], species)[:species])
     g = bdot(tab_ref[...], sel_ref[...])
     gf = bdot(ftab_ref[...], sel_far_ref[...])
 
-    far, h_far = gathered(g, width)
+    edges = slots * atoms
+    half = doubled(there)
+    far = [jnp.concatenate(x, axis=1) for x in zip(far_positions(g), far_positions(gf))]
+    centre = [
+        jnp.concatenate(
+            [spread_rows(own[c : c + 1], 8)] * slots + [spread_rows(half[c : c + 1], 8)] * tiles,
+            axis=1,
+        )
+        for c in range(3)
+    ]
     counts = spread_rows(sent_ref[8 + slots : 9 + slots, :], 8)
-    unit, inv, b, db = edge_geometry(far, own, counts, slots)
+    far_counts = spread_rows(half[8 + slots : 9 + slots], 8) - jnp.where(
+        lane_low(8), F32(0), F32(tiles)
+    )
+    valid = jnp.concatenate(
+        [(counts > F32(k)).astype(F32) for k in range(slots)]
+        + [(far_counts > F32(k)).astype(F32) for k in range(tiles)],
+        axis=1,
+    )
+    unit, inv, b, db = geometry(far, centre, valid)
     for i, x in enumerate(unit + [inv]):
-        geom_ref[i : i + 1, :] = x[0:1]
-    basis_ref[0] = b
-    basis_ref[1] = db
-    far, far_h = gathered(gf, width)
-    half = doubled(there)
-    counts = spread_rows(half[8 + slots : 9 + slots], 8) - jnp.where(
-        lane_low(8), F32(0), F32(tiles)
-    )
-    far_unit, _, far_b, _ = edge_geometry(far, half, counts, tiles)
-
-    win, wmid, wout = win_ref[0], wmid_ref[0], wout_ref[0]
-    w = radial(win, wmid, wout, b)
-    wf = radial(win, wmid, wout, far_b)
-    a, b = messages(w, h_far, unit, width, slots)
-    b_all = jnp.concatenate(b, axis=1) * scale
-    pre = mixed_pre(a * scale, b_all, h0[:, :atoms], mix_ref)
-    pre_ref[...] = pre
-    b_ref[...] = b_all
-    vec = vec_ref[...]
-    lo_part, hi_part = features(pre, b_all, vec)
-    feats_ref[0 : 2 * width] = lo_part
-    feats_ref[2 * width :] = hi_part
-    low_lanes, high_lanes = packed(lo_part, hi_part)
+        geom_ref[i : i + 1, :] = x[0:1, :edges]
+    basis_ref[0] = b[:, :edges]
+    basis_ref[1] = db[:, :edges]
+    hot = jnp.concatenate([g[16:24], gf[16:24]], axis=1)
+    h = bdot(emb, jnp.concatenate([hot, hot], axis=0).astype(BF16))
+    w = radial(win_ref[0], wmid_ref[0], wout_ref[0], b)
+    wa = w[:width] * h
+    wb = w[width:] * h
+
+    def summed(first, count):
+        sums = [jnp.zeros((width, atoms), F32) for _ in range(4)]
+        for k in range(first, first + count):
+            x = wb[:, slot(k)]
+            sums[0] = sums[0] + wa[:, slot(k)]
+            for c in range(3):
+                sums[c + 1] = sums[c + 1] + x * tile8(unit[c][:, slot(k)], width // 8)
+        return sums
+
+    ours_sum = summed(0, slots)
+    theirs = [x + roll64(x) for x in summed(slots, tiles)]
+    both = [jnp.concatenate([x, y], axis=1) * scale for x, y in zip(ours_sum, theirs)]
+    q = both[1] * both[1] + both[2] * both[2] + both[3] * both[3]
+    pre = (
+        hdot_t(mix_ref[0], both[0])
+        + hdot_t(mix_ref[1], jnp.concatenate([h0, h0_far], axis=1))
+        + hdot_t(mix_ref[2], q)
+    )
+    pre_ref[...] = pre[:, :atoms]
+    for c in range(3):
+        b_ref[:, slot(c)] = both[c + 1][:, :atoms]
+    s1 = pre * sigmoid(pre)
+    v1 = hdot_t(vec_ref[...], jnp.concatenate(both[1:], axis=1))
+    for domain, ref in ((0, feats_ref), (1, far_feats_ref)):
+        ref[0:width] = s1[:, slot(domain)]
+        for c in range(3):
+            ref[(c + 1) * width : (c + 2) * width] = v1[:, slot(2 * c + domain)]
+    low_lanes, high_lanes = packed(feats_ref[0 : 2 * width], feats_ref[2 * width :])
     near_out[...] = jnp.where(parity_odd(2 * width), low_lanes, high_lanes)
-
-    a, b = messages(wf, far_h, far_unit, width, tiles)
-    a = (a + roll64(a)) * scale
-    b_all = jnp.concatenate([x + roll64(x) for x in b], axis=1) * scale
-    pre = mixed_pre(a, b_all, doubled(h0_far[:, :atoms]), mix_ref)
-    lo_part, hi_part = features(pre, b_all, vec)
-    far_feats_ref[0 : 2 * width] = lo_part
-    far_feats_ref[2 * width :] = hi_part
 
 
 def packed(lo_part, hi_part):
@@ -567,8 +608,9 @@
 
 def tangent_one_kernel(
     basis_ref,
-    htab_ref,
+    tab_ref,
     ftab_ref,
+    emb_ref,
     sel_ref,
     there_ref,
     win_ref,
@@ -584,7 +626,8 @@
     sel_scr,
 ):
     atoms = there_ref.shape[1]
-    width = htab_ref.shape[0] // 2
+    width = emb_ref.shape[0]
+    emb = emb_ref[...]
     slots = sel_ref.shape[1] // atoms
     win, wmid, wout = win_ref[0], wmid_ref[0], wout_ref[0]
 
@@ -594,13 +637,13 @@
         edge_ref[domain, 2 * width :] = w[width:] * h
 
     w, dw = radial_pair(win, wmid, wout, basis_ref[0], basis_ref[1])
-    g = bdot(htab_ref[...], sel_ref[...])
-    store(0, w, dw, g[:width] + g[width:])
+    store(0, w, dw, far_kinds(bdot(tab_ref[...], sel_ref[...]), emb))
 
     there = there_ref[...]
     build_selector(there[8 : 8 + slots], sel_scr)
     sel_ghost_ref[...] = sel_scr[atoms:]
-    far, h = gathered(bdot(ftab_ref[...], sel_scr[...]), width)
+    g = bdot(ftab_ref[...], sel_scr[...])
+    far, h = far_positions(g), far_kinds(g, emb)
     counts = spread_rows(there[8 + slots : 9 + slots], 8)
     unit, inv, b, db = edge_geometry(far, there, counts, slots)
     for i, x in enumerate(unit + [inv]):
@@ -611,10 +654,7 @@
     scale = 1.0 / jnp.sqrt(F32(slots))
     b_all = jnp.concatenate(b, axis=1) * scale
     species = embed_ref.shape[0]
-    kind = jnp.broadcast_to(there[3:4], (species, atoms))
-    onehot = (
-        kind == (lax.broadcasted_iota(jnp.int32, (species, atoms), 0) + 1).astype(F32)
-    ).astype(F32)
+    onehot = kinds(there[3:4], species)[:species]
     pre_ref[...] = mixed_pre(a * scale, b_all, hdot_t(embed_ref[...], onehot), mix_ref)
     b_ref[...] = b_all
 
@@ -790,15 +830,15 @@
     sent = jnp.concatenate([own] + near_rows + [edge_rows], axis=0)
     pairs = [[i, (i + 1) % devices] for i in range(1, devices, 2)]
     come = lax.all_gather(sent, "space", axis_index_groups=pairs)
-    table_rows = 2 * width + 80
-    feats, far_feats, near_f, htab, ftab, geom, basis, pre, b_all, there = call(
+    feats, far_feats, near_f, tab, ftab, emb, geom, basis, pre, b_all, there = call(
         layer_one_kernel,
         [
             shape((4 * width, atoms)),
             shape((4 * width, atoms)),
             shape((rows, atoms)),
-            shape((2 * width, 2 * atoms), BF16),
-            shape((table_rows, 2 * atoms), BF16),
+            shape((32, 2 * atoms), BF16),
+            shape((32, 2 * atoms), BF16),
+            shape((width, 16), BF16),
             shape((8, edges)),
             shape((2, nbasis, edges)),
             shape((width, atoms)),
@@ -806,10 +846,7 @@
             shape((slots + 16, atoms)),
         ],
         [sent, come, sel, embed, win, wmid, wout, mix_one, vec_mix],
-        scratch=[
-            pltpu.VMEM((2 * atoms, edges // 2), BF16),
-            pltpu.VMEM((table_rows, 2 * atoms), BF16),
-        ],
+        scratch=[pltpu.VMEM((2 * atoms, edges // 2), BF16)],
         flops=2 * 10**9,
     )
     near_f = swap_near(near_f)
@@ -848,7 +885,7 @@
             shape((width, atoms)),
             shape((width, 3 * atoms)),
         ],
-        [basis, htab, ftab, sel, there, win, wmid, wout, mix_one, embed],
+        [basis, tab, ftab, emb, sel, there, win, wmid, wout, mix_one, embed],
         scratch=[pltpu.VMEM((2 * atoms, edges), BF16)],
         flops=4 * 10**9,
     )

time: 39.3 us -> 39.1 us (level)
  transfers between devices with their start and end apart: 6 -> 6, of which waited for: 3 -> 3; matrix products, arithmetic and copies ran while one was open for 0% -> 0% of each run, Pallas kernels for 21% -> 20%
where the time goes in v7:
time: 39.1 us; the launch traced here: 38.9 us
  Pallas kernels  16.6 us (42%)
  blocking collectives  9.31 us (24%)
  starting transfers between devices  6.33 us (16%)
  waiting for transfers between devices  5.27 us (13%)
  between operations  0.74 us (2%)
  other arithmetic  0.61 us (2%)
    pallas_call x7, Pallas kernels, call(): pl.pallas_call(kernel, out_shape=out_shapes, in_specs=[pl.BlockSpec(memor...  16.6 us
    all_gather x1, blocking collectives, body(): come = lax.all_gather(sent, 'space', axis_index_groups=pairs)  9.31 us
    ppermute x1, starting transfers between devices, swap_far(): return lax.ppermute(x, 'space', far_route)  4.8 us
    ppermute x1, waiting for transfers between devices, swap_far(): return lax.ppermute(x, 'space', far_route)  3.23 us
    ppermute x5, waiting for transfers between devices, swap_near(): return lax.ppermute(x, 'space', near_route)  2.05 us
    ppermute x5, starting transfers between devices, swap_near(): return lax.ppermute(x, 'space', near_route)  1.53 us
  transfers between devices with their start and end apart: 6, of which 3 were waited for; matrix products, arithmetic and copies ran while one was open for 0% of the time, Pallas kernels for 20%

profile of v7, /device:TPU:127, one launch (start us, length us, event | category | flops | bytes accessed | tf_op | source)
XLA Modules:
  0.0 38.9 jit_solution(15164815377086996250)
XLA Ops:
  0.6 0.8 %collective-permute-start.1 = (s32[128]{0:T(128)}, s32[128]{0:T(128)S(1)}, u32[]{:S(2)}, u32[]{:S(2)}) collective-permute-start(s32[128]{0:T(128)} %param.14), channel_id=1, source_target_pairs={{0,1},{1,0},{2,3},{3,2},{4,5},{5,4},{6,7},{7,6},{8,9},{9,8},{10,11... | collective-permute-start | bytes 1544 | tf_op jit(solution)/shard_map/ppermute | solution.py:795
  1.4 0.1 collective-permute-start
  1.5 1.9 %shard_map.140 = (f32[4,128]{1,0:T(4,128)S(1)}, f32[32,128]{1,0:T(8,128)S(1)}, bf16[256,3072]{1,0:T(8,128)(2,1)S(1)}, bf16[2,64,32]{2,1,0:T(8,128)(2,1)S(1)}, bf...) custom-call(f32[3,128]{1,0:T(4,128)} %pos_hbm.1, ...), custom_call_target="tpu_custom_call" | custom-call | flops 100000000 | bytes 2065408 | tf_op jit(solution)/shard_map/pallas_call | solution.py:752
  3.4 0.0 collective-permute-done.1
  3.4 0.0 collective-permute-done
  3.4 9.3 %all-gather = f32[80,128]{1,0:T(8,128)S(1)} all-gather(f32[40,128]{1,0:T(8,128)S(1)} %pad_maximum_fusion.sent_ref), channel_id=2, replica_groups={{1,2},{3,4},{5,6},{7,8},{9,10},{11,12},{13,14},{15,16},{17,18},{19,20},..., dimensions={0}, use_global_device_ids=true | all-gather | bytes 61440 | tf_op jit(solution)/shard_map/all_gather | solution.py:832
  12.7 3.0 %shard_map.141 = (f32[256,128]{1,0:T(8,128)S(1)}, f32[256,128]{1,0:T(8,128)S(1)}, f32[128,128]{1,0:T(8,128)S(1)}, bf16[32,256]{1,0:T(8,128)(2,1)S(1)}, bf16[32,2...) custom-call(f32[40,128]{1,0:T(8,128)S(1)} %pad_maximum_fusion.sent_r, ...), custom_call_target="tpu_custom_call" | custom-call | flops 2000000000 | bytes 2665984 | tf_op jit(solution)/shard_map/pallas_call | solution.py:752
  15.8 0.1 collective-permute-start.2
  15.9 1.5 %shard_map.142 = (f32[128,3072]{1,0:T(8,128)S(1)}, f32[128,3072]{1,0:T(8,128)S(1)}) custom-call(f32[2,8,3072]{2,1,0:T(8,128)S(1)} %get-tuple-element.53.basis_ref, bf16[2,64,32]{2,1,0:T(8,128)(2,1)S(1)} %get-tuple-element.44.win_ref, bf16[2,64,192]{2,1,0:T(8,128)(2,1)S(1)} %get-tuple-element.45.wmid_ref, bf16[2,128,192]{2,1,0:T(8,128)(2,1)S(1)} %get-tuple-element.46.wout_ref), custom_call_target="tpu_custom_call" | custom-call | flops 2000000000 | bytes 3497984 | tf_op jit(solution)/shard_map/pallas_call | solution.py:752
  17.4 0.0 collective-permute-done.2.near_ref
  17.4 3.6 %shard_map.143 = (f32[1,128]{1,0:T(1,128)}, f32[256,128]{1,0:T(8,128)S(1)}, f32[256,128]{1,0:T(8,128)S(1)}, f32[128,128]{1,0:T(8,128)S(1)}, f32[128,128]{1,0:T(8...) custom-call(f32[256,128]{1,0:T(8,128)S(1)} %get-tuple-element.49.feats_ref, ...), custom_call_target="tpu_custom_call" | custom-call | flops 1000000000 | bytes 5579776 | tf_op jit(solution)/shard_map/pallas_call | solution.py:752
  21.0 0.5 %collective-permute-start.3 = (f32[128,128]{1,0:T(8,128)S(1)}, f32[128,128]{1,0:T(8,128)S(1)}, u32[]{:S(2)}, u32[]{:S(2)}) collective-permute-start(f32[128,128]{1,0:T(8,128)S(1)} %get-tuple-element.60), channel_id=1, source_target_pairs={{0,1},{1,0},{2,3},{3,2},{4,5},{5,4},{6,7},{7,6},{8,9},{9,8},{10,11... | collective-permute-start | bytes 196616 | tf_op jit(solution)/shard_map/ppermute | solution.py:795
  21.5 0.9 %collective-permute-done.3.near_ref = f32[128,128]{1,0:T(8,128)S(1)} collective-permute-done((f32[128,128]{1,0:T(8,128)S(1)}, f32[128,128]{1,0:T(8,128)S(1)}, u32[]{:S(2)}, u32[]{:S(2)}) %collective-permute-start.3) | collective-permute-done | bytes 65568 | tf_op jit(solution)/shard_map/ppermute | solution.py:795
  22.4 0.1 shard_map.144.sent_ref
  22.5 4.8 %collective-permute-start.4 = (f32[392,128]{1,0:T(8,128)S(1)}, f32[392,128]{1,0:T(8,128)S(1)}, u32[]{:S(2)}, u32[]{:S(2)}) collective-permute-start(f32[392,128]{1,0:T(8,128)S(1)} %shard_map.144.sent_ref), channel_id=1, source_target_pairs={{1,2},{2,1},{3,4},{4,3},{5,6},{6,5},{7,8},{8,7},{9,10},{10,9},{11,... | collective-permute-start | bytes 602120 | tf_op jit(solution)/shard_map/ppermute | solution.py:798
  27.3 4.4 %shard_map.145 = (f32[2,192,3072]{2,1,0:T(8,128)S(1)}, bf16[128,3072]{1,0:T(8,128)(2,1)S(1)}, f32[8,3072]{1,0:T(8,128)S(1)}, f32[64,128]{1,0:T(8,128)S(1)}, f32[64,384]{1,0:T(8,128)S(1)}) custom-call(f32[2,8,3072]{2,1,0:T(8,128)S(1)} %get-tuple-element.53.basis_ref, bf16[32,256]{1,0:T(8,128)(2,1)S(1)} %get-tuple-element.64.tab_ref, ...), custom_call_target="tpu_custom_call" | custom-call | flops 4000000000 | bytes 7765504 | tf_op jit(solution)/shard_map/pallas_call | solution.py:752
  31.8 3.2 %collective-permute-done.4.far_ref = f32[392,128]{1,0:T(8,128)S(1)} collective-permute-done((f32[392,128]{1,0:T(8,128)S(1)}, f32[392,128]{1,0:T(8,128)S(1)}, u32[]{:S(2)}, u32[]{:S(2)}) %collective-permute-start.4) | collective-permute-done | bytes 200736 | tf_op jit(solution)/shard_map/ppermute | solution.py:798
  35.0 2.1 %shard_map.146 = (f32[8,128]{1,0:T(8,128)S(1)}, f32[8,128]{1,0:T(8,128)S(1)}) custom-call(f32[392,128]{1,0:T(8,128)S(1)} %shard_map.144.sent_ref, f32[392,128]{1,0:T(8,128)S(1)} %collective-permute-done.4.far_ref, f32[256,128]{1,0:T(8,128)S(1)} %get-tuple-element.63.gghost_ref, bf16[256,3072]{1,0:T(8,128)(2,1)S(1)} %get-tuple-element.42.sel_ref, ...), custom_call_target="tpu_custom_call" | custom-call | flops 1000000000 | bytes 8146944 | tf_op jit(solution)/shard_map/pallas_call | solution.py:752
  37.0 0.1 collective-permute-start.5
  37.2 1.1 %collective-permute-done.5 = f32[8,128]{1,0:T(8,128)S(1)} collective-permute-done((f32[8,128]{1,0:T(8,128)S(1)}, f32[8,128]{1,0:T(8,128)S(1)}, u32[]{:S(2)}, u32[]{:S(2)}) %collective-permute-start.5) | collective-permute-done | bytes 4128 | tf_op jit(solution)/shard_map/ppermute | solution.py:795
  38.3 0.6 %add_negate_fusion = f32[3,128]{1,0:T(4,128)} fusion(f32[8,128]{1,0:T(8,128)S(1)} %collective-permute-done.5, f32[8,128]{1,0:T(8,128)S(1)} %get-tuple-element.76, pred[128]{0:T(512)(128)(4,1)S(1)} %compare_compare_fusion), kind=kLoop, calls=%fused_computation.1 | loop fusion | flops 1152 | bytes 4736 | tf_op jit(solution)/shard_map/neg | solution.py:919
  (3 shorter events, 0.0 us)
Async XLA Ops:
  0.6 2.8 %collective-permute-start.1 = (s32[128]{0:T(128)}, s32[128]{0:T(128)S(1)}, u32[]{:S(2)}, u32[]{:S(2)}) collective-permute-start(s32[128]{0:T(128)} %param.14), channel_id=1, source_target_pairs={{0,1},{1,0},{2,3},{3,2},{4,5},{5,4},{6,7},{7,6},{8,9},{9,8},{10,11... | collective-permute-start | bytes 1544 | tf_op jit(solution)/shard_map/ppermute | solution.py:795
  1.4 2.0 %collective-permute-start = (f32[3,128]{1,0:T(4,128)}, f32[3,128]{1,0:T(4,128)S(1)}, u32[]{:S(2)}, u32[]{:S(2)}) collective-permute-start(f32[3,128]{1,0:T(4,128)} %pos_hbm.1), channel_id=1, source_target_pairs={{0,1},{1,0},{2,3},{3,2},{4,5},{5,4},{6,7},{7,6},{8,9},{9,8},{10,11... | collective-permute-start | bytes 4616 | tf_op jit(solution)/shard_map/ppermute | solution.py:795
  15.8 1.6 %collective-permute-start.2 = (f32[128,128]{1,0:T(8,128)S(1)}, f32[128,128]{1,0:T(8,128)S(1)}, u32[]{:S(2)}, u32[]{:S(2)}) collective-permute-start(f32[128,128]{1,0:T(8,128)S(1)} %get-tuple-element.51), channel_id=1, source_target_pairs={{0,1},{1,0},{2,3},{3,2},{4,5},{5,4},{6,7},{7,6},{8,9},{9,8},{10,11... | collective-permute-start | bytes 196616 | tf_op jit(solution)/shard_map/ppermute | solution.py:795
  21.0 1.4 %collective-permute-start.3 = (f32[128,128]{1,0:T(8,128)S(1)}, f32[128,128]{1,0:T(8,128)S(1)}, u32[]{:S(2)}, u32[]{:S(2)}) collective-permute-start(f32[128,128]{1,0:T(8,128)S(1)} %get-tuple-element.60), channel_id=1, source_target_pairs={{0,1},{1,0},{2,3},{3,2},{4,5},{5,4},{6,7},{7,6},{8,9},{9,8},{10,11... | collective-permute-start | bytes 196616 | tf_op jit(solution)/shard_map/ppermute | solution.py:795
  22.5 12.5 %collective-permute-start.4 = (f32[392,128]{1,0:T(8,128)S(1)}, f32[392,128]{1,0:T(8,128)S(1)}, u32[]{:S(2)}, u32[]{:S(2)}) collective-permute-start(f32[392,128]{1,0:T(8,128)S(1)} %shard_map.144.sent_ref), channel_id=1, source_target_pairs={{1,2},{2,1},{3,4},{4,3},{5,6},{6,5},{7,8},{8,7},{9,10},{10,9},{11,... | collective-permute-start | bytes 602120 | tf_op jit(solution)/shard_map/ppermute | solution.py:798
  37.0 1.3 %collective-permute-start.5 = (f32[8,128]{1,0:T(8,128)S(1)}, f32[8,128]{1,0:T(8,128)S(1)}, u32[]{:S(2)}, u32[]{:S(2)}) collective-permute-start(f32[8,128]{1,0:T(8,128)S(1)} %get-tuple-element.77), channel_id=1, source_target_pairs={{0,1},{1,0},{2,3},{3,2},{4,5},{5,4},{6,7},{7,6},{8,9},{9,8},{10,11... | collective-permute-start | bytes 12296 | tf_op jit(solution)/shard_map/ppermute | solution.py:795

commit v8 on v7

--- a/solution.py
+++ b/solution.py
@@ -488,11 +488,14 @@
     return total
 
 
+def both_parts(grads):
+    x = jnp.concatenate(list(grads), axis=0)
+    h = high(x)
+    return jnp.concatenate([h, x - h], axis=0).astype(BF16)
+
+
 def put_positions(ref, base, grads):
-    x = jnp.concatenate(list(grads), axis=0)
-    hi, lo = split(x)
-    ref[base : base + 24] = hi
-    ref[base + 24 : base + 48] = lo
+    ref[base : base + 48] = both_parts(grads)
 
 
 def rows8(x):
@@ -725,12 +728,9 @@
             carried = edge_ref[domain, 2 * width :, slot(k)]
             du = [sum_groups(carried * gb[c]) for c in range(3)]
             gp = edge_gradient(unit, spread_rows(geom[3:4, slot(k)], 8), sum_groups(drho), du)
-            x = jnp.concatenate(gp, axis=0)
             if domain == 0:
-                total = total + x
-            hi, lo = split(x)
-            scr_of[domain][0:24, slot(k)] = hi
-            scr_of[domain][24:48, slot(k)] = lo
+                total = total + jnp.concatenate(gp, axis=0)
+            scr_of[domain][:, slot(k)] = both_parts(gp)
         if domain == 0:
             centre = total
     acc = bdot_nt(pos_scr[...], sel_ref[...])

time: 39.1 us -> 39.1 us (level)
  no operation moved by 1% of the time
where the time goes in v8:
time: 39.1 us; the launch traced here: 38.9 us
  Pallas kernels  16.6 us (42%)
  blocking collectives  9.31 us (24%)
  starting transfers between devices  6.33 us (16%)
  waiting for transfers between devices  5.27 us (13%)
  between operations  0.74 us (2%)
  other arithmetic  0.61 us (2%)
    pallas_call x7, Pallas kernels, call(): pl.pallas_call(kernel, out_shape=out_shapes, in_specs=[pl.BlockSpec(memor...  16.6 us
    all_gather x1, blocking collectives, body(): come = lax.all_gather(sent, 'space', axis_index_groups=pairs)  9.31 us
    ppermute x1, starting transfers between devices, swap_far(): return lax.ppermute(x, 'space', far_route)  4.8 us
    ppermute x1, waiting for transfers between devices, swap_far(): return lax.ppermute(x, 'space', far_route)  3.23 us
    ppermute x5, waiting for transfers between devices, swap_near(): return lax.ppermute(x, 'space', near_route)  2.05 us
    ppermute x5, starting transfers between devices, swap_near(): return lax.ppermute(x, 'space', near_route)  1.53 us
  transfers between devices with their start and end apart: 6, of which 3 were waited for; matrix products, arithmetic and copies ran while one was open for 0% of the time, Pallas kernels for 20%

profile of v8, /device:TPU:127, one launch (start us, length us, event | category | flops | bytes accessed | tf_op | source)
XLA Modules:
  0.0 38.9 jit_solution(6419391928470122020)
XLA Ops:
  0.6 0.8 %collective-permute-start.1 = (s32[128]{0:T(128)}, s32[128]{0:T(128)S(1)}, u32[]{:S(2)}, u32[]{:S(2)}) collective-permute-start(s32[128]{0:T(128)} %param.14), channel_id=1, source_target_pairs={{0,1},{1,0},{2,3},{3,2},{4,5},{5,4},{6,7},{7,6},{8,9},{9,8},{10,11... | collective-permute-start | bytes 1544 | tf_op jit(solution)/shard_map/ppermute | solution.py:795
  1.4 0.1 collective-permute-start
  1.5 1.9 %shard_map.140 = (f32[4,128]{1,0:T(4,128)S(1)}, f32[32,128]{1,0:T(8,128)S(1)}, bf16[256,3072]{1,0:T(8,128)(2,1)S(1)}, bf16[2,64,32]{2,1,0:T(8,128)(2,1)S(1)}, bf...) custom-call(f32[3,128]{1,0:T(4,128)} %pos_hbm.1, ...), custom_call_target="tpu_custom_call" | custom-call | flops 100000000 | bytes 2065408 | tf_op jit(solution)/shard_map/pallas_call | solution.py:752
  3.4 0.0 collective-permute-done.1
  3.4 0.0 collective-permute-done
  3.4 9.3 %all-gather = f32[80,128]{1,0:T(8,128)S(1)} all-gather(f32[40,128]{1,0:T(8,128)S(1)} %pad_maximum_fusion.sent_ref), channel_id=2, replica_groups={{1,2},{3,4},{5,6},{7,8},{9,10},{11,12},{13,14},{15,16},{17,18},{19,20},..., dimensions={0}, use_global_device_ids=true | all-gather | bytes 61440 | tf_op jit(solution)/shard_map/all_gather | solution.py:832
  12.7 3.0 %shard_map.141 = (f32[256,128]{1,0:T(8,128)S(1)}, f32[256,128]{1,0:T(8,128)S(1)}, f32[128,128]{1,0:T(8,128)S(1)}, bf16[32,256]{1,0:T(8,128)(2,1)S(1)}, bf16[32,2...) custom-call(f32[40,128]{1,0:T(8,128)S(1)} %pad_maximum_fusion.sent_r, ...), custom_call_target="tpu_custom_call" | custom-call | flops 2000000000 | bytes 2665984 | tf_op jit(solution)/shard_map/pallas_call | solution.py:752
  15.8 0.1 collective-permute-start.2
  15.9 1.5 %shard_map.142 = (f32[128,3072]{1,0:T(8,128)S(1)}, f32[128,3072]{1,0:T(8,128)S(1)}) custom-call(f32[2,8,3072]{2,1,0:T(8,128)S(1)} %get-tuple-element.53.basis_ref, bf16[2,64,32]{2,1,0:T(8,128)(2,1)S(1)} %get-tuple-element.44.win_ref, bf16[2,64,192]{2,1,0:T(8,128)(2,1)S(1)} %get-tuple-element.45.wmid_ref, bf16[2,128,192]{2,1,0:T(8,128)(2,1)S(1)} %get-tuple-element.46.wout_ref), custom_call_target="tpu_custom_call" | custom-call | flops 2000000000 | bytes 3497984 | tf_op jit(solution)/shard_map/pallas_call | solution.py:752
  17.4 0.0 collective-permute-done.2.near_ref
  17.4 3.6 %shard_map.143 = (f32[1,128]{1,0:T(1,128)}, f32[256,128]{1,0:T(8,128)S(1)}, f32[256,128]{1,0:T(8,128)S(1)}, f32[128,128]{1,0:T(8,128)S(1)}, f32[128,128]{1,0:T(8...) custom-call(f32[256,128]{1,0:T(8,128)S(1)} %get-tuple-element.49.feats_ref, ...), custom_call_target="tpu_custom_call" | custom-call | flops 1000000000 | bytes 5579776 | tf_op jit(solution)/shard_map/pallas_call | solution.py:752
  21.0 0.5 %collective-permute-start.3 = (f32[128,128]{1,0:T(8,128)S(1)}, f32[128,128]{1,0:T(8,128)S(1)}, u32[]{:S(2)}, u32[]{:S(2)}) collective-permute-start(f32[128,128]{1,0:T(8,128)S(1)} %get-tuple-element.60), channel_id=1, source_target_pairs={{0,1},{1,0},{2,3},{3,2},{4,5},{5,4},{6,7},{7,6},{8,9},{9,8},{10,11... | collective-permute-start | bytes 196616 | tf_op jit(solution)/shard_map/ppermute | solution.py:795
  21.5 0.9 %collective-permute-done.3.near_ref = f32[128,128]{1,0:T(8,128)S(1)} collective-permute-done((f32[128,128]{1,0:T(8,128)S(1)}, f32[128,128]{1,0:T(8,128)S(1)}, u32[]{:S(2)}, u32[]{:S(2)}) %collective-permute-start.3) | collective-permute-done | bytes 65568 | tf_op jit(solution)/shard_map/ppermute | solution.py:795
  22.4 0.1 shard_map.144.sent_ref
  22.5 4.8 %collective-permute-start.4 = (f32[392,128]{1,0:T(8,128)S(1)}, f32[392,128]{1,0:T(8,128)S(1)}, u32[]{:S(2)}, u32[]{:S(2)}) collective-permute-start(f32[392,128]{1,0:T(8,128)S(1)} %shard_map.144.sent_ref), channel_id=1, source_target_pairs={{1,2},{2,1},{3,4},{4,3},{5,6},{6,5},{7,8},{8,7},{9,10},{10,9},{11,... | collective-permute-start | bytes 602120 | tf_op jit(solution)/shard_map/ppermute | solution.py:798
  27.3 4.4 %shard_map.145 = (f32[2,192,3072]{2,1,0:T(8,128)S(1)}, bf16[128,3072]{1,0:T(8,128)(2,1)S(1)}, f32[8,3072]{1,0:T(8,128)S(1)}, f32[64,128]{1,0:T(8,128)S(1)}, f32[64,384]{1,0:T(8,128)S(1)}) custom-call(f32[2,8,3072]{2,1,0:T(8,128)S(1)} %get-tuple-element.53.basis_ref, bf16[32,256]{1,0:T(8,128)(2,1)S(1)} %get-tuple-element.64.tab_ref, ...), custom_call_target="tpu_custom_call" | custom-call | flops 4000000000 | bytes 7765504 | tf_op jit(solution)/shard_map/pallas_call | solution.py:752
  31.8 3.2 %collective-permute-done.4.far_ref = f32[392,128]{1,0:T(8,128)S(1)} collective-permute-done((f32[392,128]{1,0:T(8,128)S(1)}, f32[392,128]{1,0:T(8,128)S(1)}, u32[]{:S(2)}, u32[]{:S(2)}) %collective-permute-start.4) | collective-permute-done | bytes 200736 | tf_op jit(solution)/shard_map/ppermute | solution.py:798
  35.0 2.1 %shard_map.146 = (f32[8,128]{1,0:T(8,128)S(1)}, f32[8,128]{1,0:T(8,128)S(1)}) custom-call(f32[392,128]{1,0:T(8,128)S(1)} %shard_map.144.sent_ref, f32[392,128]{1,0:T(8,128)S(1)} %collective-permute-done.4.far_ref, f32[256,128]{1,0:T(8,128)S(1)} %get-tuple-element.63.gghost_ref, bf16[256,3072]{1,0:T(8,128)(2,1)S(1)} %get-tuple-element.42.sel_ref, ...), custom_call_target="tpu_custom_call" | custom-call | flops 1000000000 | bytes 8146944 | tf_op jit(solution)/shard_map/pallas_call | solution.py:752
  37.0 0.1 collective-permute-start.5
  37.2 1.1 %collective-permute-done.5 = f32[8,128]{1,0:T(8,128)S(1)} collective-permute-done((f32[8,128]{1,0:T(8,128)S(1)}, f32[8,128]{1,0:T(8,128)S(1)}, u32[]{:S(2)}, u32[]{:S(2)}) %collective-permute-start.5) | collective-permute-done | bytes 4128 | tf_op jit(solution)/shard_map/ppermute | solution.py:795
  38.3 0.6 %add_negate_fusion = f32[3,128]{1,0:T(4,128)} fusion(f32[8,128]{1,0:T(8,128)S(1)} %collective-permute-done.5, f32[8,128]{1,0:T(8,128)S(1)} %get-tuple-element.76, pred[128]{0:T(512)(128)(4,1)S(1)} %compare_compare_fusion), kind=kLoop, calls=%fused_computation.1 | loop fusion | flops 1152 | bytes 4736 | tf_op jit(solution)/shard_map/neg | solution.py:919
  (3 shorter events, 0.0 us)
Async XLA Ops:
  0.6 2.8 %collective-permute-start.1 = (s32[128]{0:T(128)}, s32[128]{0:T(128)S(1)}, u32[]{:S(2)}, u32[]{:S(2)}) collective-permute-start(s32[128]{0:T(128)} %param.14), channel_id=1, source_target_pairs={{0,1},{1,0},{2,3},{3,2},{4,5},{5,4},{6,7},{7,6},{8,9},{9,8},{10,11... | collective-permute-start | bytes 1544 | tf_op jit(solution)/shard_map/ppermute | solution.py:795
  1.4 2.0 %collective-permute-start = (f32[3,128]{1,0:T(4,128)}, f32[3,128]{1,0:T(4,128)S(1)}, u32[]{:S(2)}, u32[]{:S(2)}) collective-permute-start(f32[3,128]{1,0:T(4,128)} %pos_hbm.1), channel_id=1, source_target_pairs={{0,1},{1,0},{2,3},{3,2},{4,5},{5,4},{6,7},{7,6},{8,9},{9,8},{10,11... | collective-permute-start | bytes 4616 | tf_op jit(solution)/shard_map/ppermute | solution.py:795
  15.8 1.6 %collective-permute-start.2 = (f32[128,128]{1,0:T(8,128)S(1)}, f32[128,128]{1,0:T(8,128)S(1)}, u32[]{:S(2)}, u32[]{:S(2)}) collective-permute-start(f32[128,128]{1,0:T(8,128)S(1)} %get-tuple-element.51), channel_id=1, source_target_pairs={{0,1},{1,0},{2,3},{3,2},{4,5},{5,4},{6,7},{7,6},{8,9},{9,8},{10,11... | collective-permute-start | bytes 196616 | tf_op jit(solution)/shard_map/ppermute | solution.py:795
  21.0 1.4 %collective-permute-start.3 = (f32[128,128]{1,0:T(8,128)S(1)}, f32[128,128]{1,0:T(8,128)S(1)}, u32[]{:S(2)}, u32[]{:S(2)}) collective-permute-start(f32[128,128]{1,0:T(8,128)S(1)} %get-tuple-element.60), channel_id=1, source_target_pairs={{0,1},{1,0},{2,3},{3,2},{4,5},{5,4},{6,7},{7,6},{8,9},{9,8},{10,11... | collective-permute-start | bytes 196616 | tf_op jit(solution)/shard_map/ppermute | solution.py:795
  22.5 12.5 %collective-permute-start.4 = (f32[392,128]{1,0:T(8,128)S(1)}, f32[392,128]{1,0:T(8,128)S(1)}, u32[]{:S(2)}, u32[]{:S(2)}) collective-permute-start(f32[392,128]{1,0:T(8,128)S(1)} %shard_map.144.sent_ref), channel_id=1, source_target_pairs={{1,2},{2,1},{3,4},{4,3},{5,6},{6,5},{7,8},{8,7},{9,10},{10,9},{11,... | collective-permute-start | bytes 602120 | tf_op jit(solution)/shard_map/ppermute | solution.py:798
  37.0 1.3 %collective-permute-start.5 = (f32[8,128]{1,0:T(8,128)S(1)}, f32[8,128]{1,0:T(8,128)S(1)}, u32[]{:S(2)}, u32[]{:S(2)}) collective-permute-start(f32[8,128]{1,0:T(8,128)S(1)} %get-tuple-element.77), channel_id=1, source_target_pairs={{0,1},{1,0},{2,3},{3,2},{4,5},{5,4},{6,7},{7,6},{8,9},{9,8},{10,11... | collective-permute-start | bytes 12296 | tf_op jit(solution)/shard_map/ppermute | solution.py:795

commit v9 on v8

--- a/solution.py
+++ b/solution.py
@@ -542,9 +542,9 @@
     feats = feats_ref[...]
     table = jnp.concatenate([feats, jnp.concatenate([g_lo, g_hi], axis=0)], axis=1)
     t_hi, t_lo = split(table)
-    g = bdot(jnp.concatenate([t_hi, t_lo], axis=0), sel_ref[...])
-
-    f = g[: 4 * width] + g[4 * width :]
+    sel = sel_ref[...]
+
+    f = bdot(t_hi, sel) + bdot(t_lo, sel)
     unit = [geom_ref[c : c + 1, :] for c in range(3)]
     along = f[width : 2 * width] * spread_rows(unit[0], width)
     along = along + f[2 * width : 3 * width] * spread_rows(unit[1], width)

time: 39.1 us -> 39.1 us (level)
  no operation moved by 1% of the time
where the time goes in v9:
time: 39.1 us; the launch traced here: 38.9 us
  Pallas kernels  16.6 us (42%)
  blocking collectives  9.31 us (24%)
  starting transfers between devices  6.33 us (16%)
  waiting for transfers between devices  5.28 us (14%)
  between operations  0.74 us (2%)
  other arithmetic  0.61 us (2%)
    pallas_call x7, Pallas kernels, call(): pl.pallas_call(kernel, out_shape=out_shapes, in_specs=[pl.BlockSpec(memor...  16.6 us
    all_gather x1, blocking collectives, body(): come = lax.all_gather(sent, 'space', axis_index_groups=pairs)  9.31 us
    ppermute x1, starting transfers between devices, swap_far(): return lax.ppermute(x, 'space', far_route)  4.8 us
    ppermute x1, waiting for transfers between devices, swap_far(): return lax.ppermute(x, 'space', far_route)  3.23 us
    ppermute x5, waiting for transfers between devices, swap_near(): return lax.ppermute(x, 'space', near_route)  2.05 us
    ppermute x5, starting transfers between devices, swap_near(): return lax.ppermute(x, 'space', near_route)  1.53 us
  transfers between devices with their start and end apart: 6, of which 3 were waited for; matrix products, arithmetic and copies ran while one was open for 0% of the time, Pallas kernels for 20%

profile of v9, /device:TPU:127, one launch (start us, length us, event | category | flops | bytes accessed | tf_op | source)
XLA Modules:
  0.0 38.9 jit_solution(8563102846075729422)
XLA Ops:
  0.6 0.8 %collective-permute-start.1 = (s32[128]{0:T(128)}, s32[128]{0:T(128)S(1)}, u32[]{:S(2)}, u32[]{:S(2)}) collective-permute-start(s32[128]{0:T(128)} %param.14), channel_id=1, source_target_pairs={{0,1},{1,0},{2,3},{3,2},{4,5},{5,4},{6,7},{7,6},{8,9},{9,8},{10,11... | collective-permute-start | bytes 1544 | tf_op jit(solution)/shard_map/ppermute | solution.py:795
  1.4 0.1 collective-permute-start
  1.5 1.9 %shard_map.140 = (f32[4,128]{1,0:T(4,128)S(1)}, f32[32,128]{1,0:T(8,128)S(1)}, bf16[256,3072]{1,0:T(8,128)(2,1)S(1)}, bf16[2,64,32]{2,1,0:T(8,128)(2,1)S(1)}, bf...) custom-call(f32[3,128]{1,0:T(4,128)} %pos_hbm.1, ...), custom_call_target="tpu_custom_call" | custom-call | flops 100000000 | bytes 2065408 | tf_op jit(solution)/shard_map/pallas_call | solution.py:752
  3.4 0.0 collective-permute-done.1
  3.4 0.0 collective-permute-done
  3.4 9.3 %all-gather = f32[80,128]{1,0:T(8,128)S(1)} all-gather(f32[40,128]{1,0:T(8,128)S(1)} %pad_maximum_fusion.sent_ref), channel_id=2, replica_groups={{1,2},{3,4},{5,6},{7,8},{9,10},{11,12},{13,14},{15,16},{17,18},{19,20},..., dimensions={0}, use_global_device_ids=true | all-gather | bytes 61440 | tf_op jit(solution)/shard_map/all_gather | solution.py:832
  12.7 3.0 %shard_map.141 = (f32[256,128]{1,0:T(8,128)S(1)}, f32[256,128]{1,0:T(8,128)S(1)}, f32[128,128]{1,0:T(8,128)S(1)}, bf16[32,256]{1,0:T(8,128)(2,1)S(1)}, bf16[32,2...) custom-call(f32[40,128]{1,0:T(8,128)S(1)} %pad_maximum_fusion.sent_r, ...), custom_call_target="tpu_custom_call" | custom-call | flops 2000000000 | bytes 2665984 | tf_op jit(solution)/shard_map/pallas_call | solution.py:752
  15.8 0.1 collective-permute-start.2
  15.9 1.5 %shard_map.142 = (f32[128,3072]{1,0:T(8,128)S(1)}, f32[128,3072]{1,0:T(8,128)S(1)}) custom-call(f32[2,8,3072]{2,1,0:T(8,128)S(1)} %get-tuple-element.53.basis_ref, bf16[2,64,32]{2,1,0:T(8,128)(2,1)S(1)} %get-tuple-element.44.win_ref, bf16[2,64,192]{2,1,0:T(8,128)(2,1)S(1)} %get-tuple-element.45.wmid_ref, bf16[2,128,192]{2,1,0:T(8,128)(2,1)S(1)} %get-tuple-element.46.wout_ref), custom_call_target="tpu_custom_call" | custom-call | flops 2000000000 | bytes 3497984 | tf_op jit(solution)/shard_map/pallas_call | solution.py:752
  17.4 0.0 collective-permute-done.2.near_ref
  17.4 3.6 %shard_map.143 = (f32[1,128]{1,0:T(1,128)}, f32[256,128]{1,0:T(8,128)S(1)}, f32[256,128]{1,0:T(8,128)S(1)}, f32[128,128]{1,0:T(8,128)S(1)}, f32[128,128]{1,0:T(8...) custom-call(f32[256,128]{1,0:T(8,128)S(1)} %get-tuple-element.49.feats_ref, ...), custom_call_target="tpu_custom_call" | custom-call | flops 1000000000 | bytes 5579776 | tf_op jit(solution)/shard_map/pallas_call | solution.py:752
  21.1 0.5 %collective-permute-start.3 = (f32[128,128]{1,0:T(8,128)S(1)}, f32[128,128]{1,0:T(8,128)S(1)}, u32[]{:S(2)}, u32[]{:S(2)}) collective-permute-start(f32[128,128]{1,0:T(8,128)S(1)} %get-tuple-element.60), channel_id=1, source_target_pairs={{0,1},{1,0},{2,3},{3,2},{4,5},{5,4},{6,7},{7,6},{8,9},{9,8},{10,11... | collective-permute-start | bytes 196616 | tf_op jit(solution)/shard_map/ppermute | solution.py:795
  21.5 0.9 %collective-permute-done.3.near_ref = f32[128,128]{1,0:T(8,128)S(1)} collective-permute-done((f32[128,128]{1,0:T(8,128)S(1)}, f32[128,128]{1,0:T(8,128)S(1)}, u32[]{:S(2)}, u32[]{:S(2)}) %collective-permute-start.3) | collective-permute-done | bytes 65568 | tf_op jit(solution)/shard_map/ppermute | solution.py:795
  22.5 0.1 shard_map.144.sent_ref
  22.5 4.8 %collective-permute-start.4 = (f32[392,128]{1,0:T(8,128)S(1)}, f32[392,128]{1,0:T(8,128)S(1)}, u32[]{:S(2)}, u32[]{:S(2)}) collective-permute-start(f32[392,128]{1,0:T(8,128)S(1)} %shard_map.144.sent_ref), channel_id=1, source_target_pairs={{1,2},{2,1},{3,4},{4,3},{5,6},{6,5},{7,8},{8,7},{9,10},{10,9},{11,... | collective-permute-start | bytes 602120 | tf_op jit(solution)/shard_map/ppermute | solution.py:798
  27.3 4.4 %shard_map.145 = (f32[2,192,3072]{2,1,0:T(8,128)S(1)}, bf16[128,3072]{1,0:T(8,128)(2,1)S(1)}, f32[8,3072]{1,0:T(8,128)S(1)}, f32[64,128]{1,0:T(8,128)S(1)}, f32[64,384]{1,0:T(8,128)S(1)}) custom-call(f32[2,8,3072]{2,1,0:T(8,128)S(1)} %get-tuple-element.53.basis_ref, bf16[32,256]{1,0:T(8,128)(2,1)S(1)} %get-tuple-element.64.tab_ref, ...), custom_call_target="tpu_custom_call" | custom-call | flops 4000000000 | bytes 7765504 | tf_op jit(solution)/shard_map/pallas_call | solution.py:752
  31.8 3.2 %collective-permute-done.4.far_ref = f32[392,128]{1,0:T(8,128)S(1)} collective-permute-done((f32[392,128]{1,0:T(8,128)S(1)}, f32[392,128]{1,0:T(8,128)S(1)}, u32[]{:S(2)}, u32[]{:S(2)}) %collective-permute-start.4) | collective-permute-done | bytes 200736 | tf_op jit(solution)/shard_map/ppermute | solution.py:798
  35.0 2.1 %shard_map.146 = (f32[8,128]{1,0:T(8,128)S(1)}, f32[8,128]{1,0:T(8,128)S(1)}) custom-call(f32[392,128]{1,0:T(8,128)S(1)} %shard_map.144.sent_ref, f32[392,128]{1,0:T(8,128)S(1)} %collective-permute-done.4.far_ref, f32[256,128]{1,0:T(8,128)S(1)} %get-tuple-element.63.gghost_ref, bf16[256,3072]{1,0:T(8,128)(2,1)S(1)} %get-tuple-element.42.sel_ref, ...), custom_call_target="tpu_custom_call" | custom-call | flops 1000000000 | bytes 8146944 | tf_op jit(solution)/shard_map/pallas_call | solution.py:752
  37.1 0.1 collective-permute-start.5
  37.2 1.1 %collective-permute-done.5 = f32[8,128]{1,0:T(8,128)S(1)} collective-permute-done((f32[8,128]{1,0:T(8,128)S(1)}, f32[8,128]{1,0:T(8,128)S(1)}, u32[]{:S(2)}, u32[]{:S(2)}) %collective-permute-start.5) | collective-permute-done | bytes 4128 | tf_op jit(solution)/shard_map/ppermute | solution.py:795
  38.3 0.6 %add_negate_fusion = f32[3,128]{1,0:T(4,128)} fusion(f32[8,128]{1,0:T(8,128)S(1)} %collective-permute-done.5, f32[8,128]{1,0:T(8,128)S(1)} %get-tuple-element.76, pred[128]{0:T(512)(128)(4,1)S(1)} %compare_compare_fusion), kind=kLoop, calls=%fused_computation.1 | loop fusion | flops 1152 | bytes 4736 | tf_op jit(solution)/shard_map/neg | solution.py:919
  (3 shorter events, 0.0 us)
Async XLA Ops:
  0.6 2.8 %collective-permute-start.1 = (s32[128]{0:T(128)}, s32[128]{0:T(128)S(1)}, u32[]{:S(2)}, u32[]{:S(2)}) collective-permute-start(s32[128]{0:T(128)} %param.14), channel_id=1, source_target_pairs={{0,1},{1,0},{2,3},{3,2},{4,5},{5,4},{6,7},{7,6},{8,9},{9,8},{10,11... | collective-permute-start | bytes 1544 | tf_op jit(solution)/shard_map/ppermute | solution.py:795
  1.4 2.0 %collective-permute-start = (f32[3,128]{1,0:T(4,128)}, f32[3,128]{1,0:T(4,128)S(1)}, u32[]{:S(2)}, u32[]{:S(2)}) collective-permute-start(f32[3,128]{1,0:T(4,128)} %pos_hbm.1), channel_id=1, source_target_pairs={{0,1},{1,0},{2,3},{3,2},{4,5},{5,4},{6,7},{7,6},{8,9},{9,8},{10,11... | collective-permute-start | bytes 4616 | tf_op jit(solution)/shard_map/ppermute | solution.py:795
  15.8 1.6 %collective-permute-start.2 = (f32[128,128]{1,0:T(8,128)S(1)}, f32[128,128]{1,0:T(8,128)S(1)}, u32[]{:S(2)}, u32[]{:S(2)}) collective-permute-start(f32[128,128]{1,0:T(8,128)S(1)} %get-tuple-element.51), channel_id=1, source_target_pairs={{0,1},{1,0},{2,3},{3,2},{4,5},{5,4},{6,7},{7,6},{8,9},{9,8},{10,11... | collective-permute-start | bytes 196616 | tf_op jit(solution)/shard_map/ppermute | solution.py:795
  21.1 1.4 %collective-permute-start.3 = (f32[128,128]{1,0:T(8,128)S(1)}, f32[128,128]{1,0:T(8,128)S(1)}, u32[]{:S(2)}, u32[]{:S(2)}) collective-permute-start(f32[128,128]{1,0:T(8,128)S(1)} %get-tuple-element.60), channel_id=1, source_target_pairs={{0,1},{1,0},{2,3},{3,2},{4,5},{5,4},{6,7},{7,6},{8,9},{9,8},{10,11... | collective-permute-start | bytes 196616 | tf_op jit(solution)/shard_map/ppermute | solution.py:795
  22.5 12.5 %collective-permute-start.4 = (f32[392,128]{1,0:T(8,128)S(1)}, f32[392,128]{1,0:T(8,128)S(1)}, u32[]{:S(2)}, u32[]{:S(2)}) collective-permute-start(f32[392,128]{1,0:T(8,128)S(1)} %shard_map.144.sent_ref), channel_id=1, source_target_pairs={{1,2},{2,1},{3,4},{4,3},{5,6},{6,5},{7,8},{8,7},{9,10},{10,9},{11,... | collective-permute-start | bytes 602120 | tf_op jit(solution)/shard_map/ppermute | solution.py:798
  37.1 1.3 %collective-permute-start.5 = (f32[8,128]{1,0:T(8,128)S(1)}, f32[8,128]{1,0:T(8,128)S(1)}, u32[]{:S(2)}, u32[]{:S(2)}) collective-permute-start(f32[8,128]{1,0:T(8,128)S(1)} %get-tuple-element.77), channel_id=1, source_target_pairs={{0,1},{1,0},{2,3},{3,2},{4,5},{5,4},{6,7},{7,6},{8,9},{9,8},{10,11... | collective-permute-start | bytes 12296 | tf_op jit(solution)/shard_map/ppermute | solution.py:795
